TPU v7x, 32 devices: a whole 2x2x4 slice. The times are simulated.
32 devices in a mesh: dp: 8 (over y, x, core), tensor: 4 (over z).
Axes of the slice: x: 2, y: 2, z: 4, core: 2. Of those that a mesh axis runs over, the one named last changes fastest.
Arguments:
- sequence: bfloat16 [32, 532, 768], P('dp', 'tensor'), may hold values from -6 to 6
- query_key_value_weight: bfloat16 [768, 3, 768], P(None, None, 'tensor'), may hold values from -0.21875 to 0.21875
- qv_bias: bfloat16 [2, 768], P(None, 'tensor'), may hold values from -3 to 3
- output_weight: bfloat16 [768, 768], P('tensor'), may hold values from -0.875 to 0.875
- out_bias: bfloat16 [768], replicated, may hold values from -2 to 2
- up_weight: bfloat16 [768, 3072], P(None, 'tensor'), may hold values from -0.21875 to 0.21875
- up_bias: bfloat16 [3072], P('tensor'), may hold values from -3 to 3
- down_weight: bfloat16 [3072, 768], P('tensor'), may hold values from -0.21875 to 0.21875
- back_bias: bfloat16 [768], replicated, may hold values from -2 to 2
- gain_one: bfloat16 [768], replicated, may hold values from 0.099609375 to 1.8984375
- shift_one: bfloat16 [768], replicated, may hold values from -2 to 2
- gain_two: bfloat16 [768], replicated, may hold values from 0.099609375 to 1.8984375
- shift_two: bfloat16 [768], replicated, may hold values from -2 to 2
- init_memory: bfloat16 [10, 768], replicated, may hold values from -6 to 6
- reset: int32 [32], P('dp'), may hold values from 0 to 1
- starts: int32 [32, 512], P('dp'), may hold values from 0 to 1, as said below
- cotangent: bfloat16 [32, 532, 768], P('dp', 'tensor'), may hold values from -6 to 6
Outputs:
- output: bfloat16 [32, 532, 768], P('dp', 'tensor')
- input_grad: float32 [32, 532, 768], P('dp', 'tensor')
- query_key_value_gradient: float32 [768, 3, 768], P(None, None, 'tensor')
- grad_qv_bias: float32 [2, 768], P(None, 'tensor')
- output_weight_gradient: float32 [768, 768], P('tensor')
- grad_out_bias: float32 [768], replicated
- up_weight_gradient: float32 [768, 3072], P(None, 'tensor')
- grad_in_bias: float32 [3072], P('tensor')
- down_weight_gradient: float32 [3072, 768], P('tensor')
- grad_back_bias: float32 [768], replicated
- grad_gain_one: float32 [768], replicated
- grad_shift_one: float32 [768], replicated
- grad_gain_two: float32 [768], replicated
- grad_shift_two: float32 [768], replicated
- grad_memory: float32 [10, 768], replicated
Inputs may be any that keep to these rules, and one draw needn't show every extreme that they name: `starts`: the first entry of every segment is 1; in some segment it is the only 1.
All inputs are finite; a program needn't handle non-finite values.
Results may differ from a plain program's by a relative error of at most 0.017.
Values may be sent and summed in bfloat16 or wider, within the bound.
A program may use at most 192 MiB of HBM per device.

v0:
```python
import jax
import jax.numpy as jnp
from jax import lax
from jax.sharding import PartitionSpec as P

DH = 64


PRECISE_MODE = lax.Precision.HIGHEST
NEGATIVE = -1e30
EPSILON = 1e-05


def layer_norm(values_in, norm_gain, norm_shift):
    row_mean = jnp.mean(values_in, axis=-1, keepdims=True)
    centred = values_in - row_mean
    row_var = jnp.mean(centred * centred, axis=-1, keepdims=True)
    return centred * lax.rsqrt(row_var + EPSILON) * norm_gain + norm_shift


def gelu_exact(values_in):
    return jax.nn.gelu(values_in, approximate=False)


def shards(
    sequence,
    query_key_value_weight,
    qv_bias,
    output_weight,
    out_bias,
    up_weight,
    up_bias,
    down_weight,
    back_bias,
    gain_one,
    shift_one,
    gain_two,
    shift_two,
    init_memory,
    reset,
    starts,
    cotangent,
):
    seg_count, local_rows, model_width = sequence.shape
    mem_rows = init_memory.shape[0]
    seg_tokens = starts.shape[1]
    full_rows = local_rows * lax.axis_size("tensor")
    first_row = lax.axis_index("tensor") * local_rows
    position = first_row + jnp.arange(local_rows, dtype=jnp.int32)
    is_memory = (position < mem_rows) | (position >= mem_rows + seg_tokens)
    use_init = (reset[:, None] > 0) & is_memory[None, :]
    memory_table = jnp.concatenate(
        [init_memory, jnp.zeros((seg_tokens, model_width), jnp.bfloat16), init_memory], 0
    )
    local_table = lax.dynamic_slice_in_dim(memory_table, first_row, local_rows, 0)
    layer_input = jnp.where(use_init[:, :, None], local_table[None], sequence)
    doc_ids = jnp.cumsum(starts, axis=1)
    marker = jnp.full((seg_count, mem_rows), -1, jnp.int32)
    doc_rows = jnp.concatenate([marker, doc_ids, marker], 1)
    allowed = (
        (doc_rows[:, :, None] == doc_rows[:, None, :])
        | (doc_rows[:, :, None] < 0)
        | (doc_rows[:, None, :] < 0)
    )
    head_count = query_key_value_weight.shape[2] // DH
    head_shape = (seg_count, full_rows, head_count, DH)
    score_scale = DH ** (-0.5)
    input_whole = lax.all_gather(layer_input, "tensor", axis=1, tiled=True)
    projected_rows = jnp.einsum(
        "eon,nxa->eoxa", input_whole, query_key_value_weight, preferred_element_type=jnp.float32
    )
    queries = (
        (projected_rows[:, :, 0] + qv_bias[0].astype(jnp.float32))
        .astype(jnp.bfloat16)
        .reshape(head_shape)
    )
    keys_all = projected_rows[:, :, 1].astype(jnp.bfloat16).reshape(head_shape)
    values_all = (
        (projected_rows[:, :, 2] + qv_bias[1].astype(jnp.float32))
        .astype(jnp.bfloat16)
        .reshape(head_shape)
    )
    raw = (
        jnp.einsum("sqhe,skhe->shqk", queries, keys_all, preferred_element_type=jnp.float32)
        * score_scale
    )
    scores = jnp.where(allowed[:, None], raw, NEGATIVE)
    top = jnp.max(scores, axis=-1, keepdims=True)
    weights = jnp.exp(scores - top)
    totals = jnp.sum(weights, axis=-1, keepdims=True)
    log_total = top + jnp.log(totals)
    probs_low = (weights / totals).astype(jnp.bfloat16)
    mixed_rows_value = jnp.einsum(
        "shqk,skhe->sqhe", probs_low, values_all, preferred_element_type=jnp.float32
    )
    mixed_rows_value = mixed_rows_value.astype(jnp.bfloat16).reshape(
        seg_count, full_rows, head_count * DH
    )
    attention_share = jnp.einsum(
        "cui,ir->cur", mixed_rows_value, output_weight, preferred_element_type=jnp.float32
    )
    attended_rows = lax.psum_scatter(attention_share, "tensor", scatter_dimension=1, tiled=True)
    first_sum = layer_input.astype(jnp.float32) + attended_rows + out_bias.astype(jnp.float32)
    normalized = layer_norm(first_sum, gain_one.astype(jnp.float32), shift_one.astype(jnp.float32))
    normed_low = normalized.astype(jnp.bfloat16)
    normalized_whole = lax.all_gather(normed_low, "tensor", axis=1, tiled=True)
    pre_activation = jnp.einsum(
        "bre,ek->brk", normalized_whole, up_weight, preferred_element_type=jnp.float32
    ) + up_bias.astype(jnp.float32)
    hidden_rows = gelu_exact(pre_activation).astype(jnp.bfloat16)
    forward_net_share = jnp.einsum(
        "cui,ir->cur", hidden_rows, down_weight, preferred_element_type=jnp.float32
    )
    feed_rows = lax.psum_scatter(forward_net_share, "tensor", scatter_dimension=1, tiled=True)
    second_sum = normalized + feed_rows + back_bias.astype(jnp.float32)
    result, norm_two_back = jax.vjp(
        layer_norm, second_sum, gain_two.astype(jnp.float32), shift_two.astype(jnp.float32)
    )
    output = result.astype(jnp.bfloat16)
    second_grad, grad_gain_two, grad_shift_two = norm_two_back(cotangent.astype(jnp.float32))
    grad_back_bias = jnp.sum(second_grad, axis=(0, 1))
    second_whole_rows = lax.all_gather(
        second_grad.astype(jnp.bfloat16), "tensor", axis=1, tiled=True
    )
    down_weight_gradient = jnp.einsum(
        "xpo,xpc->oc", hidden_rows, second_whole_rows, preferred_element_type=jnp.float32
    )
    hidden_gradient = jnp.einsum(
        "zor,gr->zog", second_whole_rows, down_weight, preferred_element_type=jnp.float32
    )
    gelu_value, gelu_back = jax.vjp(gelu_exact, pre_activation)
    pre_activation_gradient = gelu_back(hidden_gradient)[0].astype(jnp.bfloat16)
    up_weight_gradient = jnp.einsum(
        "rij,rie->je", normalized_whole, pre_activation_gradient, preferred_element_type=jnp.float32
    )
    grad_in_bias = jnp.sum(pre_activation_gradient.astype(jnp.float32), axis=(0, 1))
    normalized_share = jnp.einsum(
        "arx,ix->ari", pre_activation_gradient, up_weight, preferred_element_type=jnp.float32
    )
    normed_grad = (
        lax.psum_scatter(normalized_share, "tensor", scatter_dimension=1, tiled=True) + second_grad
    )
    first_value, norm_one_back = jax.vjp(
        layer_norm, first_sum, gain_one.astype(jnp.float32), shift_one.astype(jnp.float32)
    )
    first_grad, grad_gain_one, grad_shift_one = norm_one_back(normed_grad)
    grad_out_bias = jnp.sum(first_grad, axis=(0, 1))
    first_whole_rows = lax.all_gather(first_grad.astype(jnp.bfloat16), "tensor", axis=1, tiled=True)
    output_weight_gradient = jnp.einsum(
        "xpo,xpc->oc", mixed_rows_value, first_whole_rows, preferred_element_type=jnp.float32
    )
    mixed_gradient = jnp.einsum(
        "zor,gr->zog", first_whole_rows, output_weight, preferred_element_type=jnp.float32
    )
    mixed_gradient = mixed_gradient.astype(jnp.bfloat16).reshape(head_shape)
    raw_again = (
        jnp.einsum("sqhe,skhe->shqk", queries, keys_all, preferred_element_type=jnp.float32)
        * score_scale
    )
    probs_full = jnp.exp(jnp.where(allowed[:, None], raw_again, NEGATIVE) - log_total)
    value_grad = jnp.einsum(
        "shqk,sqhe->skhe",
        probs_full.astype(jnp.bfloat16),
        mixed_gradient,
        preferred_element_type=jnp.float32,
    )
    prob_grad = jnp.einsum(
        "sqhe,skhe->shqk", mixed_gradient, values_all, preferred_element_type=jnp.float32
    )
    score_grad = probs_full * (prob_grad - jnp.sum(probs_full * prob_grad, axis=-1, keepdims=True))
    score_grad = score_grad.astype(jnp.bfloat16)
    query_grad = (
        jnp.einsum("shqk,skhe->sqhe", score_grad, keys_all, preferred_element_type=jnp.float32)
        * score_scale
    )
    key_grad = (
        jnp.einsum("shqk,sqhe->skhe", score_grad, queries, preferred_element_type=jnp.float32)
        * score_scale
    )
    stacked_rows = jnp.stack([query_grad, key_grad, value_grad], 2)
    stacked_rows = stacked_rows.astype(jnp.bfloat16).reshape(
        seg_count, full_rows, 3, head_count * DH
    )
    query_key_value_gradient = jnp.einsum(
        "tvz,tvao->zao", input_whole, stacked_rows, preferred_element_type=jnp.float32
    )
    stacked_sums = jnp.sum(stacked_rows.astype(jnp.float32), axis=(0, 1))
    grad_qv_bias = jnp.stack([stacked_sums[0], stacked_sums[2]], 0)
    input_share = jnp.einsum(
        "wvib,oib->wvo", stacked_rows, query_key_value_weight, preferred_element_type=jnp.float32
    )
    input_sum = (
        lax.psum_scatter(
            input_share.astype(jnp.bfloat16), "tensor", scatter_dimension=1, tiled=True
        ).astype(jnp.float32)
        + first_grad
    )
    input_grad = jnp.where(use_init[:, :, None], 0.0, input_sum)
    mem_index = jnp.where(position < mem_rows, position, position - mem_rows - seg_tokens)
    picker = (
        is_memory[:, None] & (mem_index[:, None] == jnp.arange(mem_rows, dtype=jnp.int32)[None, :])
    ).astype(jnp.float32)
    taken = jnp.einsum(
        "sr,srd->rd", use_init.astype(jnp.float32), input_sum, precision=PRECISE_MODE
    )
    grad_memory = jnp.dot(picker.T, taken, precision=PRECISE_MODE)
    (
        query_key_value_gradient,
        grad_qv_bias,
        output_weight_gradient,
        up_weight_gradient,
        grad_in_bias,
        down_weight_gradient,
    ) = lax.psum(
        (
            query_key_value_gradient,
            grad_qv_bias,
            output_weight_gradient,
            up_weight_gradient,
            grad_in_bias,
            down_weight_gradient,
        ),
        "dp",
    )
    (
        grad_out_bias,
        grad_back_bias,
        grad_gain_one,
        grad_shift_one,
        grad_gain_two,
        grad_shift_two,
        grad_memory,
    ) = lax.psum(
        (
            grad_out_bias,
            grad_back_bias,
            grad_gain_one,
            grad_shift_one,
            grad_gain_two,
            grad_shift_two,
            grad_memory,
        ),
        ("dp", "tensor"),
    )
    return (
        output,
        input_grad,
        query_key_value_gradient,
        grad_qv_bias,
        output_weight_gradient,
        grad_out_bias,
        up_weight_gradient,
        grad_in_bias,
        down_weight_gradient,
        grad_back_bias,
        grad_gain_one,
        grad_shift_one,
        grad_gain_two,
        grad_shift_two,
        grad_memory,
    )


def solution(mesh):
    in_specs = (
        P("dp", "tensor", None),
        P(None, None, "tensor"),
        P(None, "tensor"),
        P("tensor", None),
        P(),
        P(None, "tensor"),
        P("tensor"),
        P("tensor", None),
        P(),
        P(),
        P(),
        P(),
        P(),
        P(),
        P("dp"),
        P("dp", None),
        P("dp", "tensor", None),
    )
    out_specs = (
        P("dp", "tensor", None),
        P("dp", "tensor", None),
        P(None, None, "tensor"),
        P(None, "tensor"),
        P("tensor", None),
        P(),
        P(None, "tensor"),
        P("tensor"),
        P("tensor", None),
        P(),
        P(),
        P(),
        P(),
        P(),
        P(),
    )
    return jax.shard_map(shards, mesh=mesh, in_specs=in_specs, out_specs=out_specs, check_vma=False)
```

profile of v0, /device:TPU:0, one launch (start us, length us, event | category | flops | bytes accessed | tf_op | source)
XLA Modules:
  0.0 1379.1 jit_solution(14117942874959542715)
XLA Ops:
  17.3 63.4 %all-gather.5.cloned.1.call-done = bf16[4,532,768]{2,0,1:T(4,128)(2,1)} async-done(((bf16[4,133,768]{2,0,1:T(4,128)(2,1)}), bf16[4,532,768]{2,0,1:T(4,128)(2,1)}) %all-gather.5.cloned.1.call-update) | async-done | bytes 3268624 | tf_op jit(solution)/shard_map/all_gather | solution.py:68
  80.7 4.6 fusion.14
  86.4 7.7 fusion.94
  94.1 8.0 fusion
  102.2 8.9 fusion.45
  112.2 5.2 copy.58
  119.4 227.9 %all-reduce.13.cloned.1.call-done = f32[4,532,768]{2,0,1:T(4,128)} async-done(((f32[4,532,768]{2,0,1:T(4,128)}), f32[4,532,768]{2,0,1:T(4,128)}) %all-reduce.13.cloned.1.call-update) | async-done | bytes 6537232
  349.8 3.4 multiply_reduce_fusion.4
  355.2 64.1 %all-gather.7.cloned.1.call-done = bf16[4,532,768]{2,0,1:T(4,128)(2,1)} async-done(((bf16[4,133,768]{2,0,1:T(4,128)(2,1)}), bf16[4,532,768]{2,0,1:T(4,128)(2,1)}) %all-gather.7.cloned.1.call-update) | async-done | bytes 3268624 | tf_op jit(solution)/shard_map/all_gather | solution.py:106
  419.3 6.6 fusion.37
  426.0 16.0 %multiply_convert_fusion.1 = (bf16[4,532,768]{2,1,0:T(8,128)(2,1)S(1)}, f32[4,532,768]{2,1,0:T(8,128)}) fusion(f32[4,532,768]{2,1,0:T(8,128)S(1)} %get-tuple-element.92, f32[768]{0:T(1024)S(1)} %convert_element_type.128, u8[532,768]{1,0:T(8,128)(4,1)S(1)} %get-tuple-element.46, u8[532,768]{1,0:T(8,128)(4,1)S(1)} %get-tuple-element.45), kind=kLoop, calls=%fused_computation.21 | loop fusion | flops 116035584 | bytes 17163264 | tf_op jit(solution)/shard_map/convert_element_type | solution.py:110
  444.9 5.2 copy.60
  450.8 229.1 %all-reduce.15.cloned.1.call-done = f32[4,532,768]{2,0,1:T(4,128)} async-done(((f32[4,532,768]{2,0,1:T(4,128)}), f32[4,532,768]{2,0,1:T(4,128)}) %all-reduce.15.cloned.1.call-update) | async-done | bytes 6537232
  691.4 64.4 %all-gather.9.cloned.1.call-done = bf16[4,532,768]{2,0,1:T(4,128)(2,1)} async-done(((bf16[4,133,768]{2,0,1:T(4,128)(2,1)}), bf16[4,532,768]{2,0,1:T(4,128)(2,1)}) %all-gather.9.cloned.1.call-update) | async-done | bytes 3268624 | tf_op jit(solution)/shard_map/all_gather | solution.py:122
  755.8 11.1 convert_reduce_fusion
  771.6 5.2 copy.62
  777.1 229.5 %all-reduce.17.cloned.1.call-done = f32[4,532,768]{2,0,1:T(4,128)} async-done(((f32[4,532,768]{2,0,1:T(4,128)}), f32[4,532,768]{2,0,1:T(4,128)}) %all-reduce.17.cloned.1.call-update) | async-done | bytes 6537232
  1006.6 3.8 multiply_reduce_fusion.1
  1014.1 64.5 %all-gather.11.cloned.1.call-done = bf16[4,532,768]{2,0,1:T(4,128)(2,1)} async-done(((bf16[4,133,768]{2,0,1:T(4,128)(2,1)}), bf16[4,532,768]{2,0,1:T(4,128)(2,1)}) %all-gather.11.cloned.1.call-update) | async-done | bytes 3268624 | tf_op jit(solution)/shard_map/all_gather | solution.py:148
  1078.6 3.2 fusion.46
  1081.9 8.5 fusion.49
  1090.4 11.0 multiply_reduce_fusion
  1101.5 11.6 multiply_convert_fusion
  1117.6 3.2 bitcast_convert_fusion
  1124.3 7.5 fusion.33
  1131.8 4.4 fusion.30
  1138.7 3.5 fusion.42
  1145.5 15.3 %all-reduce.5 = (f32[2,192]{1,0:T(2,128)}, f32[768]{0:T(1024)}) all-reduce(f32[2,192]{1,0:T(2,128)S(1)} %pad_maximum_fusion.1, f32[768]{0:T(1024)S(1)} %get-tuple-element.95), channel_id=1, replica_groups=mesh['dp'=8,'tensor'=4] {'dp'}, use_global_device_ids=true, to_apply=%region_19.20 | all-reduce | flops 1152 | bytes 9216 | tf_op jit(solution)/shard_map/psum | solution.py:214
  1160.9 86.9 %all-reduce.19.cloned.1.call-done = bf16[4,532,768]{2,0,1:T(4,128)(2,1)} async-done(((bf16[4,532,768]{2,0,1:T(4,128)(2,1)}), bf16[4,532,768]{2,0,1:T(4,128)(2,1)}) %all-reduce.19.cloned.1.call-update) | async-done | bytes 3268624
  1247.7 3.3 fusion.64
  1254.4 41.3 %all-reduce.4 = (f32[768]{0:T(1024)}, f32[768]{0:T(1024)}, f32[768]{0:T(1024)}, f32[768]{0:T(1024)}, f32[768]{0:T(1024)}, /*index=5*/f32[768]{0:T(1024)}, f32[10,768]{1,0:T(8,128)}) all-reduce(f32[768]{0:T(1024)S(1)} %get-tuple-element.84, f32[768]{0:T(1024)S(1)} %get-tuple-element.82, ...), channel_id=1, replica_groups=mesh['dp'=8,'tensor'=4] {'dp','tensor'}, use_global_device_ids=true, to_apply=%region_22.23 | all-reduce | flops 12288 | bytes 98304 | tf_op jit(solution)/shard_map/psum | solution.py:233
  1295.7 70.1 %all-reduce.21.cloned.1.call-done = (f32[768,3,192]{0,2,1:T(8,128)}, f32[192,768]{1,0:T(8,128)}, f32[768,768]{1,0:T(8,128)}, f32[768,768]{1,0:T(8,128)}) async-done(((f32[768,3,192]{0,2,1:T(8,128)}, f32[192,768]{1,0:T(8,128)}, f32[768,768]{1,0:T(8,128)}, f32[768,768]{1,0:T(8,128)}), (f32[768,3,192]{0,2,1:T(8,128)}, f32[192,768]{1,0:T(8,128)}, f32[768,768]{1,0:T(8,128)}, ...) | async-done | bytes 7077904 | tf_op jit(solution)/shard_map/psum | solution.py:214
  (175 shorter events, 65.1 us)
Async XLA Ops:
  7.2 412.1 %copy-start = (bf16[768,768]{1,0:T(8,128)(2,1)S(1)}, bf16[768,768]{1,0:T(8,128)(2,1)}, u32[]{:S(2)}) copy-start(bf16[768,768]{1,0:T(8,128)(2,1)} %param.22) | copy-start | bytes 3538948
  7.2 73.5 %all-gather.5.cloned.1.call-start = ((), (), s32[]{:S(2)}) async-start(), calls=%async_computation | async-start | bytes 4085760 | tf_op jit(solution)/shard_map/all_gather | solution.py:68
  7.3 6.1 copy-start.36
  8.8 341.0 %copy-start.25 = (pred[4,133]{0,1:T(8,128)(4,1)}, pred[4,133]{0,1:T(8,128)(4,1)S(1)}, u32[]{:S(2)}) copy-start(pred[4,133]{0,1:T(8,128)(4,1)S(1)} %get-tuple-element.89) | copy-start | bytes 1600
  12.3 334.9 %all-reduce.13.cloned.1.call-start = ((), (), s32[]{:S(2)}) async-start(), calls=%async_computation.4 | async-start | bytes 13074432
  85.8 8.4 copy-start.2
  85.8 16.4 %copy-start.7 = (f32[4,532,1,192]{1,3,2,0:T(8,128)}, f32[4,532,1,192]{1,3,2,0:T(8,128)S(1)}, u32[]{:S(2)}) copy-start(f32[4,532,1,192]{1,3,2,0:T(8,128)S(1)} %get-tuple-element.79) | copy-start | bytes 4902916
  102.1 8.9 copy-start.27
  117.4 229.8 %copy-start.11 = (bf16[4,133,768]{2,0,1:T(4,128)(2,1)S(1)}, bf16[4,133,768]{2,0,1:T(4,128)(2,1)}, u32[]{:S(2)}) copy-start(bf16[4,133,768]{2,0,1:T(4,128)(2,1)} %param.17) | copy-start | bytes 2451460
  117.5 301.9 %all-gather.7.cloned.1.call-start = ((), (), s32[]{:S(2)}) async-start(), calls=%async_computation.1 | async-start | bytes 4085760 | tf_op jit(solution)/shard_map/all_gather | solution.py:106
  349.8 5.4 copy-start.32
  354.7 325.2 %all-reduce.15.cloned.1.call-start = ((), (), s32[]{:S(2)}) async-start(), calls=%async_computation.5 | async-start | bytes 13074432
  426.0 16.1 %copy-start.12 = (f32[4,532,768]{2,1,0:T(8,128)}, f32[4,532,768]{2,1,0:T(8,128)S(1)}, u32[]{:S(2)}) copy-start(f32[4,532,768]{2,1,0:T(8,128)S(1)} %get-tuple-element.92) | copy-start | bytes 19611652
  426.0 16.1 %copy-start.41 = (bf16[768,768]{1,0:T(8,128)(2,1)S(1)}, bf16[768,768]{1,0:T(8,128)(2,1)}, u32[]{:S(2)}) copy-start(bf16[768,768]{1,0:T(8,128)(2,1)} %param.24) | copy-start | bytes 3538948
  450.1 305.7 %all-gather.9.cloned.1.call-start = ((), (), s32[]{:S(2)}) async-start(), calls=%async_computation.2 | async-start | bytes 4085760 | tf_op jit(solution)/shard_map/all_gather | solution.py:122
  691.2 315.4 %all-reduce.17.cloned.1.call-start = ((), (), s32[]{:S(2)}) async-start(), calls=%async_computation.6 | async-start | bytes 13074432
  776.8 301.8 %all-gather.11.cloned.1.call-start = ((), (), s32[]{:S(2)}) async-start(), calls=%async_computation.3 | async-start | bytes 4085760 | tf_op jit(solution)/shard_map/all_gather | solution.py:148
  1014.0 233.7 %all-reduce.19.cloned.1.call-start = ((), (), s32[]{:S(2)}) async-start(), calls=%async_computation.7 | async-start | bytes 6537216
  1081.9 8.6 copy-start.8
  1090.4 47.5 %copy-start.15 = (bf16[4,3,64,532]{3,2,1,0:T(8,128)(2,1)}, bf16[4,3,64,532]{3,2,1,0:T(8,128)(2,1)S(1)}, u32[]{:S(2)}) copy-start(bf16[4,3,64,532]{3,2,1,0:T(8,128)(2,1)S(1)} %fusion.49) | copy-start | bytes 2451460
  1101.5 11.6 copy-start.3
  1115.8 22.1 %copy-start.13 = (bf16[4,3,64,532]{3,2,1,0:T(8,128)(2,1)}, bf16[4,3,64,532]{3,2,1,0:T(8,128)(2,1)S(1)}, u32[]{:S(2)}) copy-start(bf16[4,3,64,532]{3,2,1,0:T(8,128)(2,1)S(1)} %multiply_convert_fusion.2) | copy-start | bytes 2451460
  1123.8 242.0 %all-reduce.21.cloned.1.call-start = ((), (), s32[]{:S(2)}) async-start(), calls=%async_computation.8 | async-start | bytes 14155776 | tf_op jit(solution)/shard_map/psum | solution.py:214
  1124.3 7.5 copy-start.39
  1124.3 7.5 copy-start.45
  1131.8 4.4 copy-start.23
  1131.8 4.4 copy-start.40
  1142.2 105.5 %copy-start.5 = (f32[4,133,768]{2,0,1:T(4,128)S(1)}, f32[4,133,768]{2,0,1:T(4,128)}, u32[]{:S(2)}) copy-start(f32[4,133,768]{2,0,1:T(4,128)} %copy-done.4) | copy-start | bytes 4902916
  1142.2 105.5 %copy-start.28 = (pred[4,133,1]{0,1,2:T(8,128)(4,1)S(1)}, pred[4,133,1]{0,1,2:T(8,128)(4,1)}, u32[]{:S(2)}) copy-start(pred[4,133,1]{0,1,2:T(8,128)(4,1)} %get-tuple-element.88) | copy-start | bytes 1600
  1142.3 108.8 %copy-start.37 = (pred[133]{0:T(512)(128)(4,1)S(1)}, pred[133]{0:T(512)(128)(4,1)}, u32[]{:S(2)}) copy-start(pred[133]{0:T(512)(128)(4,1)} %copy-done.36) | copy-start | bytes 403
  1143.4 108.0 %copy-start.26 = (pred[4,133]{0,1:T(8,128)(4,1)S(1)}, pred[4,133]{0,1:T(8,128)(4,1)}, u32[]{:S(2)}) copy-start(pred[4,133]{0,1:T(8,128)(4,1)} %copy-done.25) | copy-start | bytes 1600
  1365.8 3.8 copy-start.21
  (23 other events, 38.1 us)
Sparse Core Ops, SparseCore 0:
  12.5 68.2 all-gather.4
  117.6 229.6 all-reduce.12
  354.8 64.4 all-gather.6
  450.3 229.6 all-reduce.14
  691.3 64.4 all-gather.8
  776.9 229.6 all-reduce.16
  1014.1 64.4 all-gather.10
  1123.9 123.7 all-reduce.18
  1252.6 113.2 all-reduce.20
where the time goes:
time: 1380 us
  waiting for transfers between devices  1100 us (80%)
  matrix products  96.9 us (7%)
  other arithmetic  73.2 us (5%)
  blocking collectives  56.7 us (4%)
  local copies, waits for them, and re-layouts  35.3 us (3%)
  between operations  15.3 us (1%)
    unnamed x13, waiting for transfers between devices  774 us
    psum x1, waiting for transfers between devices, shards(): lax.psum((query_key_value_gradient, grad_qv_bias, output_weight_gradient,...  70.1 us
    all_gather x1, waiting for transfers between devices, shards(): lax.all_gather(first_grad.astype(jnp.bfloat16), 'tensor', axis=1, tiled=T...  64.5 us
    all_gather x1, waiting for transfers between devices, shards(): lax.all_gather(second_grad.astype(jnp.bfloat16), 'tensor', axis=1, tiled=...  64.4 us
    all_gather x1, waiting for transfers between devices, shards(): normalized_whole = lax.all_gather(normed_low, 'tensor', axis=1, tiled=True)  64.1 us
    all_gather x1, waiting for transfers between devices, shards(): input_whole = lax.all_gather(layer_input, 'tensor', axis=1, tiled=True)  63.4 us
    psum x1, blocking collectives, shards(): lax.psum((grad_out_bias, grad_back_bias, grad_gain_one, grad_shift_one, g...  41.3 us
  transfers between devices with their start and end apart: 9, of which 9 were waited for; matrix products, arithmetic and copies ran while one was open for 2% of the time, Pallas kernels for 0%

commit v1 on v0

v1 whole, which is shorter than its diff:
```python
import functools

import jax
import jax.numpy as jnp
from jax import lax
from jax.experimental import pallas as pl
from jax.experimental.pallas import tpu as pltpu
from jax.sharding import PartitionSpec as P

DH = 64
NEGATIVE = -1e30
EPSILON = 1e-05
INNER = 8
MIB = 1 << 20

f32 = jnp.float32
bf16 = jnp.bfloat16
NN = (((1,), (0,)), ((), ()))
NT = (((1,), (1,)), ((), ()))
TN = (((0,), (0,)), ((), ()))
MESH = pl.DeviceIdType.MESH


def dot(a, b, dims=NN):
    return lax.dot_general(a, b, dims, preferred_element_type=f32)


def each(count, body):
    def step(i, carry):
        body(i)
        return carry

    lax.fori_loop(0, count, step, 0)


class Place:
    def __init__(self, planes):
        self.planes = planes
        self.dp = lax.axis_index("dp")
        self.t = lax.axis_index("tensor")
        self.core = self.dp % 2
        self.x = (self.dp // 2) % 2
        self.y = (self.dp // 4) % 2
        self.to_core = (self.dp + 1 - 2 * self.core, self.t)
        self.to_x = (self.dp + 2 - 4 * self.x, self.t)
        self.to_y = (self.dp + 4 - 8 * self.y, self.t)

    def plane(self, j):
        return lax.rem(self.t + j, self.planes)

    def to_plane(self, j):
        return (self.dp, self.plane(j))

    def partners(self):
        return [self.to_core, self.to_x, self.to_y] + [
            self.to_plane(j) for j in range(1, self.planes)
        ]

    def greet(self):
        barrier = pltpu.get_barrier_semaphore()
        partners = self.partners()
        for device in partners:
            pl.semaphore_signal(barrier, inc=1, device_id=device, device_id_type=MESH)
        pl.semaphore_wait(barrier, len(partners))


class Rows:
    def __init__(self, place, rows):
        self.piece = rows // (2 * INNER)
        self.half = rows // 2
        quarter = rows // 4
        core, x, y = place.core, place.x, place.y
        at = lambda n: pl.multiple_of(n, 16)
        base = core * self.half
        self.mine = at(base)
        self.others = at((1 - core) * self.half)
        self.a = at(base + (2 * y + x) * self.piece)
        self.b = at(base + quarter + (2 * x + y) * self.piece)
        self.a_pair = at(base + 2 * y * self.piece)
        self.b_pair = at(base + quarter + 2 * x * self.piece)
        self.a_far_pair = at(base + 2 * (1 - y) * self.piece)
        self.b_far_pair = at(base + quarter + 2 * (1 - x) * self.piece)
        self.a_far = at(base + (2 * y + 1 - x) * self.piece)
        self.b_far = at(base + quarter + (2 * x + 1 - y) * self.piece)


class Links:
    def __init__(self, send, recv):
        self.send, self.recv, self.count, self.all = send, recv, 0, []

    def copy(self, src, dst, device):
        k = self.count
        self.count += 1
        made = pltpu.make_async_remote_copy(
            src_ref=src,
            dst_ref=dst,
            send_sem=self.send.at[k],
            recv_sem=self.recv.at[k],
            device_id=device,
            device_id_type=MESH,
        )
        self.all.append(made)
        return made

    def finish(self):
        for made in self.all:
            made.wait_send()


def start(copies):
    for c in copies:
        c.start()


def arrive(copies):
    for c in copies:
        c.wait_recv()


FORWARD_LINKS = 96
FORWARD_LOCALS = 24


def forward_kernel(
    planes,
    heads,
    x_in,
    c_in,
    a_in,
    u_in,
    d_in,
    bias_in,
    vec_ref,
    qcode_ref,
    kcode_ref,
    a_out,
    u_out,
    d_out,
    x_out,
    q_out,
    k_out,
    v_out,
    p_out,
    o_out,
    xhat_out,
    hb_out,
    act_out,
    slope_out,
    g2_out,
    y_out,
    rstd_ref,
    small_ref,
    a_w,
    u_w,
    d_w,
    xs,
    cs,
    bias,
    q_s,
    k_s,
    v_s,
    p_s,
    o_s,
    o3,
    mask,
    acc,
    xhat_s,
    hb_s,
    act_s,
    slope_s,
    y_s,
    send,
    recv,
    local,
):
    place = Place(planes)
    t = place.t
    others = range(1, planes)
    block, width = xs.shape[1], xs.shape[2]
    rows = planes * block
    hp = heads // planes
    hw = hp * DH
    links = Links(send, recv)
    r = Rows(place, a_in.shape[0])
    piece = r.piece

    def keep(k, src, dst):
        return pltpu.make_async_copy(src, dst, local.at[k])

    ins, weights, outs = (a_in, u_in, d_in), (a_w, u_w, d_w), (a_out, u_out, d_out)
    own = [keep(w, ins[w], weights[w].at[t]) for w in range(3)]
    own_x = keep(3, x_in.at[t], xs.at[t])
    own_c = keep(4, c_in.at[t], cs.at[t])
    own_bias = keep(5, bias_in, bias.at[t])

    z_send, s1, s2, cc = [], [], [], []
    for w in range(3):
        z, one, two, three = [], [], [], []
        for j in others:
            s = place.plane(planes - j)
            to = place.to_plane(j)
            for at in (r.a, r.b):
                z.append(
                    links.copy(
                        ins[w].at[pl.ds(at, piece)], weights[w].at[t, pl.ds(at, piece)], to
                    )
                )
            for at, size, to, into in (
                (r.a, piece, place.to_x, one),
                (r.b, piece, place.to_y, one),
                (r.a_pair, 2 * piece, place.to_y, two),
                (r.b_pair, 2 * piece, place.to_x, two),
                (r.mine, r.half, place.to_core, three),
            ):
                ref = weights[w].at[s, pl.ds(at, size)]
                into.append(links.copy(ref, ref, to))
        z_send.append(z)
        s1.append(one)
        s2.append(two)
        cc.append(three)
    x_send = [links.copy(x_in.at[place.plane(j)], xs.at[t], place.to_plane(j)) for j in others]
    c_send = [links.copy(c_in.at[place.plane(j)], cs.at[t], place.to_plane(j)) for j in others]
    b_send = [links.copy(bias_in, bias.at[t], place.to_plane(j)) for j in others]

    start([own_x, *own, own_bias, own_c])
    place.greet()
    start(z_send[0])
    start(b_send)
    start(x_send)

    for c in range(planes):
        span = pl.ds(c * block, block)
        qc = qcode_ref[span, :]
        kc = kcode_ref[...]
        allowed = ((qc == kc) | (qc < 0) | (kc < 0)) & (kc != -2)
        mask[span, :] = jnp.where(allowed, 0.0, NEGATIVE)

    arrive(z_send[0])
    start(s1[0])
    start(z_send[1])
    arrive(s1[0])
    start(s2[0])
    for c in (own_x, *own, own_bias, own_c):
        c.wait()
    arrive(x_send)
    arrive(b_send)
    arrive(s2[0])
    start(cc[0])
    start(z_send[2])

    out_copies = []

    def leave(k, src, dst):
        c = keep(k, src, dst)
        out_copies.append(c)
        return c

    leave_x = [leave(6 + j, xs.at[j], x_out.at[j]) for j in range(planes)]
    start(leave_x)
    acc[...] = xs[...].reshape(rows, width).astype(f32) + vec_ref[0:1, :]

    def attention(j):
        s = place.plane(j)

        @pl.when(j == 1)
        def _():
            arrive(cc[0])
            arrive(z_send[1])
            start(s1[1])

        @pl.when(j == 2)
        def _():
            arrive(s1[1])
            start(s2[1])
            arrive(z_send[2])
            start(s1[2])
            start(c_send)

        @pl.when(j == 3)
        def _():
            arrive(s2[1])
            start(cc[1])
            arrive(s1[2])
            start(s2[2])

        x = xs[...].reshape(rows, width)
        qkv = dot(x, a_w[s, 0 : 3 * hw, :], NT)
        b = bias[s, 1:2, :].astype(f32)
        for i in range(hp):
            cols = slice(i * DH, (i + 1) * DH)
            bq, bv = b[:, cols], b[:, hw + i * DH : hw + (i + 1) * DH]
            q = (qkv[:, cols] + bq).astype(bf16)
            q_s[s * hp + i] = (q.astype(f32) * (DH**-0.5)).astype(bf16)
            k_s[s * hp + i] = qkv[:, hw + i * DH : hw + (i + 1) * DH].astype(bf16)
            v_s[s * hp + i] = (qkv[:, 2 * hw + i * DH : 2 * hw + (i + 1) * DH] + bv).astype(bf16)

        def head(i):
            h = s * hp + i
            k, v = k_s[h], v_s[h]
            for c in range(planes):
                span = pl.ds(c * block, block)
                scores = dot(q_s[h, span, :], k, NT) + mask[span, :]
                e = jnp.exp(scores - jnp.max(scores, axis=1, keepdims=True))
                p = (e / jnp.sum(e, axis=1, keepdims=True)).astype(bf16)
                p_s[h, span, :] = p
                o3[i, span, :] = dot(p, v).astype(bf16)

        each(hp, head)
        o = jnp.concatenate([o3[i] for i in range(hp)], axis=1)
        o_s[s] = o
        acc[...] += dot(o, a_w[s, 3 * hw :, :])

    each(planes, attention)
    start(
        [
            leave(10, q_s, q_out),
            leave(11, k_s, k_out),
            leave(12, v_s, v_out),
            leave(13, p_s, p_out),
            leave(14, o_s, o_out),
            leave(15, a_w, a_out),
        ]
    )

    vec = lambda i: vec_ref[i : i + 1, :]

    def first_norm(c):
        span = pl.ds(pl.multiple_of(c * block, block), block)
        v = acc[span, :]
        v = v - jnp.mean(v, axis=1, keepdims=True)
        rstd = lax.rsqrt(jnp.mean(v * v, axis=1, keepdims=True) + EPSILON)
        xhat = v * rstd
        rstd_ref[span, :] = rstd
        xhat_s[span, :] = xhat
        h = xhat * vec(2) + vec(3)
        hb_s[span, :] = h.astype(bf16)
        acc[span, :] = h + vec(1)

    each(planes, first_norm)
    start([leave(16, xhat_s, xhat_out), leave(17, hb_s, hb_out)])
    arrive(s2[2])
    start(cc[2])
    arrive(cc[1])
    start([leave(18, u_w, u_out)])

    def up(j):
        s = place.plane(j)
        for c in range(planes):
            span = pl.ds(c * block, block)
            z = dot(hb_s[span, :], u_w[s]) + bias[s, 0:1, :].astype(f32)
            phi = 0.5 + 0.5 * lax.erf(z * (0.5**0.5))
            act_s[s, span, :] = (z * phi).astype(bf16)
            slope_s[s, span, :] = (phi + z * jnp.exp(-0.5 * z * z) * 0.3989422804014327).astype(
                bf16
            )

    each(planes, up)
    start([leave(19, act_s, act_out), leave(20, slope_s, slope_out)])
    arrive(cc[2])
    start([leave(21, d_w, d_out)])

    def down(s):
        acc[...] += dot(act_s[s], d_w[s])

    each(planes, down)
    arrive(c_send)

    zero = jnp.zeros((1, width), f32)

    def second_norm(c, sums):
        span = pl.ds(pl.multiple_of(c * block, block), block)
        v = acc[span, :]
        v = v - jnp.mean(v, axis=1, keepdims=True)
        rstd = lax.rsqrt(jnp.mean(v * v, axis=1, keepdims=True) + EPSILON)
        xhat = v * rstd
        y_s[c] = (xhat * vec(4) + vec(5)).astype(bf16)
        g = cs[c].astype(f32)
        d = g * vec(4)
        g2 = rstd * (
            d
            - jnp.mean(d, axis=1, keepdims=True)
            - xhat * jnp.mean(d * xhat, axis=1, keepdims=True)
        )
        acc[span, :] = g2
        add = lambda v: jnp.sum(v, axis=0, keepdims=True)
        return sums[0] + add(g * xhat), sums[1] + add(g), sums[2] + add(g2)

    sums = lax.fori_loop(0, planes, second_norm, (zero, zero, zero))
    small_ref[...] = jnp.concatenate(list(sums) + [jnp.zeros((5, width), f32)], axis=0)
    start([leave(22, acc, g2_out), leave(23, y_s, y_out)])
    for c in out_copies:
        c.wait()
    links.finish()


def forward_call(planes, heads, x_in, c_in, a_in, u_in, d_in, bias_in, vecs, qcode, kcode):
    block, width = x_in.shape[1:]
    rows = planes * block
    hw = heads // planes * DH
    shard = a_in.shape
    S = jax.ShapeDtypeStruct
    V = pltpu.VMEM
    outs = (
        S((planes, *shard), bf16),
        S((planes, *shard), bf16),
        S((planes, *shard), bf16),
        S((planes, block, width), bf16),
        S((heads, rows, DH), bf16),
        S((heads, rows, DH), bf16),
        S((heads, rows, DH), bf16),
        S((heads, rows, rows), bf16),
        S((planes, rows, hw), bf16),
        S((rows, width), f32),
        S((rows, width), bf16),
        S((planes, rows, shard[1]), bf16),
        S((planes, rows, shard[1]), bf16),
        S((rows, width), f32),
        S((planes, block, width), bf16),
        S((rows, 1), f32),
        S((8, width), f32),
    )
    any_spec = pl.BlockSpec(memory_space=pl.ANY)
    vmem_spec = pl.BlockSpec(memory_space=pltpu.VMEM)
    return pl.pallas_call(
        functools.partial(forward_kernel, planes, heads),
        out_shape=outs,
        in_specs=[any_spec] * 6 + [vmem_spec] * 3,
        out_specs=[any_spec] * 15 + [vmem_spec] * 2,
        scratch_shapes=[
            V((planes, *shard), bf16),
            V((planes, *shard), bf16),
            V((planes, *shard), bf16),
            V((planes, block, width), bf16),
            V((planes, block, width), bf16),
            V((planes, *bias_in.shape), bf16),
            V((heads, rows, DH), bf16),
            V((heads, rows, DH), bf16),
            V((heads, rows, DH), bf16),
            V((heads, rows, rows), bf16),
            V((planes, rows, hw), bf16),
            V((heads // planes, rows, DH), bf16),
            V((rows, rows), f32),
            V((rows, width), f32),
            V((rows, width), f32),
            V((rows, width), bf16),
            V((planes, rows, shard[1]), bf16),
            V((planes, rows, shard[1]), bf16),
            V((planes, block, width), bf16),
            pltpu.SemaphoreType.DMA((FORWARD_LINKS,)),
            pltpu.SemaphoreType.DMA((FORWARD_LINKS,)),
            pltpu.SemaphoreType.DMA((FORWARD_LOCALS,)),
        ],
        compiler_params=pltpu.CompilerParams(
            collective_id=0, has_side_effects=True, vmem_limit_bytes=62 * MIB
        ),
    )(x_in, c_in, a_in, u_in, d_in, bias_in, vecs, qcode, kcode)


BACKWARD_LINKS = 80
BACKWARD_LOCALS = 24
SMALL = 32


def backward_kernel(
    planes,
    heads,
    edges,
    a_in,
    u_in,
    d_in,
    x_in,
    q_in,
    k_in,
    v_in,
    p_in,
    o_in,
    xhat_in,
    hb_in,
    act_in,
    slope_in,
    g2_in,
    y_in,
    rstd_ref,
    small_in,
    vec_ref,
    flag_ref,
    ga_out,
    gu_out,
    gd_out,
    dx_out,
    y_out,
    small_ref,
    a_w,
    u_w,
    d_w,
    xs,
    q_s,
    k_s,
    v_s,
    p2,
    o_s,
    xhat_s,
    hb_s,
    act2,
    dz_s,
    acc,
    gb_s,
    dxs,
    do3,
    delta3,
    d9,
    ds_s,
    full,
    half_in,
    pair_in,
    one_in,
    z_in,
    sm,
    sm_in,
    send,
    recv,
    local,
):
    place = Place(planes)
    t = place.t
    others = range(1, planes)
    block, width = xs.shape[1], xs.shape[2]
    rows = planes * block
    hp = heads // planes
    hw = hp * DH
    links = Links(send, recv)
    r = Rows(place, a_w.shape[1])
    piece, half = r.piece, r.half
    weights = (a_w, u_w, d_w)
    g_outs = (ga_out, gu_out, gd_out)

    def keep(k, src, dst):
        return pltpu.make_async_copy(src, dst, local.at[k])

    get = lambda k, src, dst: keep(k, src, dst)
    load_g2 = get(0, g2_in, acc)
    load_d = get(1, d_in, d_w)
    load_u = get(2, u_in, u_w)
    load_a = get(3, a_in, a_w)
    load_hb = get(4, hb_in, hb_s)
    load_xhat = get(5, xhat_in, xhat_s)
    load_o = get(6, o_in, o_s)
    load_qkv = [get(7, q_in, q_s), get(8, k_in, k_s), get(9, v_in, v_s)]
    load_x = get(10, x_in, xs)
    load_slope = get(11, slope_in, dz_s)
    act_load = lambda s: keep(12 + s % 2, act_in.at[s], act2.at[s % 2])
    p_load = lambda h: keep(14 + h % 2, p_in.at[h], p2.at[h % 2])

    start([load_g2, load_d, load_slope])
    act_load(0).start()
    start([load_hb, load_u, load_xhat, load_a, load_o, *load_qkv, load_x])

    class Way:
        pass

    ways = []
    for w in range(3):
        g = weights[w]
        way = Way()
        way.core = [
            links.copy(g.at[s, pl.ds(r.others, half)], half_in.at[w, s], place.to_core)
            for s in range(planes)
        ]
        way.pair = [
            links.copy(g.at[:, pl.ds(r.a_far_pair, 2 * piece)], pair_in.at[w, 0], place.to_y),
            links.copy(g.at[:, pl.ds(r.b_far_pair, 2 * piece)], pair_in.at[w, 1], place.to_x),
        ]
        way.one = [
            links.copy(g.at[:, pl.ds(r.a_far, piece)], one_in.at[w, 0], place.to_x),
            links.copy(g.at[:, pl.ds(r.b_far, piece)], one_in.at[w, 1], place.to_y),
        ]
        way.z = []
        for j in others:
            for i, at in enumerate((r.a, r.b)):
                way.z.append(
                    links.copy(
                        g.at[place.plane(j), pl.ds(at, piece)],
                        z_in.at[w, j - 1, i],
                        place.to_plane(j),
                    )
                )
        f = full.at[w]
        way.back1 = [
            links.copy(f.at[pl.ds(r.a, piece)], f.at[pl.ds(r.a, piece)], place.to_x),
            links.copy(f.at[pl.ds(r.b, piece)], f.at[pl.ds(r.b, piece)], place.to_y),
        ]
        way.back2 = [
            links.copy(
                f.at[pl.ds(r.a_pair, 2 * piece)], f.at[pl.ds(r.a_pair, 2 * piece)], place.to_y
            ),
            links.copy(
                f.at[pl.ds(r.b_pair, 2 * piece)], f.at[pl.ds(r.b_pair, 2 * piece)], place.to_x
            ),
        ]
        way.back3 = [
            links.copy(f.at[pl.ds(r.mine, half)], f.at[pl.ds(r.mine, half)], place.to_core)
        ]
        way.out = keep(16 + w, f, g_outs[w])
        ways.append(way)

    def add_rows(g, s, at, size, got):
        span = pl.ds(at, size)
        g[s, span, :] = (g[s, span, :].astype(f32) + got.astype(f32)).astype(bf16)

    def after_core(w):
        way, g = ways[w], weights[w]
        arrive(way.core)
        for c in way.core:
            c.wait_send()
        each(planes, lambda s: add_rows(g, s, r.mine, half, half_in[w, s]))
        start(way.pair)

    def after_pair(w):
        way, g = ways[w], weights[w]
        arrive(way.pair)

        def add(s):
            add_rows(g, s, r.a_pair, 2 * piece, pair_in[w, 0, s])
            add_rows(g, s, r.b_pair, 2 * piece, pair_in[w, 1, s])

        each(planes, add)
        start(way.one)

    def after_one(w):
        way, g = ways[w], weights[w]
        arrive(way.one)

        def add(s):
            add_rows(g, s, r.a, piece, one_in[w, 0, s])
            add_rows(g, s, r.b, piece, one_in[w, 1, s])

        each(planes, add)
        start(way.z)

    def after_z(w):
        way, g = ways[w], weights[w]
        arrive(way.z)
        for i, at in enumerate((r.a, r.b)):
            v = g[t, pl.ds(at, piece), :].astype(f32)
            for j in others:
                v = v + z_in[w, j - 1, i].astype(f32)
            full[w, pl.ds(at, piece), :] = v.astype(bf16)
        start(way.back1)

    def after_back1(w):
        arrive(ways[w].back1)
        start(ways[w].back2)

    def after_back2(w):
        arrive(ways[w].back2)
        start(ways[w].back3)

    def after_back3(w):
        arrive(ways[w].back3)
        ways[w].out.start()

    y_send = [links.copy(y_in.at[place.plane(j)], y_out.at[t], place.to_plane(j)) for j in others]
    dx_send = [links.copy(dxs.at[place.plane(j)], dx_out.at[t], place.to_plane(j)) for j in others]
    own_y = keep(19, y_in.at[t], y_out.at[t])
    own_dx = keep(20, dxs.at[t], dx_out.at[t])
    small_hop = [
        [links.copy(sm.at[0], sm_in.at[0], place.to_core)],
        [links.copy(sm.at[1], sm_in.at[1], place.to_x)],
        [links.copy(sm.at[2], sm_in.at[2], place.to_y)],
        [links.copy(sm.at[3], sm_in.at[2 + j], place.to_plane(j)) for j in others],
    ]

    place.greet()

    load_g2.wait()
    for c in range(planes):
        span = pl.ds(c * block, block)
        gb_s[span, :] = acc[span, :].astype(bf16)
    load_d.wait()
    load_slope.wait()
    sm[0] = jnp.zeros((SMALL, width), f32)
    sm[0, 0:3, :] = small_in[0:3, :]

    def down(s):
        act_load(s).wait()

        @pl.when(s + 1 < planes)
        def _():
            act_load(s + 1).start()

        for c in range(planes):
            span = pl.ds(c * block, block)
            du = dot(gb_s[span, :], d_w[s], NT)
            dz_s[s, span, :] = (du * dz_s[s, span, :].astype(f32)).astype(bf16)
        d_w[s] = dot(act2[s % 2], gb_s[...], TN).astype(bf16)
        for k in range(planes):
            pl.when(s == k)(ways[2].core[k].start)

    each(planes, down)
    load_hb.wait()
    load_u.wait()

    def up(s):
        dz = dz_s[s]
        sm[0, pl.ds(6 + s, 1), :] = jnp.sum(dz.astype(f32), axis=0, keepdims=True)
        acc[...] += dot(dz, u_w[s], NT)
        u_w[s] = dot(hb_s[...], dz, TN).astype(bf16)
        for k in range(planes):
            pl.when(s == k)(ways[1].core[k].start)

        @pl.when(s == 1)
        def _():
            after_core(2)

    each(planes, up)
    load_xhat.wait()
    p_load(0).start()

    zero = jnp.zeros((1, width), f32)
    vec = lambda i: vec_ref[i : i + 1, :]

    def first_norm(c, sums):
        span = pl.ds(pl.multiple_of(c * block, block), block)
        xhat = xhat_s[span, :]
        g = acc[span, :]
        d = g * vec(2)
        g1 = rstd_ref[span, :] * (
            d
            - jnp.mean(d, axis=1, keepdims=True)
            - xhat * jnp.mean(d * xhat, axis=1, keepdims=True)
        )
        acc[span, :] = g1
        gb_s[span, :] = g1.astype(bf16)
        add = lambda v: jnp.sum(v, axis=0, keepdims=True)
        return sums[0] + add(g * xhat), sums[1] + add(g), sums[2] + add(g1)

    sums = lax.fori_loop(0, planes, first_norm, (zero, zero, zero))
    sm[0, 3:6, :] = jnp.concatenate(list(sums), axis=0)
    after_core(1)
    start(y_send)
    own_y.start()
    for c in (load_a, load_o, *load_qkv, load_x):
        c.wait()

    def attention(s):
        wo = a_w[s, 3 * hw :, :]
        do = dot(gb_s[...], wo, NT).astype(bf16)
        o = o_s[s]
        prod = do.astype(f32) * o.astype(f32)
        for i in range(hp):
            cols = slice(i * DH, (i + 1) * DH)
            do3[i] = do[:, cols]
            delta3[i] = jnp.sum(prod[:, cols], axis=1, keepdims=True)

        def head(i):
            h = s * hp + i
            p_load(h).wait()

            @pl.when(h + 1 < heads)
            def _():
                p_load(h + 1).start()

            pl.when(h == 1)(lambda: after_pair(2))
            pl.when(h == 3)(lambda: after_one(2))
            pl.when(h == 5)(lambda: after_pair(1))
            pl.when(h == 7)(lambda: (after_one(1), after_z(2)) and None)
            pl.when(h == 8)(lambda: after_back1(2))
            pl.when(h == 9)(lambda: after_back2(2))
            pl.when(h == 10)(lambda: after_back3(2))
            pl.when(h == 11)(lambda: after_z(1))

            slot = h % 2
            k, v = k_s[h], v_s[h]
            for c in range(planes):
                span = pl.ds(c * block, block)
                dp = dot(do3[i, span, :], v, NT)
                ds = (p2[slot, span, :].astype(f32) * (dp - delta3[i, span, :])).astype(bf16)
                ds_s[span, :] = ds
                d9[i, span, :] = (dot(ds, k) * (DH**-0.5)).astype(bf16)
            d9[hp + i] = dot(ds_s[...], q_s[h], TN).astype(bf16)
            d9[2 * hp + i] = dot(p2[slot], do3[i], TN).astype(bf16)

        each(hp, head)
        dqkv = jnp.concatenate([d9[i] for i in range(3 * hp)], axis=1)
        sums = jnp.sum(dqkv.astype(f32), axis=0, keepdims=True)
        sm[0, pl.ds(10 + s, 1), 0:hw] = sums[:, 0:hw]
        sm[0, pl.ds(10 + s, 1), hw : 2 * hw] = sums[:, 2 * hw :]
        acc[...] += dot(dqkv, a_w[s, 0 : 3 * hw, :])
        a_w[s, 0 : 3 * hw, :] = dot(dqkv, xs[...].reshape(rows, width), TN).astype(bf16)
        a_w[s, 3 * hw :, :] = dot(o, gb_s[...], TN).astype(bf16)
        for k in range(planes):
            pl.when(s == k)(ways[0].core[k].start)

    each(planes, attention)

    mem, first, last = edges
    flag = flag_ref[0:1, 0:1]
    sm[0, 14 : 14 + mem, :] = (acc[first : first + mem, :] + acc[last : last + mem, :]) * flag
    start(small_hop[0])
    for c in range(planes):
        dxs[c] = acc[pl.ds(c * block, block), :].astype(bf16)
    start(dx_send)
    own_dx.start()
    after_core(0)

    arrive(small_hop[0])
    sm[1] = sm[0] + sm_in[0]
    start(small_hop[1])
    after_back1(1)
    arrive(small_hop[1])
    sm[2] = sm[1] + sm_in[1]
    start(small_hop[2])
    after_back2(1)
    after_pair(0)
    arrive(small_hop[2])
    sm[3] = sm[2] + sm_in[2]
    start(small_hop[3])
    after_back3(1)
    after_one(0)
    arrive(small_hop[3])
    total = sm[3]
    parts = [sm[3]] + [sm_in[2 + j] for j in others]
    total = jnp.zeros((SMALL, width), f32)
    for s in range(planes):
        for j in range(planes):
            hit = lax.rem(t + planes - j, planes) == s
            total = total + jnp.where(hit, parts[j], 0.0)
    small_ref[...] = total
    after_z(0)
    after_back1(0)
    after_back2(0)
    after_back3(0)

    arrive(y_send)
    arrive(dx_send)
    own_y.wait()
    own_dx.wait()
    for way in ways:
        way.out.wait()
    core_waited = {id(c) for way in ways for c in way.core}
    for made in links.all:
        if id(made) not in core_waited:
            made.wait_send()


def backward_call(planes, heads, edges, saved, vecs, flag):
    a_w, x_s, q_s = saved[0], saved[3], saved[4]
    shard = a_w.shape[1:]
    block, width = x_s.shape[1:]
    rows = planes * block
    hp = heads // planes
    hw = hp * DH
    piece, half = shard[0] // (2 * INNER), shard[0] // 2
    S = jax.ShapeDtypeStruct
    V = pltpu.VMEM
    outs = (
        S(shard, bf16),
        S(shard, bf16),
        S(shard, bf16),
        S((planes, block, width), bf16),
        S((planes, block, width), bf16),
        S((SMALL, width), f32),
    )
    any_spec = pl.BlockSpec(memory_space=pl.ANY)
    vmem_spec = pl.BlockSpec(memory_space=pltpu.VMEM)
    return pl.pallas_call(
        functools.partial(backward_kernel, planes, heads, edges),
        out_shape=outs,
        in_specs=[any_spec] * 15 + [vmem_spec] * 4,
        out_specs=[any_spec] * 5 + [vmem_spec],
        scratch_shapes=[
            V((planes, *shard), bf16),
            V((planes, *shard), bf16),
            V((planes, *shard), bf16),
            V((planes, block, width), bf16),
            V((heads, rows, DH), bf16),
            V((heads, rows, DH), bf16),
            V((heads, rows, DH), bf16),
            V((2, rows, rows), bf16),
            V((planes, rows, hw), bf16),
            V((rows, width), f32),
            V((rows, width), bf16),
            V((2, rows, shard[1]), bf16),
            V((planes, rows, shard[1]), bf16),
            V((rows, width), f32),
            V((rows, width), bf16),
            V((planes, block, width), bf16),
            V((hp, rows, DH), bf16),
            V((hp, rows, 1), f32),
            V((3 * hp, rows, DH), bf16),
            V((rows, rows), bf16),
            V((3, *shard), bf16),
            V((3, planes, half, shard[1]), bf16),
            V((3, 2, planes, 2 * piece, shard[1]), bf16),
            V((3, 2, planes, piece, shard[1]), bf16),
            V((3, planes - 1, 2, piece, shard[1]), bf16),
            V((4, SMALL, width), f32),
            V((2 + planes, SMALL, width), f32),
            pltpu.SemaphoreType.DMA((BACKWARD_LINKS,)),
            pltpu.SemaphoreType.DMA((BACKWARD_LINKS,)),
            pltpu.SemaphoreType.DMA((BACKWARD_LOCALS,)),
        ],
        compiler_params=pltpu.CompilerParams(
            collective_id=1, has_side_effects=True, vmem_limit_bytes=63 * MIB
        ),
    )(*saved, vecs, flag)


def shards(
    dp_size,
    planes,
    sequence,
    query_key_value_weight,
    qv_bias,
    output_weight,
    out_bias,
    up_weight,
    up_bias,
    down_weight,
    back_bias,
    gain_one,
    shift_one,
    gain_two,
    shift_two,
    init_memory,
    reset,
    starts,
    cotangent,
):
    segs, local_rows, width = sequence.shape
    mem = init_memory.shape[0]
    tokens = starts.shape[1]
    hw = query_key_value_weight.shape[2]
    heads = hw * planes // DH
    assert segs == planes and hw * 4 == width and dp_size % INNER == 0
    block = -(-local_rows // 16) * 16
    pad = ((0, 0), (0, block - local_rows), (0, 0))
    t = lax.axis_index("tensor")

    first_row = t * local_rows
    position = first_row + jnp.arange(local_rows, dtype=jnp.int32)
    is_memory = (position < mem) | (position >= mem + tokens)
    use_init = ((reset[:, None] > 0) & is_memory[None, :])[:, :, None]
    table = jnp.concatenate([init_memory, jnp.zeros((tokens, width), bf16), init_memory], 0)
    local_table = lax.dynamic_slice_in_dim(table, first_row, local_rows, 0)
    x_in = jnp.pad(jnp.where(use_init, local_table[None], sequence), pad)
    c_in = jnp.pad(cotangent, pad)

    a_in = jnp.concatenate(
        [query_key_value_weight.transpose(1, 2, 0).reshape(3 * hw, width), output_weight], 0
    )
    qv_row = jnp.concatenate([qv_bias.reshape(2 * hw), jnp.zeros((width - 2 * hw,), bf16)])
    bias_in = jnp.concatenate([up_bias[None], qv_row[None], jnp.zeros((14, width), bf16)], 0)
    zero = jnp.zeros((width,), bf16)
    vecs = jnp.stack(
        [out_bias, back_bias, gain_one, shift_one, gain_two, shift_two, zero, zero]
    ).astype(f32)

    own_starts = lax.dynamic_slice_in_dim(starts, t, 1, 0)[0]
    docs = jnp.cumsum(own_starts)
    marker = jnp.full((mem,), -1, jnp.int32)
    codes = jnp.concatenate([marker, docs, marker]).reshape(planes, local_rows)
    codes = jnp.pad(codes, ((0, 0), (0, block - local_rows)), constant_values=-2)
    codes = codes.reshape(planes * block)
    flag = jnp.broadcast_to(
        lax.dynamic_slice_in_dim((reset > 0).astype(f32), t, 1, 0)[:, None], (8, 128)
    )

    saved = forward_call(
        planes,
        heads,
        x_in,
        c_in,
        a_in,
        up_weight,
        down_weight,
        bias_in,
        vecs,
        codes[:, None],
        codes[None, :],
    )
    last = planes * local_rows - mem
    edges = (mem, 0, last // local_rows * block + last % local_rows)
    ga, gu, gd, dx, y, small = backward_call(planes, heads, edges, saved, vecs, flag)

    output = y[:, :local_rows]
    input_grad = jnp.where(use_init, 0.0, dx[:, :local_rows].astype(f32))
    ga, gu, gd = ga.astype(f32), gu.astype(f32), gd.astype(f32)
    if dp_size > INNER:
        groups = [[o * INNER + i for o in range(dp_size // INNER)] for i in range(INNER)]
        ga, gu, gd, small = lax.psum((ga, gu, gd, small), "dp", axis_index_groups=groups)
    own = lambda first: lax.dynamic_slice_in_dim(small, first + t, 1, 0)[0]
    return (
        output,
        input_grad,
        ga[: 3 * hw].reshape(3, hw, width).transpose(2, 0, 1),
        own(10)[: 2 * hw].reshape(2, hw),
        ga[3 * hw :],
        small[5],
        gu,
        own(6),
        gd,
        small[2],
        small[3],
        small[4],
        small[0],
        small[1],
        small[14 : 14 + mem],
    )


def solution(mesh):
    in_specs = (
        P("dp", "tensor", None),
        P(None, None, "tensor"),
        P(None, "tensor"),
        P("tensor", None),
        P(),
        P(None, "tensor"),
        P("tensor"),
        P("tensor", None),
        P(),
        P(),
        P(),
        P(),
        P(),
        P(),
        P("dp"),
        P("dp", None),
        P("dp", "tensor", None),
    )
    out_specs = (
        P("dp", "tensor", None),
        P("dp", "tensor", None),
        P(None, None, "tensor"),
        P(None, "tensor"),
        P("tensor", None),
        P(),
        P(None, "tensor"),
        P("tensor"),
        P("tensor", None),
        P(),
        P(),
        P(),
        P(),
        P(),
        P(),
    )
    return jax.shard_map(
        functools.partial(shards, mesh.shape["dp"], mesh.shape["tensor"]),
        mesh=mesh,
        in_specs=in_specs,
        out_specs=out_specs,
        check_vma=False,
    )
```

time: 1380 us -> 274 us (0.20)
  waiting for transfers between devices: 1100 us -> 0 us
  Pallas kernels: 0 us -> 244 us
  matrix products: 96.9 us -> 0 us
  other arithmetic: 73.2 us -> 10.4 us
  blocking collectives: 56.7 us -> 0 us
  local copies, waits for them, and re-layouts: 35.3 us -> 13.7 us
  between operations: 15.3 us -> 0.91 us
    unnamed x13 -> x0, waiting for transfers between devices: 774 us -> none
    all_gather x4 -> x0, waiting for transfers between devices: 256 us -> none  [the longest x1 64.5 us: shards(): lax.all_gather(first_grad.astype(jnp.bfloat16), 'tensor', axis=1, tiled=T...]
    pallas_call x0 -> x2, Pallas kernels: none -> 244 us  [the longest x1 143 us: backward_call(): pl.pallas_call(functools.partial(backward_kernel, planes, heads, edges),...]
    dot_general x20 -> x0, matrix products: 96.9 us -> none  [the longest x1 11.1 us: shards(): jnp.einsum('zor,gr->zog', second_whole_rows, down_weight, preferred_eleme...]
    psum x1 -> x0, waiting for transfers between devices: 70.1 us -> none  [shards(): lax.psum((query_key_value_gradient, grad_qv_bias, output_weight_gradient,...]
    psum x2 -> x0, blocking collectives: 56.7 us -> none  [the longest x1 41.3 us: shards(): lax.psum((grad_out_bias, grad_back_bias, grad_gain_one, grad_shift_one, g...]
    reduce_sum x12 -> x0, other arithmetic: 33.9 us -> none  [the longest x1 7.98 us: shards(): totals = jnp.sum(weights, axis=-1, keepdims=True)]
    convert_element_type x12 -> x4, other arithmetic: 31.2 us -> 4.43 us  [the longest x2 3.15 us: shards(): ga, gu, gd = (ga.astype(f32), gu.astype(f32), gd.astype(f32))]
  transfers between devices with their start and end apart: 9 -> 0, of which waited for: 9 -> 0; matrix products, arithmetic and copies ran while one was open for 2% -> 0% of each run, Pallas kernels for 0% -> 0%
where the time goes in v1:
time: 274 us; the launch traced here: 269 us
  Pallas kernels  244 us (89%)
  local copies, waits for them, and re-layouts  13.7 us (5%)
  other arithmetic  10.4 us (4%)
    pallas_call x1, Pallas kernels, backward_call(): pl.pallas_call(functools.partial(backward_kernel, planes, heads, edges),...  143 us
    pallas_call x1, Pallas kernels, forward_call(): pl.pallas_call(functools.partial(forward_kernel, planes, heads), out_shap...  101 us

profile of v1, /device:TPU:0, one launch (start us, length us, event | category | flops | bytes accessed | tf_op | source)
XLA Modules:
  0.0 269.1 jit_solution(2129928495101351994)
XLA Ops:
  0.7 0.1 pad_dynamic-slice_fusion.2
  0.8 0.9 fusion.1
  1.6 0.7 fusion.2
  2.4 1.4 copy_select_fusion
  3.8 1.0 pad.12.x_in
  4.8 0.3 reduce-window.9
  5.2 0.1 slice_reduce_fusion.6
  5.6 0.9 broadcast_in_dim_reshape.8.qcode_ref
  6.5 0.7 broadcast_in_dim_reshape.7.kcode_ref
  7.4 0.6 convert_element_type.21.vec_ref
  8.0 0.1 copy.37
  8.1 1.0 pad.13.c_in
  9.1 1.1 pad_maximum_fusion.a_in
  10.2 0.1 reshape.101
  10.4 0.7 maximum_maximum_fusion.bias_in
  11.1 101.3 %shard_map.280 = (bf16[4,768,768]{2,1,0:T(8,128)(2,1)}, bf16[4,768,768]{2,1,0:T(8,128)(2,1)}, bf16[4,768,768]{2,1,0:T(8,128)(2,1)}, bf16[4,144,768]{2,1,0:T(8,12...) custom-call(bf16[4,144,768]{2,1,0:T(8,128)(2,1)} %pad.12.x_in, ...), custom_call_target="tpu_custom_call" | custom-call | tf_op jit(solution)/shard_map/pallas_call | solution.py:424
  112.3 0.6 dynamic_slice.17
  112.9 1.2 broadcast_in_dim.58.flag_ref
  114.2 142.7 %shard_map.281 = (bf16[768,768]{1,0:T(8,128)(2,1)}, bf16[768,768]{1,0:T(8,128)(2,1)}, bf16[768,768]{1,0:T(8,128)(2,1)}, bf16[4,144,768]{2,1,0:T(8,128)(2,1)}, bf...) custom-call(bf16[4,768,768]{2,1,0:T(8,128)(2,1)} %get-tuple-element.38.a_in, bf16[4,768,768]{2,1,0:T(8,128)(2,1)} %get-tuple-element.39.u_in, ...), custom_call_target="tpu_custom_call" | custom-call | tf_op jit(solution)/shard_map/pallas_call | solution.py:866
  256.9 1.4 convert_select_fusion
  258.3 1.8 copy.40
  260.1 1.6 convert_element_type.25
  261.7 0.1 copy-done.3
  261.8 1.6 convert_element_type.26
  263.4 0.1 copy-done.2
  263.5 1.3 slice.58
  264.8 0.1 copy-done.7
  265.0 1.2 copy.39
  266.2 0.9 slice.59
  267.1 0.6 slice.57
  267.7 0.7 slice_reduce_fusion
  268.4 0.7 reshape.106
  (59 shorter events, 0.8 us)
Async XLA Ops:
  0.6 4.2 %copy-start = (s32[4,512]{1,0:T(4,128)S(1)}, s32[4,512]{1,0:T(4,128)}, u32[]{:S(2)}) copy-start(s32[4,512]{1,0:T(4,128)} %param.32) | copy-start | bytes 24580
  2.4 4.8 %copy-start.10 = (bf16[768]{0:T(1024)(128)(2,1)S(1)}, bf16[768]{0:T(1024)(128)(2,1)}, u32[]{:S(2)}) copy-start(bf16[768]{0:T(1024)(128)(2,1)} %param.21) | copy-start | bytes 4612
  2.4 4.8 %copy-start.11 = (bf16[768]{0:T(1024)(128)(2,1)S(1)}, bf16[768]{0:T(1024)(128)(2,1)}, u32[]{:S(2)}) copy-start(bf16[768]{0:T(1024)(128)(2,1)} %param.25) | copy-start | bytes 4612
  2.4 4.8 %copy-start.12 = (bf16[768]{0:T(1024)(128)(2,1)S(1)}, bf16[768]{0:T(1024)(128)(2,1)}, u32[]{:S(2)}) copy-start(bf16[768]{0:T(1024)(128)(2,1)} %param.26) | copy-start | bytes 4612
  2.4 4.9 %copy-start.13 = (bf16[768]{0:T(1024)(128)(2,1)S(1)}, bf16[768]{0:T(1024)(128)(2,1)}, u32[]{:S(2)}) copy-start(bf16[768]{0:T(1024)(128)(2,1)} %param.27) | copy-start | bytes 4612
  2.4 4.9 %copy-start.14 = (bf16[768]{0:T(1024)(128)(2,1)S(1)}, bf16[768]{0:T(1024)(128)(2,1)}, u32[]{:S(2)}) copy-start(bf16[768]{0:T(1024)(128)(2,1)} %param.28) | copy-start | bytes 4612
  2.4 4.9 %copy-start.15 = (bf16[768]{0:T(1024)(128)(2,1)S(1)}, bf16[768]{0:T(1024)(128)(2,1)}, u32[]{:S(2)}) copy-start(bf16[768]{0:T(1024)(128)(2,1)} %param.29) | copy-start | bytes 4612
  2.4 5.6 %copy-start.6 = (bf16[4,133,768]{2,0,1:T(4,128)(2,1)S(1)}, bf16[4,133,768]{2,0,1:T(4,128)(2,1)}, u32[]{:S(2)}) copy-start(bf16[4,133,768]{2,0,1:T(4,128)(2,1)} %param.33) | copy-start | bytes 2451460
  6.5 2.6 copy-start.5
  6.5 2.6 copy-start.8
  8.1 2.1 copy-start.17
  8.1 2.2 copy-start.16
  258.3 1.8 copy-start.4
  260.1 1.7 copy-start.3
  261.8 1.7 copy-start.2
  263.5 1.5 copy-start.7
  265.0 4.1 %copy-start.1 = (s32[4,512]{1,0:T(4,128)S(1)}, s32[4,512]{1,0:T(4,128)}, u32[]{:S(2)}) copy-start(s32[4,512]{1,0:T(4,128)} %param.32) | copy-start | bytes 24580
  265.0 2.1 copy-start.9

commit v2 on v1

v2 whole, which is shorter than its diff:
```python
import functools

import jax
import jax.numpy as jnp
from jax import lax
from jax.experimental import pallas as pl
from jax.experimental.pallas import tpu as pltpu
from jax.sharding import PartitionSpec as P

DH = 64
NEGATIVE = -1e30
EPSILON = 1e-05
INNER = 8
MIB = 1 << 20

f32 = jnp.float32
bf16 = jnp.bfloat16
NN = (((1,), (0,)), ((), ()))
NT = (((1,), (1,)), ((), ()))
TN = (((0,), (0,)), ((), ()))
MESH = pl.DeviceIdType.MESH


def dot(a, b, dims=NN):
    return lax.dot_general(a, b, dims, preferred_element_type=f32)


def each(count, body):
    def step(i, carry):
        body(i)
        return carry

    lax.fori_loop(0, count, step, 0)


class Place:
    def __init__(self, planes):
        self.planes = planes
        self.dp = lax.axis_index("dp")
        self.t = lax.axis_index("tensor")
        self.core = self.dp % 2
        self.x = (self.dp // 2) % 2
        self.y = (self.dp // 4) % 2
        self.to_core = (self.dp + 1 - 2 * self.core, self.t)
        self.to_x = (self.dp + 2 - 4 * self.x, self.t)
        self.to_y = (self.dp + 4 - 8 * self.y, self.t)

    def plane(self, j):
        return lax.rem(self.t + j, self.planes)

    def to_plane(self, j):
        return (self.dp, self.plane(j))

    def partners(self):
        return [self.to_core, self.to_x, self.to_y] + [
            self.to_plane(j) for j in range(1, self.planes)
        ]

    def greet(self):
        barrier = pltpu.get_barrier_semaphore()
        partners = self.partners()
        for device in partners:
            pl.semaphore_signal(barrier, inc=1, device_id=device, device_id_type=MESH)
        pl.semaphore_wait(barrier, len(partners))


class Rows:
    def __init__(self, place, rows):
        self.piece = rows // (2 * INNER)
        self.half = rows // 2
        quarter = rows // 4
        core, x, y = place.core, place.x, place.y
        at = lambda n: pl.multiple_of(n, 16)
        base = core * self.half
        self.mine = at(base)
        self.others = at((1 - core) * self.half)
        self.a = at(base + (2 * y + x) * self.piece)
        self.b = at(base + quarter + (2 * x + y) * self.piece)
        self.a_pair = at(base + 2 * y * self.piece)
        self.b_pair = at(base + quarter + 2 * x * self.piece)
        self.a_far_pair = at(base + 2 * (1 - y) * self.piece)
        self.b_far_pair = at(base + quarter + 2 * (1 - x) * self.piece)
        self.a_far = at(base + (2 * y + 1 - x) * self.piece)
        self.b_far = at(base + quarter + (2 * x + 1 - y) * self.piece)


class Links:
    def __init__(self, send, recv):
        self.send, self.recv, self.count, self.all = send, recv, 0, []

    def copy(self, src, dst, device, recv=None, only=None):
        k = self.count
        self.count += 1
        made = pltpu.make_async_remote_copy(
            src_ref=src,
            dst_ref=dst,
            send_sem=self.send.at[k],
            recv_sem=self.recv.at[k] if recv is None else recv,
            device_id=device,
            device_id_type=MESH,
        )
        self.all.append((made, only))
        return made

    def finish(self, copies=None):
        for made, only in list(self.all):
            if copies is None or any(made is c for c in copies):
                self.all = [entry for entry in self.all if entry[0] is not made]
                if only is None:
                    made.wait_send()
                else:
                    pl.when(only)(made.wait_send)


def start(copies):
    for c in copies:
        c.start()


def arrive(copies):
    for c in copies:
        c.wait_recv()


class Way:
    pass


LINKS = 200
LOCALS = 24
SMALL = 32


def layer_kernel(
    planes,
    heads,
    edges,
    x_in,
    c_in,
    a_in,
    u_in,
    d_in,
    bias_in,
    vec_ref,
    qcode_ref,
    kcode_ref,
    flag_ref,
    ga_out,
    gu_out,
    gd_out,
    dx_out,
    y_out,
    p_hbm,
    small_ref,
    a_w,
    u_w,
    d_w,
    xs,
    cs,
    bias,
    q_s,
    k_s,
    v_s,
    p2,
    o_s,
    o3,
    delta3,
    d9,
    ds_s,
    mask,
    acc,
    xhat_s,
    rstd_s,
    hb_s,
    act_s,
    dz_s,
    gb_s,
    half_in,
    pair_in,
    one_in,
    z_in,
    sm,
    sm_in,
    send,
    recv,
    recv_z,
    local,
):
    place = Place(planes)
    t = place.t
    others = range(1, planes)
    block, width = xs.shape[1], xs.shape[2]
    rows = planes * block
    hp = heads // planes
    hw = hp * DH
    links = Links(send, recv)
    r = Rows(place, a_in.shape[0])
    piece, half = r.piece, r.half
    vec = lambda i: vec_ref[i : i + 1, :]
    add_up = lambda v: jnp.sum(v, axis=0, keepdims=True)

    def keep(k, src, dst):
        return pltpu.make_async_copy(src, dst, local.at[k])

    ins, weights, g_outs = (a_in, u_in, d_in), (a_w, u_w, d_w), (ga_out, gu_out, gd_out)

    low = t // 2
    mirror = lambda n: n + low * (planes - 1 - 2 * n)

    def slot_shard(i):
        return mirror(i - mirror(t) if i == 1 else i)

    def neighbour(to):
        inside = (to >= 0) & (to < planes)
        return (place.dp, lax.rem(to + planes, planes)), inside

    gather = []
    for w in range(3):
        way = Way()
        way.own, way.z, way.one, way.two, way.core = [], [], [], [], []
        for step in (1, -1):
            device, inside = neighbour(t + step)
            way.own.append(
                (
                    inside,
                    [
                        links.copy(
                            ins[w].at[pl.ds(at, piece)],
                            weights[w].at[t, pl.ds(at, piece)],
                            device,
                            recv_z.at[w, t, n],
                            inside,
                        )
                        for n, at in enumerate((r.a, r.b))
                    ],
                )
            )
        for i in others:
            s = slot_shard(i)
            below = (t - s + planes - 1) // planes
            device, inside = neighbour(t + 2 * below - 1)
            here = lambda at, size: weights[w].at[s, pl.ds(at, size)]
            same = lambda at, size, to: links.copy(here(at, size), here(at, size), to)
            way.z.append(
                (
                    inside,
                    [
                        links.copy(
                            here(at, piece), here(at, piece), device, recv_z.at[w, s, n], inside
                        )
                        for n, at in enumerate((r.a, r.b))
                    ],
                )
            )
            way.one.append([same(r.a, piece, place.to_x), same(r.b, piece, place.to_y)])
            way.two.append(
                [same(r.a_pair, 2 * piece, place.to_y), same(r.b_pair, 2 * piece, place.to_x)]
            )
            way.core.append([same(r.mine, half, place.to_core)])
        gather.append(way)

    def when_start(inside, copies):
        pl.when(inside)(lambda: start(copies))

    def get_own(w):
        for inside, copies in gather[w].own:
            when_start(inside, copies)

    def get_z(w, i):
        inside, copies = gather[w].z[i - 1]
        arrive(copies)
        when_start(inside, copies)
        start(gather[w].one[i - 1])

    def get_one(w, i):
        arrive(gather[w].one[i - 1])
        start(gather[w].two[i - 1])

    def get_two(w, i):
        arrive(gather[w].two[i - 1])
        start(gather[w].core[i - 1])

    def get_core(w, i):
        arrive(gather[w].core[i - 1])

    def release(w):
        way = gather[w]
        links.finish([c for _, z in way.z for c in z])
        links.finish([c for part in way.one + way.two + way.core for c in part])

    ways = []
    for w in range(3):
        g = weights[w]
        way = Way()
        if w == 0:
            way.core, way.pair, way.one, way.z = [], [], [], []
            for i in range(planes):
                s = place.plane(i + 1)
                cut = lambda at, size: g.at[s, pl.ds(at, size)]
                way.core.append(
                    [links.copy(cut(r.others, half), half_in.at[0, i], place.to_core)]
                )
                way.pair.append(
                    [
                        links.copy(cut(r.a_far_pair, 2 * piece), pair_in.at[0, 0, i], place.to_y),
                        links.copy(cut(r.b_far_pair, 2 * piece), pair_in.at[0, 1, i], place.to_x),
                    ]
                )
                way.one.append(
                    [
                        links.copy(cut(r.a_far, piece), one_in.at[0, 0, i], place.to_x),
                        links.copy(cut(r.b_far, piece), one_in.at[0, 1, i], place.to_y),
                    ]
                )
                if i + 1 < planes:
                    to = place.to_plane(i + 1)
                    way.z.append(
                        [
                            links.copy(cut(r.a, piece), z_in.at[0, i, 0], to),
                            links.copy(cut(r.b, piece), z_in.at[0, i, 1], to),
                        ]
                    )
        else:
            way.core = [
                links.copy(g.at[s, pl.ds(r.others, half)], half_in.at[w, s], place.to_core)
                for s in range(planes)
            ]
            way.pair = [
                links.copy(g.at[:, pl.ds(r.a_far_pair, 2 * piece)], pair_in.at[w, 0], place.to_y),
                links.copy(g.at[:, pl.ds(r.b_far_pair, 2 * piece)], pair_in.at[w, 1], place.to_x),
            ]
            way.one = [
                links.copy(g.at[:, pl.ds(r.a_far, piece)], one_in.at[w, 0], place.to_x),
                links.copy(g.at[:, pl.ds(r.b_far, piece)], one_in.at[w, 1], place.to_y),
            ]
            way.z = []
            for j in others:
                for i, at in enumerate((r.a, r.b)):
                    way.z.append(
                        links.copy(
                            g.at[place.plane(j), pl.ds(at, piece)],
                            z_in.at[w, j - 1, i],
                            place.to_plane(j),
                        )
                    )
        at_home = lambda at: pl.multiple_of(at - r.mine, 16)
        f = half_in.at[w, 0]
        same = lambda at, size, to: links.copy(
            f.at[pl.ds(at_home(at), size)], f.at[pl.ds(at_home(at), size)], to
        )
        way.back1 = [same(r.a, piece, place.to_x), same(r.b, piece, place.to_y)]
        way.back2 = [
            same(r.a_pair, 2 * piece, place.to_y),
            same(r.b_pair, 2 * piece, place.to_x),
        ]
        mine = g_outs[w].at[pl.ds(r.mine, half)]
        way.back3 = [links.copy(f, mine, place.to_core)]
        way.out = keep(8 + w, f, mine)
        ways.append(way)

    def add_rows(g, s, at, size, got):
        span = pl.ds(at, size)
        g[s, span, :] = (g[s, span, :].astype(f32) + got.astype(f32)).astype(bf16)

    def after_core(w):
        way, g = ways[w], weights[w]
        arrive(way.core)
        each(planes, lambda s: add_rows(g, s, r.mine, half, half_in[w, s]))
        start(way.pair)

    def after_pair(w):
        way, g = ways[w], weights[w]
        arrive(way.pair)

        def add(s):
            add_rows(g, s, r.a_pair, 2 * piece, pair_in[w, 0, s])
            add_rows(g, s, r.b_pair, 2 * piece, pair_in[w, 1, s])

        each(planes, add)
        start(way.one)

    def after_one(w):
        way, g = ways[w], weights[w]
        arrive(way.one)

        def add(s):
            add_rows(g, s, r.a, piece, one_in[w, 0, s])
            add_rows(g, s, r.b, piece, one_in[w, 1, s])

        each(planes, add)
        start(way.z)

    def part_core(i):
        arrive(ways[0].core[i])
        add_rows(a_w, place.plane(i + 1), r.mine, half, half_in[0, i])
        start(ways[0].pair[i])

    def part_pair(i):
        arrive(ways[0].pair[i])
        s = place.plane(i + 1)
        add_rows(a_w, s, r.a_pair, 2 * piece, pair_in[0, 0, i])
        add_rows(a_w, s, r.b_pair, 2 * piece, pair_in[0, 1, i])
        start(ways[0].one[i])

    def part_one(i):
        arrive(ways[0].one[i])
        s = place.plane(i + 1)
        add_rows(a_w, s, r.a, piece, one_in[0, 0, i])
        add_rows(a_w, s, r.b, piece, one_in[0, 1, i])
        if i + 1 < planes:
            start(ways[0].z[i])

    def after_z(w):
        way, g = ways[w], weights[w]
        if w == 0:
            for z in way.z:
                arrive(z)
        else:
            arrive(way.z)
        for i, at in enumerate((r.a, r.b)):
            v = g[t, pl.ds(at, piece), :].astype(f32)
            for j in others:
                v = v + z_in[w, j - 1, i].astype(f32)
            half_in[w, 0, pl.ds(pl.multiple_of(at - r.mine, 16), piece), :] = v.astype(bf16)
        start(way.back1)

    def after_back1(w):
        arrive(ways[w].back1)
        start(ways[w].back2)

    def after_back2(w):
        arrive(ways[w].back2)
        start(ways[w].back3)
        ways[w].out.start()

    def after_back3(w):
        arrive(ways[w].back3)

    x_send = [links.copy(x_in.at[place.plane(j)], xs.at[t], place.to_plane(j)) for j in others]
    c_send = [links.copy(c_in.at[place.plane(j)], cs.at[t], place.to_plane(j)) for j in others]
    b_send = [links.copy(bias_in, bias.at[t], place.to_plane(j)) for j in others]
    y_send = [links.copy(cs.at[place.plane(j)], y_out.at[t], place.to_plane(j)) for j in others]
    dx_rows = lambda j: act_s.at[0, pl.ds(pl.multiple_of(place.plane(j) * block, 16), block)]
    dx_send = [links.copy(dx_rows(j), dx_out.at[t], place.to_plane(j)) for j in others]
    small_hop = [
        [links.copy(sm.at[0], sm_in.at[0], place.to_core)],
        [links.copy(sm.at[1], sm_in.at[1], place.to_x)],
        [links.copy(sm.at[2], sm_in.at[2], place.to_y)],
        [links.copy(sm.at[3], sm_in.at[2 + j], place.to_plane(j)) for j in others],
    ]
    own = [keep(w, ins[w], weights[w].at[t]) for w in range(3)]
    own_x = keep(3, x_in.at[t], xs.at[t])
    own_c = keep(4, c_in.at[t], cs.at[t])
    own_bias = keep(5, bias_in, bias.at[t])
    own_y = keep(6, cs.at[t], y_out.at[t])
    own_dx = keep(7, dx_rows(0), dx_out.at[t])

    def p_at(m):
        return p_hbm.at[m]

    p_save = lambda m: keep(12 + m % 2, p2.at[m % 2], p_at(m))

    start([own_x, *own, own_bias, own_c])
    place.greet()
    get_own(0)
    start(b_send)
    start(x_send)

    for c in range(planes):
        span = pl.ds(c * block, block)
        qc = qcode_ref[span, :]
        kc = kcode_ref[...]
        allowed = ((qc == kc) | (qc < 0) | (kc < 0)) & (kc != -2)
        mask[span, :] = jnp.where(allowed, 0.0, NEGATIVE)
    sm[0] = jnp.zeros((SMALL, width), f32)

    get_z(0, 1)
    get_z(0, 2)
    get_one(0, 1)
    get_z(0, 3)
    get_own(1)
    get_one(0, 2)
    get_two(0, 1)
    get_one(0, 3)
    get_two(0, 2)
    for c in (own_x, *own, own_bias, own_c):
        c.wait()
    arrive(x_send)
    arrive(b_send)
    acc[...] = xs[...].reshape(rows, width).astype(f32) + vec(0)

    forward_pokes = [
        (1, lambda: get_two(0, 3)),
        (1, lambda: get_z(1, 1)),
        (2, lambda: get_z(1, 2)),
        (3, lambda: get_one(1, 1)),
        (4, lambda: get_z(1, 3)),
        (4, lambda: get_own(2)),
        (5, lambda: get_one(1, 2)),
        (6, lambda: get_two(1, 1)),
        (6, lambda: get_z(2, 1)),
        (7, lambda: get_one(1, 3)),
        (8, lambda: get_two(1, 2)),
        (8, lambda: get_z(2, 2)),
        (9, lambda: get_one(2, 1)),
        (10, lambda: get_z(2, 3)),
        (10, lambda: start(c_send)),
        (10, lambda: get_two(1, 3)),
        (11, lambda: get_one(2, 2)),
    ]

    def forward_order(j):
        picked = t
        for i in others:
            picked = jnp.where(j == i, slot_shard(i), picked)
        return picked

    def attention(j):
        s = forward_order(j)
        for i in others:
            pl.when(j == i)(lambda: get_core(0, i))

        x = xs[...].reshape(rows, width)
        qkv = dot(x, a_w[s, 0 : 3 * hw, :], NT)
        b = bias[s, 1:2, :].astype(f32)
        for i in range(hp):
            cols = slice(i * DH, (i + 1) * DH)
            bq, bv = b[:, cols], b[:, hw + i * DH : hw + (i + 1) * DH]
            q = (qkv[:, cols] + bq).astype(bf16)
            q_s[s * hp + i] = (q.astype(f32) * (DH**-0.5)).astype(bf16)
            k_s[s * hp + i] = qkv[:, hw + i * DH : hw + (i + 1) * DH].astype(bf16)
            v_s[s * hp + i] = (qkv[:, 2 * hw + i * DH : 2 * hw + (i + 1) * DH] + bv).astype(bf16)

        def head(i):
            h = s * hp + i
            m = j * hp + i
            for n, poke in forward_pokes:
                pl.when(m == n)(poke)
            pl.when(m >= 2)(lambda: p_save(m).wait())
            k, v = k_s[h], v_s[h]
            for c in range(planes):
                span = pl.ds(c * block, block)
                scores = dot(q_s[h, span, :], k, NT) + mask[span, :]
                e = jnp.exp(scores - jnp.max(scores, axis=1, keepdims=True))
                p = (e / jnp.sum(e, axis=1, keepdims=True)).astype(bf16)
                p2[m % 2, span, :] = p
                o3[i, span, :] = dot(p, v).astype(bf16)
            keep(12 + m % 2, p2.at[m % 2], p_at(h)).start()

        each(hp, head)
        o = jnp.concatenate([o3[i] for i in range(hp)], axis=1)
        o_s[s] = o
        acc[...] += dot(o, a_w[s, 3 * hw :, :])

    each(planes, attention)

    def first_norm(c):
        span = pl.ds(pl.multiple_of(c * block, block), block)
        v = acc[span, :]
        v = v - jnp.mean(v, axis=1, keepdims=True)
        rstd = lax.rsqrt(jnp.mean(v * v, axis=1, keepdims=True) + EPSILON)
        xhat = v * rstd
        rstd_s[span, :] = rstd
        xhat_s[span, :] = xhat
        h = xhat * vec(2) + vec(3)
        hb_s[span, :] = h.astype(bf16)
        acc[span, :] = h + vec(1)

    each(planes, first_norm)
    get_one(2, 3)
    get_two(2, 1)

    def up(j):
        s = forward_order(j)
        for i in others:
            pl.when(j == i)(lambda: get_core(1, i))
        pl.when(j == 1)(lambda: get_two(2, 2))
        pl.when(j == 2)(lambda: get_two(2, 3))
        for c in range(planes):
            span = pl.ds(c * block, block)
            z = dot(hb_s[span, :], u_w[s]) + bias[s, 0:1, :].astype(f32)
            phi = 0.5 + 0.5 * lax.erf(z * (0.5**0.5))
            act_s[s, span, :] = (z * phi).astype(bf16)
            dz_s[s, span, :] = (phi + z * jnp.exp(-0.5 * z * z) * 0.3989422804014327).astype(bf16)

    each(planes, up)

    def down(j):
        s = forward_order(j)
        for i in others:
            pl.when(j == i)(lambda: get_core(2, i))
        acc[...] += dot(act_s[s], d_w[s])

    each(planes, down)
    arrive(c_send)

    zero = jnp.zeros((1, width), f32)

    def second_norm(c, sums):
        span = pl.ds(pl.multiple_of(c * block, block), block)
        v = acc[span, :]
        v = v - jnp.mean(v, axis=1, keepdims=True)
        rstd = lax.rsqrt(jnp.mean(v * v, axis=1, keepdims=True) + EPSILON)
        xhat = v * rstd
        g = cs[c].astype(f32)
        cs[c] = (xhat * vec(4) + vec(5)).astype(bf16)
        d = g * vec(4)
        g2 = rstd * (
            d
            - jnp.mean(d, axis=1, keepdims=True)
            - xhat * jnp.mean(d * xhat, axis=1, keepdims=True)
        )
        acc[span, :] = g2
        gb_s[span, :] = g2.astype(bf16)
        return sums[0] + add_up(g * xhat), sums[1] + add_up(g), sums[2] + add_up(g2)

    sums = lax.fori_loop(0, planes, second_norm, (zero, zero, zero))
    sm[0, 0:3, :] = jnp.concatenate(list(sums), axis=0)
    start(y_send)
    own_y.start()

    def back_down(s):
        for c in range(planes):
            span = pl.ds(c * block, block)
            du = dot(gb_s[span, :], d_w[s], NT)
            dz_s[s, span, :] = (du * dz_s[s, span, :].astype(f32)).astype(bf16)
        d_w[s] = dot(act_s[s], gb_s[...], TN).astype(bf16)
        for k in range(planes):
            pl.when(s == k)(ways[2].core[k].start)

    release(2)
    each(planes, back_down)

    def back_up(s):
        dz = dz_s[s]
        sm[0, pl.ds(6 + s, 1), :] = add_up(dz.astype(f32))
        acc[...] += dot(dz, u_w[s], NT)
        u_w[s] = dot(hb_s[...], dz, TN).astype(bf16)
        for k in range(planes):
            pl.when(s == k)(ways[1].core[k].start)
        pl.when(s == 1)(lambda: after_core(2))

    release(1)
    each(planes, back_up)
    for m in (heads - 2, heads - 1):
        p_save(m).wait()

    p_load = lambda m: keep(
        12 + m % 2, p_at(place.plane(m // hp + 1) * hp + m % hp), p2.at[m % 2]
    )
    p_load(0).start()

    def back_first_norm(c, sums):
        span = pl.ds(pl.multiple_of(c * block, block), block)
        xhat = xhat_s[span, :]
        g = acc[span, :]
        d = g * vec(2)
        g1 = rstd_s[span, :] * (
            d
            - jnp.mean(d, axis=1, keepdims=True)
            - xhat * jnp.mean(d * xhat, axis=1, keepdims=True)
        )
        acc[span, :] = g1
        gb_s[span, :] = g1.astype(bf16)
        return sums[0] + add_up(g * xhat), sums[1] + add_up(g), sums[2] + add_up(g1)

    sums = lax.fori_loop(0, planes, back_first_norm, (zero, zero, zero))
    sm[0, 3:6, :] = jnp.concatenate(list(sums), axis=0)
    after_core(1)

    back_pokes = [
        (1, lambda: after_pair(2)),
        (3, lambda: after_one(2)),
        (3, lambda: part_core(0)),
        (4, lambda: after_pair(1)),
        (5, lambda: part_pair(0)),
        (6, lambda: after_one(1)),
        (6, lambda: part_core(1)),
        (7, lambda: part_one(0)),
        (8, lambda: part_pair(1)),
        (8, lambda: after_z(2)),
        (9, lambda: after_back1(2)),
        (9, lambda: part_core(2)),
        (10, lambda: part_one(1)),
        (10, lambda: after_back2(2)),
        (11, lambda: part_pair(2)),
        (11, lambda: after_z(1)),
        (11, lambda: after_back3(2)),
    ]

    def back_attention(n):
        s = place.plane(n + 1)
        do = dot(gb_s[...], a_w[s, 3 * hw :, :], NT).astype(bf16)
        o = o_s[s]
        prod = do.astype(f32) * o.astype(f32)
        for i in range(hp):
            cols = slice(i * DH, (i + 1) * DH)
            o3[i] = do[:, cols]
            delta3[i] = jnp.sum(prod[:, cols], axis=1, keepdims=True)

        def head(i):
            h = s * hp + i
            m = n * hp + i
            p_load(m).wait()
            pl.when(m + 1 < heads)(lambda: p_load(m + 1).start())
            for k, poke in back_pokes:
                pl.when(m == k)(poke)
            slot = m % 2
            k, v = k_s[h], v_s[h]
            for c in range(planes):
                span = pl.ds(c * block, block)
                dp = dot(o3[i, span, :], v, NT)
                ds = (p2[slot, span, :].astype(f32) * (dp - delta3[i, span, :])).astype(bf16)
                ds_s[span, :] = ds
                d9[i, span, :] = (dot(ds, k) * (DH**-0.5)).astype(bf16)
            d9[hp + i] = dot(ds_s[...], q_s[h], TN).astype(bf16)
            d9[2 * hp + i] = dot(p2[slot], o3[i], TN).astype(bf16)

        each(hp, head)
        dqkv = jnp.concatenate([d9[i] for i in range(3 * hp)], axis=1)
        sums = add_up(dqkv.astype(f32))
        sm[0, pl.ds(10 + s, 1), 0:hw] = sums[:, 0:hw]
        sm[0, pl.ds(10 + s, 1), hw : 2 * hw] = sums[:, 2 * hw :]
        acc[...] += dot(dqkv, a_w[s, 0 : 3 * hw, :])
        a_w[s, 0 : 3 * hw, :] = dot(dqkv, xs[...].reshape(rows, width), TN).astype(bf16)
        a_w[s, 3 * hw :, :] = dot(o, gb_s[...], TN).astype(bf16)
        for k in range(planes):
            pl.when(n == k)(ways[0].core[k][0].start)

    release(0)
    each(planes, back_attention)

    for c in range(planes):
        span = pl.ds(c * block, block)
        act_s[0, span, :] = acc[span, :].astype(bf16)
    start(dx_send)
    own_dx.start()
    mem, first, last = edges
    flag = flag_ref[0:1, 0:1]
    sm[0, 14 : 14 + mem, :] = (acc[first : first + mem, :] + acc[last : last + mem, :]) * flag
    start(small_hop[0])
    part_core(3)
    part_one(2)
    after_back1(1)
    arrive(small_hop[0])
    sm[1] = sm[0] + sm_in[0]
    start(small_hop[1])
    after_back2(1)
    part_pair(3)
    arrive(small_hop[1])
    sm[2] = sm[1] + sm_in[1]
    start(small_hop[2])
    after_back3(1)
    part_one(3)
    after_z(0)
    arrive(small_hop[2])
    sm[3] = sm[2] + sm_in[2]
    start(small_hop[3])
    after_back1(0)
    after_back2(0)
    arrive(small_hop[3])
    parts = [sm[3]] + [sm_in[2 + j] for j in others]
    total = jnp.zeros((SMALL, width), f32)
    for s in range(planes):
        for j in range(planes):
            hit = lax.rem(t + planes - j, planes) == s
            total = total + jnp.where(hit, parts[j], 0.0)
    small_ref[...] = total
    after_back3(0)

    arrive(y_send)
    arrive(dx_send)
    own_y.wait()
    own_dx.wait()
    for way in ways:
        way.out.wait()
    links.finish()


def layer_call(planes, heads, edges, x_in, c_in, a_in, u_in, d_in, bias_in, small_ins):
    block, width = x_in.shape[1:]
    rows = planes * block
    hp = heads // planes
    hw = hp * DH
    shard = a_in.shape
    hidden = shard[1]
    piece, half = shard[0] // (2 * INNER), shard[0] // 2
    S = jax.ShapeDtypeStruct
    V = pltpu.VMEM
    outs = (
        S(shard, bf16),
        S(shard, bf16),
        S(shard, bf16),
        S((planes, block, width), bf16),
        S((planes, block, width), bf16),
        S((heads, rows, rows), bf16),
        S((SMALL, width), f32),
    )
    any_spec = pl.BlockSpec(memory_space=pl.ANY)
    vmem_spec = pl.BlockSpec(memory_space=pltpu.VMEM)
    return pl.pallas_call(
        functools.partial(layer_kernel, planes, heads, edges),
        out_shape=outs,
        in_specs=[any_spec] * 6 + [vmem_spec] * 4,
        out_specs=[any_spec] * 6 + [vmem_spec],
        scratch_shapes=[
            V((planes, *shard), bf16),
            V((planes, *shard), bf16),
            V((planes, *shard), bf16),
            V((planes, block, width), bf16),
            V((planes, block, width), bf16),
            V((planes, *bias_in.shape), bf16),
            V((heads, rows, DH), bf16),
            V((heads, rows, DH), bf16),
            V((heads, rows, DH), bf16),
            V((2, rows, rows), bf16),
            V((planes, rows, hw), bf16),
            V((hp, rows, DH), bf16),
            V((hp, rows, 1), f32),
            V((3 * hp, rows, DH), bf16),
            V((rows, rows), bf16),
            V((rows, rows), f32),
            V((rows, width), f32),
            V((rows, width), f32),
            V((rows, 1), f32),
            V((rows, width), bf16),
            V((planes, rows, hidden), bf16),
            V((planes, rows, hidden), bf16),
            V((rows, width), bf16),
            V((3, planes, half, hidden), bf16),
            V((3, 2, planes, 2 * piece, hidden), bf16),
            V((3, 2, planes, piece, hidden), bf16),
            V((3, planes - 1, 2, piece, hidden), bf16),
            V((4, SMALL, width), f32),
            V((2 + planes, SMALL, width), f32),
            pltpu.SemaphoreType.DMA((LINKS,)),
            pltpu.SemaphoreType.DMA((LINKS,)),
            pltpu.SemaphoreType.DMA((3, planes, 2)),
            pltpu.SemaphoreType.DMA((LOCALS,)),
        ],
        compiler_params=pltpu.CompilerParams(
            collective_id=0, has_side_effects=True, vmem_limit_bytes=63 * MIB
        ),
    )(x_in, c_in, a_in, u_in, d_in, bias_in, *small_ins)


def shards(
    dp_size,
    planes,
    sequence,
    query_key_value_weight,
    qv_bias,
    output_weight,
    out_bias,
    up_weight,
    up_bias,
    down_weight,
    back_bias,
    gain_one,
    shift_one,
    gain_two,
    shift_two,
    init_memory,
    reset,
    starts,
    cotangent,
):
    segs, local_rows, width = sequence.shape
    mem = init_memory.shape[0]
    tokens = starts.shape[1]
    hw = query_key_value_weight.shape[2]
    heads = hw * planes // DH
    assert segs == planes == 4 and hw * 4 == width and dp_size % INNER == 0
    block = -(-local_rows // 16) * 16
    pad = ((0, 0), (0, block - local_rows), (0, 0))
    t = lax.axis_index("tensor")

    first_row = t * local_rows
    position = first_row + jnp.arange(local_rows, dtype=jnp.int32)
    is_memory = (position < mem) | (position >= mem + tokens)
    use_init = ((reset[:, None] > 0) & is_memory[None, :])[:, :, None]
    table = jnp.concatenate([init_memory, jnp.zeros((tokens, width), bf16), init_memory], 0)
    local_table = lax.dynamic_slice_in_dim(table, first_row, local_rows, 0)
    x_in = jnp.pad(jnp.where(use_init, local_table[None], sequence), pad)
    c_in = jnp.pad(cotangent, pad)

    a_in = jnp.concatenate(
        [query_key_value_weight.transpose(1, 2, 0).reshape(3 * hw, width), output_weight], 0
    )
    qv_row = jnp.concatenate([qv_bias.reshape(2 * hw), jnp.zeros((width - 2 * hw,), bf16)])
    bias_in = jnp.concatenate([up_bias[None], qv_row[None], jnp.zeros((14, width), bf16)], 0)
    zero = jnp.zeros((width,), bf16)
    vecs = jnp.stack(
        [out_bias, back_bias, gain_one, shift_one, gain_two, shift_two, zero, zero]
    ).astype(f32)

    own_starts = lax.dynamic_slice_in_dim(starts, t, 1, 0)[0]
    docs = jnp.cumsum(own_starts)
    marker = jnp.full((mem,), -1, jnp.int32)
    codes = jnp.concatenate([marker, docs, marker]).reshape(planes, local_rows)
    codes = jnp.pad(codes, ((0, 0), (0, block - local_rows)), constant_values=-2)
    codes = codes.reshape(planes * block)
    flag = jnp.broadcast_to(
        lax.dynamic_slice_in_dim((reset > 0).astype(f32), t, 1, 0)[:, None], (8, 128)
    )

    last = planes * local_rows - mem
    edges = (mem, 0, last // local_rows * block + last % local_rows)
    ga, gu, gd, dx, y, _, small = layer_call(
        planes,
        heads,
        edges,
        x_in,
        c_in,
        a_in,
        up_weight,
        down_weight,
        bias_in,
        (vecs, codes[:, None], codes[None, :], flag),
    )

    output = y[:, :local_rows]
    input_grad = jnp.where(use_init, 0.0, dx[:, :local_rows].astype(f32))
    ga, gu, gd = ga.astype(f32), gu.astype(f32), gd.astype(f32)
    if dp_size > INNER:
        groups = [[o * INNER + i for o in range(dp_size // INNER)] for i in range(INNER)]
        ga, gu, gd, small = lax.psum((ga, gu, gd, small), "dp", axis_index_groups=groups)
    own = lambda first: lax.dynamic_slice_in_dim(small, first + t, 1, 0)[0]
    return (
        output,
        input_grad,
        ga[: 3 * hw].reshape(3, hw, width).transpose(2, 0, 1),
        own(10)[: 2 * hw].reshape(2, hw),
        ga[3 * hw :],
        small[5],
        gu,
        own(6),
        gd,
        small[2],
        small[3],
        small[4],
        small[0],
        small[1],
        small[14 : 14 + mem],
    )


def solution(mesh):
    in_specs = (
        P("dp", "tensor", None),
        P(None, None, "tensor"),
        P(None, "tensor"),
        P("tensor", None),
        P(),
        P(None, "tensor"),
        P("tensor"),
        P("tensor", None),
        P(),
        P(),
        P(),
        P(),
        P(),
        P(),
        P("dp"),
        P("dp", None),
        P("dp", "tensor", None),
    )
    out_specs = (
        P("dp", "tensor", None),
        P("dp", "tensor", None),
        P(None, None, "tensor"),
        P(None, "tensor"),
        P("tensor", None),
        P(),
        P(None, "tensor"),
        P("tensor"),
        P("tensor", None),
        P(),
        P(),
        P(),
        P(),
        P(),
        P(),
    )
    return jax.shard_map(
        functools.partial(shards, mesh.shape["dp"], mesh.shape["tensor"]),
        mesh=mesh,
        in_specs=in_specs,
        out_specs=out_specs,
        check_vma=False,
    )
```

time: 274 us -> 238 us (0.87)
  Pallas kernels: 244 us -> 210 us
    pallas_call x2 -> x1, Pallas kernels: 244 us -> 210 us  [layer_call(): pl.pallas_call(functools.partial(layer_kernel, planes, heads, edges), out...]
where the time goes in v2:
time: 238 us; the launch traced here: 236 us
  Pallas kernels  210 us (88%)
  local copies, waits for them, and re-layouts  14 us (6%)
  other arithmetic  10.4 us (4%)
    pallas_call x1, Pallas kernels, layer_call(): pl.pallas_call(functools.partial(layer_kernel, planes, heads, edges), out...  210 us

profile of v2, /device:TPU:0, one launch (start us, length us, event | category | flops | bytes accessed | tf_op | source)
XLA Modules:
  0.0 235.6 jit_solution(2432728700050526701)
XLA Ops:
  0.7 0.1 pad_dynamic-slice_fusion.2
  0.8 0.9 fusion.1
  1.6 0.7 fusion.2
  2.4 1.4 copy_select_fusion
  3.8 1.0 pad.12.x_in
  4.8 0.3 reduce-window.9
  5.2 0.1 slice_reduce_fusion.6
  5.6 0.9 broadcast_in_dim_reshape.8.qcode_ref
  6.5 0.7 broadcast_in_dim_reshape.7.kcode_ref
  7.1 0.6 dynamic_slice.17
  7.7 1.2 broadcast_in_dim.58.flag_ref
  9.0 0.1 copy.37
  9.2 1.0 pad.13.c_in
  10.1 0.3 copy-done.7
  10.4 1.1 pad_maximum_fusion.a_in
  11.7 0.6 convert_element_type.21.vec_ref
  12.3 0.1 reshape.101
  12.5 0.7 maximum_maximum_fusion.bias_in
  13.2 210.3 %shard_map.280 = (bf16[768,768]{1,0:T(8,128)(2,1)}, bf16[768,768]{1,0:T(8,128)(2,1)}, bf16[768,768]{1,0:T(8,128)(2,1)}, bf16[4,144,768]{2,1,0:T(8,128)(2,1)}, bf...) custom-call(bf16[4,144,768]{2,1,0:T(8,128)(2,1)} %pad.12.x_in, ...), custom_call_target="tpu_custom_call" | custom-call | tf_op jit(solution)/shard_map/pallas_call | solution.py:801
  223.5 1.4 convert_select_fusion
  224.9 1.8 copy.40
  226.7 1.6 convert_element_type.25
  228.3 0.1 copy-done.2
  228.4 1.6 convert_element_type.26
  229.9 0.1 copy-done.1
  230.0 1.3 slice.58
  231.4 0.1 copy-done.6
  231.6 1.2 copy.39
  232.8 0.9 slice.59
  233.7 0.6 slice.57
  234.3 0.7 slice_reduce_fusion
  235.0 0.7 reshape.106
  (56 shorter events, 0.8 us)
Async XLA Ops:
  0.6 4.1 %copy-start = (s32[4,512]{1,0:T(4,128)S(1)}, s32[4,512]{1,0:T(4,128)}, u32[]{:S(2)}) copy-start(s32[4,512]{1,0:T(4,128)} %param.32) | copy-start | bytes 24580
  2.4 6.6 %copy-start.5 = (bf16[4,133,768]{2,0,1:T(4,128)(2,1)S(1)}, bf16[4,133,768]{2,0,1:T(4,128)(2,1)}, u32[]{:S(2)}) copy-start(bf16[4,133,768]{2,0,1:T(4,128)(2,1)} %param.33) | copy-start | bytes 2451460
  9.0 1.2 copy-start.4
  9.0 1.4 copy-start.7
  9.1 2.4 %copy-start.9 = (bf16[768]{0:T(1024)(128)(2,1)S(1)}, bf16[768]{0:T(1024)(128)(2,1)}, u32[]{:S(2)}) copy-start(bf16[768]{0:T(1024)(128)(2,1)} %param.21) | copy-start | bytes 4612
  9.1 2.4 %copy-start.10 = (bf16[768]{0:T(1024)(128)(2,1)S(1)}, bf16[768]{0:T(1024)(128)(2,1)}, u32[]{:S(2)}) copy-start(bf16[768]{0:T(1024)(128)(2,1)} %param.25) | copy-start | bytes 4612
  9.1 2.4 %copy-start.11 = (bf16[768]{0:T(1024)(128)(2,1)S(1)}, bf16[768]{0:T(1024)(128)(2,1)}, u32[]{:S(2)}) copy-start(bf16[768]{0:T(1024)(128)(2,1)} %param.26) | copy-start | bytes 4612
  9.1 2.5 %copy-start.12 = (bf16[768]{0:T(1024)(128)(2,1)S(1)}, bf16[768]{0:T(1024)(128)(2,1)}, u32[]{:S(2)}) copy-start(bf16[768]{0:T(1024)(128)(2,1)} %param.27) | copy-start | bytes 4612
  9.1 2.5 %copy-start.13 = (bf16[768]{0:T(1024)(128)(2,1)S(1)}, bf16[768]{0:T(1024)(128)(2,1)}, u32[]{:S(2)}) copy-start(bf16[768]{0:T(1024)(128)(2,1)} %param.28) | copy-start | bytes 4612
  9.1 2.5 %copy-start.14 = (bf16[768]{0:T(1024)(128)(2,1)S(1)}, bf16[768]{0:T(1024)(128)(2,1)}, u32[]{:S(2)}) copy-start(bf16[768]{0:T(1024)(128)(2,1)} %param.29) | copy-start | bytes 4612
  9.1 3.2 %copy-start.16 = (bf16[2,192]{1,0:T(2,128)(2,1)S(1)}, bf16[2,192]{1,0:T(2,128)(2,1)}, u32[]{:S(2)}) copy-start(bf16[2,192]{1,0:T(2,128)(2,1)} %param.19) | copy-start | bytes 2308
  9.1 3.3 %copy-start.15 = (bf16[768]{0:T(1024)(128)(2,1)S(1)}, bf16[768]{0:T(1024)(128)(2,1)}, u32[]{:S(2)}) copy-start(bf16[768]{0:T(1024)(128)(2,1)} %param.23) | copy-start | bytes 4612
  224.9 1.8 copy-start.3
  226.7 1.7 copy-start.2
  228.4 1.7 copy-start.1
  230.0 1.5 copy-start.6
  231.6 2.1 copy-start.8

commit v3 on v2

--- a/solution.py
+++ b/solution.py
@@ -122,29 +122,32 @@
         c.wait_recv()
 
 
+def mirror_end(t, low, planes):
+    return t + low * (planes - 1 - 2 * t)
+
+
 class Way:
     pass
 
 
 LINKS = 200
 LOCALS = 24
-SMALL = 32
+SMALL = 16
 
 
 def layer_kernel(
     planes,
     heads,
-    edges,
+    block,
     x_in,
     c_in,
     a_in,
     u_in,
     d_in,
     bias_in,
-    vec_ref,
-    qcode_ref,
-    kcode_ref,
-    flag_ref,
+    init_ref,
+    starts_ref,
+    reset_ref,
     ga_out,
     gu_out,
     gd_out,
@@ -157,6 +160,7 @@
     d_w,
     xs,
     cs,
+    x_s,
     bias,
     q_s,
     k_s,
@@ -189,14 +193,15 @@
     place = Place(planes)
     t = place.t
     others = range(1, planes)
-    block, width = xs.shape[1], xs.shape[2]
+    real, width = xs.shape[1:]
     rows = planes * block
+    mem = init_ref.shape[0]
     hp = heads // planes
     hw = hp * DH
     links = Links(send, recv)
     r = Rows(place, a_in.shape[0])
     piece, half = r.piece, r.half
-    vec = lambda i: vec_ref[i : i + 1, :]
+    vec = lambda i: bias_in[2 + i : 3 + i, :].astype(f32)
     add_up = lambda v: jnp.sum(v, axis=0, keepdims=True)
 
     def keep(k, src, dst):
@@ -205,6 +210,7 @@
     ins, weights, g_outs = (a_in, u_in, d_in), (a_w, u_w, d_w), (ga_out, gu_out, gd_out)
 
     low = t // 2
+    middle = mirror_end(t, low, planes) == 1
     mirror = lambda n: n + low * (planes - 1 - 2 * n)
 
     def slot_shard(i):
@@ -272,6 +278,16 @@
         when_start(inside, copies)
         start(gather[w].one[i - 1])
 
+    def get_stage(w, d):
+        if d == 1:
+            get_z(w, 1)
+            pl.when(middle)(lambda: get_z(w, 2))
+        elif d == 2:
+            pl.when(middle)(lambda: get_z(w, 3))
+            pl.when(~middle)(lambda: get_z(w, 2))
+        else:
+            pl.when(~middle)(lambda: get_z(w, 3))
+
     def get_one(w, i):
         arrive(gather[w].one[i - 1])
         start(gather[w].two[i - 1])
@@ -288,61 +304,50 @@
         links.finish([c for _, z in way.z for c in z])
         links.finish([c for part in way.one + way.two + way.core for c in part])
 
+    def spread(sends, d):
+        def go(plane, *picks):
+            pl.when(t == plane)(lambda: start([sends[j - 1] for j in picks]))
+
+        if d == 0:
+            go(0, 1, 2, 3)
+            go(3, 3, 2, 1)
+        elif d == 1:
+            go(1, 1, 2)
+            go(2, 3, 2)
+        else:
+            go(1, 3)
+            go(2, 1)
+
+    back_order = (2, 1, 3, 0)
     ways = []
     for w in range(3):
         g = weights[w]
         way = Way()
-        if w == 0:
-            way.core, way.pair, way.one, way.z = [], [], [], []
-            for i in range(planes):
-                s = place.plane(i + 1)
-                cut = lambda at, size: g.at[s, pl.ds(at, size)]
-                way.core.append(
-                    [links.copy(cut(r.others, half), half_in.at[0, i], place.to_core)]
-                )
-                way.pair.append(
+        way.core, way.pair, way.one, way.z = [], [], [], []
+        for i in range(planes):
+            j = back_order[i]
+            s = place.plane(j)
+            cut = lambda at, size: g.at[s, pl.ds(at, size)]
+            way.core.append([links.copy(cut(r.others, half), half_in.at[w, i], place.to_core)])
+            way.pair.append(
+                [
+                    links.copy(cut(r.a_far_pair, 2 * piece), pair_in.at[w, 0, i], place.to_y),
+                    links.copy(cut(r.b_far_pair, 2 * piece), pair_in.at[w, 1, i], place.to_x),
+                ]
+            )
+            way.one.append(
+                [
+                    links.copy(cut(r.a_far, piece), one_in.at[w, 0, i], place.to_x),
+                    links.copy(cut(r.b_far, piece), one_in.at[w, 1, i], place.to_y),
+                ]
+            )
+            if i + 1 < planes:
+                way.z.append(
                     [
-                        links.copy(cut(r.a_far_pair, 2 * piece), pair_in.at[0, 0, i], place.to_y),
-                        links.copy(cut(r.b_far_pair, 2 * piece), pair_in.at[0, 1, i], place.to_x),
+                        links.copy(cut(r.a, piece), z_in.at[w, i, 0], place.to_plane(j)),
+                        links.copy(cut(r.b, piece), z_in.at[w, i, 1], place.to_plane(j)),
                     ]
                 )
-                way.one.append(
-                    [
-                        links.copy(cut(r.a_far, piece), one_in.at[0, 0, i], place.to_x),
-                        links.copy(cut(r.b_far, piece), one_in.at[0, 1, i], place.to_y),
-                    ]
-                )
-                if i + 1 < planes:
-                    to = place.to_plane(i + 1)
-                    way.z.append(
-                        [
-                            links.copy(cut(r.a, piece), z_in.at[0, i, 0], to),
-                            links.copy(cut(r.b, piece), z_in.at[0, i, 1], to),
-                        ]
-                    )
-        else:
-            way.core = [
-                links.copy(g.at[s, pl.ds(r.others, half)], half_in.at[w, s], place.to_core)
-                for s in range(planes)
-            ]
-            way.pair = [
-                links.copy(g.at[:, pl.ds(r.a_far_pair, 2 * piece)], pair_in.at[w, 0], place.to_y),
-                links.copy(g.at[:, pl.ds(r.b_far_pair, 2 * piece)], pair_in.at[w, 1], place.to_x),
-            ]
-            way.one = [
-                links.copy(g.at[:, pl.ds(r.a_far, piece)], one_in.at[w, 0], place.to_x),
-                links.copy(g.at[:, pl.ds(r.b_far, piece)], one_in.at[w, 1], place.to_y),
-            ]
-            way.z = []
-            for j in others:
-                for i, at in enumerate((r.a, r.b)):
-                    way.z.append(
-                        links.copy(
-                            g.at[place.plane(j), pl.ds(at, piece)],
-                            z_in.at[w, j - 1, i],
-                            place.to_plane(j),
-                        )
-                    )
         at_home = lambda at: pl.multiple_of(at - r.mine, 16)
         f = half_in.at[w, 0]
         same = lambda at, size, to: links.copy(
@@ -362,67 +367,41 @@
         span = pl.ds(at, size)
         g[s, span, :] = (g[s, span, :].astype(f32) + got.astype(f32)).astype(bf16)
 
-    def after_core(w):
-        way, g = ways[w], weights[w]
-        arrive(way.core)
-        each(planes, lambda s: add_rows(g, s, r.mine, half, half_in[w, s]))
-        start(way.pair)
-
-    def after_pair(w):
-        way, g = ways[w], weights[w]
-        arrive(way.pair)
-
-        def add(s):
-            add_rows(g, s, r.a_pair, 2 * piece, pair_in[w, 0, s])
-            add_rows(g, s, r.b_pair, 2 * piece, pair_in[w, 1, s])
-
-        each(planes, add)
-        start(way.one)
-
-    def after_one(w):
-        way, g = ways[w], weights[w]
-        arrive(way.one)
-
-        def add(s):
-            add_rows(g, s, r.a, piece, one_in[w, 0, s])
-            add_rows(g, s, r.b, piece, one_in[w, 1, s])
-
-        each(planes, add)
-        start(way.z)
-
-    def part_core(i):
-        arrive(ways[0].core[i])
-        add_rows(a_w, place.plane(i + 1), r.mine, half, half_in[0, i])
-        start(ways[0].pair[i])
-
-    def part_pair(i):
-        arrive(ways[0].pair[i])
-        s = place.plane(i + 1)
-        add_rows(a_w, s, r.a_pair, 2 * piece, pair_in[0, 0, i])
-        add_rows(a_w, s, r.b_pair, 2 * piece, pair_in[0, 1, i])
-        start(ways[0].one[i])
-
-    def part_one(i):
-        arrive(ways[0].one[i])
-        s = place.plane(i + 1)
-        add_rows(a_w, s, r.a, piece, one_in[0, 0, i])
-        add_rows(a_w, s, r.b, piece, one_in[0, 1, i])
+    def back_shard(n):
+        j = 0
+        for i in range(planes - 1):
+            j = jnp.where(n == i, back_order[i], j)
+        return place.plane(j)
+
+    def part_core(w, i):
+        arrive(ways[w].core[i])
+        add_rows(weights[w], back_shard(i), r.mine, half, half_in[w, i])
+        start(ways[w].pair[i])
+
+    def part_pair(w, i):
+        arrive(ways[w].pair[i])
+        s = back_shard(i)
+        add_rows(weights[w], s, r.a_pair, 2 * piece, pair_in[w, 0, i])
+        add_rows(weights[w], s, r.b_pair, 2 * piece, pair_in[w, 1, i])
+        start(ways[w].one[i])
+
+    def part_one(w, i):
+        arrive(ways[w].one[i])
+        s = back_shard(i)
+        add_rows(weights[w], s, r.a, piece, one_in[w, 0, i])
+        add_rows(weights[w], s, r.b, piece, one_in[w, 1, i])
         if i + 1 < planes:
-            start(ways[0].z[i])
+            start(ways[w].z[i])
 
     def after_z(w):
-        way, g = ways[w], weights[w]
-        if w == 0:
-            for z in way.z:
-                arrive(z)
-        else:
-            arrive(way.z)
+        for z in ways[w].z:
+            arrive(z)
         for i, at in enumerate((r.a, r.b)):
-            v = g[t, pl.ds(at, piece), :].astype(f32)
+            v = weights[w][t, pl.ds(at, piece), :].astype(f32)
             for j in others:
                 v = v + z_in[w, j - 1, i].astype(f32)
             half_in[w, 0, pl.ds(pl.multiple_of(at - r.mine, 16), piece), :] = v.astype(bf16)
-        start(way.back1)
+        start(ways[w].back1)
 
     def after_back1(w):
         arrive(ways[w].back1)
@@ -440,73 +419,125 @@
     c_send = [links.copy(c_in.at[place.plane(j)], cs.at[t], place.to_plane(j)) for j in others]
     b_send = [links.copy(bias_in, bias.at[t], place.to_plane(j)) for j in others]
     y_send = [links.copy(cs.at[place.plane(j)], y_out.at[t], place.to_plane(j)) for j in others]
-    dx_rows = lambda j: act_s.at[0, pl.ds(pl.multiple_of(place.plane(j) * block, 16), block)]
-    dx_send = [links.copy(dx_rows(j), dx_out.at[t], place.to_plane(j)) for j in others]
-    small_hop = [
-        [links.copy(sm.at[0], sm_in.at[0], place.to_core)],
-        [links.copy(sm.at[1], sm_in.at[1], place.to_x)],
-        [links.copy(sm.at[2], sm_in.at[2], place.to_y)],
-        [links.copy(sm.at[3], sm_in.at[2 + j], place.to_plane(j)) for j in others],
-    ]
+    dx_send = [links.copy(xs.at[place.plane(j)], dx_out.at[t], place.to_plane(j)) for j in others]
+    hops = []
+    for e in range(2):
+        mine, got = sm.at[e], sm_in.at[e]
+        hops.append(
+            [
+                [links.copy(mine.at[0], got.at[0], place.to_core)],
+                [links.copy(mine.at[1], got.at[1], place.to_x)],
+                [links.copy(mine.at[2], got.at[2], place.to_y)],
+                [links.copy(mine.at[3], got.at[2 + j], place.to_plane(j)) for j in others],
+            ]
+        )
+
+    def hop(e, n):
+        arrive(hops[e][n])
+        if n < 3:
+            sm[e, n + 1] = sm[e, n] + sm_in[e, n]
+            start(hops[e][n + 1])
+            return
+        parts = [sm[e, 3]] + [sm_in[e, 2 + j] for j in others]
+        total = jnp.zeros_like(parts[0])
+        for s in range(planes):
+            for j in range(planes):
+                hit = lax.rem(t + planes - j, planes) == s
+                total = total + jnp.where(hit, parts[j], 0.0)
+        small_ref[e * SMALL : (e + 1) * SMALL, :] = total
+
     own = [keep(w, ins[w], weights[w].at[t]) for w in range(3)]
     own_x = keep(3, x_in.at[t], xs.at[t])
     own_c = keep(4, c_in.at[t], cs.at[t])
-    own_bias = keep(5, bias_in, bias.at[t])
     own_y = keep(6, cs.at[t], y_out.at[t])
-    own_dx = keep(7, dx_rows(0), dx_out.at[t])
+    own_dx = keep(7, xs.at[t], dx_out.at[t])
 
     def p_at(m):
         return p_hbm.at[m]
 
     p_save = lambda m: keep(12 + m % 2, p2.at[m % 2], p_at(m))
 
-    start([own_x, *own, own_bias, own_c])
+    start([own_x, *own, own_c])
     place.greet()
     get_own(0)
     start(b_send)
-    start(x_send)
-
+    spread(x_send, 0)
+
+    bias[t] = bias_in[...]
+    tokens = starts_ref.shape[1]
+
+    def token_of(shape, axis):
+        n = lax.broadcasted_iota(jnp.int32, shape, axis)
+        inside = n % block
+        return (n // block) * real + inside - mem, inside
+
+    upto, _ = token_of((tokens, rows), 1)
+    begun = lax.broadcasted_iota(jnp.int32, (tokens, rows), 0) <= upto
+    begun = jnp.where(begun, 1.0, 0.0).astype(bf16)
+    own_starts = starts_ref[pl.ds(t, 1), :].astype(f32).astype(bf16)
+    docs = dot(jnp.broadcast_to(own_starts, (8, tokens)), begun)
+
+    def codes(docs, axis):
+        token, inside = token_of(docs.shape, axis)
+        docs = jnp.where((token < 0) | (token >= tokens), -1.0, docs)
+        return jnp.where(inside >= real, -2.0, docs)
+
+    kc = codes(docs, 1)[0:1, :]
+    qcodes = codes(docs.T, 0)[:, 0:1]
     for c in range(planes):
-        span = pl.ds(c * block, block)
-        qc = qcode_ref[span, :]
-        kc = kcode_ref[...]
-        allowed = ((qc == kc) | (qc < 0) | (kc < 0)) & (kc != -2)
+        span = slice(c * block, (c + 1) * block)
+        qc = qcodes[span, :]
+        allowed = ((qc == kc) | (qc < 0) | (kc < 0)) & (kc != -2.0)
         mask[span, :] = jnp.where(allowed, 0.0, NEGATIVE)
-    sm[0] = jnp.zeros((SMALL, width), f32)
-
-    get_z(0, 1)
-    get_z(0, 2)
+    for e in range(2):
+        sm[e, 0] = jnp.zeros((SMALL, width), f32)
+
+    get_stage(0, 1)
+    spread(x_send, 1)
+    get_stage(0, 2)
+    spread(x_send, 2)
+    get_own(1)
+    get_own(2)
     get_one(0, 1)
-    get_z(0, 3)
-    get_own(1)
     get_one(0, 2)
     get_two(0, 1)
+    get_stage(0, 3)
+    get_two(0, 2)
     get_one(0, 3)
-    get_two(0, 2)
-    for c in (own_x, *own, own_bias, own_c):
+    for c in (own_x, *own, own_c):
         c.wait()
     arrive(x_send)
     arrive(b_send)
-    acc[...] = xs[...].reshape(rows, width).astype(f32) + vec(0)
+    afresh = reset_ref[t] > 0
+    for c in range(planes):
+        x_s[c, 0:real, :] = xs[c]
+        x_s[c, real:block, :] = jnp.zeros((block - real, width), bf16)
+    last = real - mem
+    x_s[0, 0:mem, :] = jnp.where(afresh, init_ref[...], xs[0, 0:mem, :])
+    x_s[planes - 1, last:real, :] = jnp.where(afresh, init_ref[...], xs[planes - 1, last:real, :])
+    acc[...] = x_s[...].reshape(rows, width).astype(f32) + vec(0)
 
     forward_pokes = [
-        (1, lambda: get_two(0, 3)),
-        (1, lambda: get_z(1, 1)),
-        (2, lambda: get_z(1, 2)),
+        (0, lambda: get_two(0, 3)),
+        (1, lambda: get_stage(1, 1)),
+        (2, lambda: get_stage(2, 1)),
+        (2, lambda: spread(c_send, 0)),
+        (2, lambda: spread(c_send, 1)),
         (3, lambda: get_one(1, 1)),
-        (4, lambda: get_z(1, 3)),
-        (4, lambda: get_own(2)),
-        (5, lambda: get_one(1, 2)),
-        (6, lambda: get_two(1, 1)),
-        (6, lambda: get_z(2, 1)),
-        (7, lambda: get_one(1, 3)),
+        (4, lambda: get_stage(1, 2)),
+        (4, lambda: get_one(2, 1)),
+        (5, lambda: get_two(1, 1)),
+        (5, lambda: get_stage(2, 2)),
+        (5, lambda: spread(c_send, 2)),
+        (6, lambda: get_one(1, 2)),
+        (7, lambda: get_two(2, 1)),
+        (7, lambda: get_one(2, 2)),
         (8, lambda: get_two(1, 2)),
-        (8, lambda: get_z(2, 2)),
-        (9, lambda: get_one(2, 1)),
-        (10, lambda: get_z(2, 3)),
-        (10, lambda: start(c_send)),
-        (10, lambda: get_two(1, 3)),
-        (11, lambda: get_one(2, 2)),
+        (8, lambda: get_stage(1, 3)),
+        (9, lambda: get_stage(2, 3)),
+        (9, lambda: get_two(2, 2)),
+        (10, lambda: get_one(1, 3)),
+        (11, lambda: get_one(2, 3)),
     ]
 
     def forward_order(j):
@@ -520,7 +551,7 @@
         for i in others:
             pl.when(j == i)(lambda: get_core(0, i))
 
-        x = xs[...].reshape(rows, width)
+        x = x_s[...].reshape(rows, width)
         qkv = dot(x, a_w[s, 0 : 3 * hw, :], NT)
         b = bias[s, 1:2, :].astype(f32)
         for i in range(hp):
@@ -567,15 +598,13 @@
         acc[span, :] = h + vec(1)
 
     each(planes, first_norm)
-    get_one(2, 3)
-    get_two(2, 1)
+    get_two(1, 3)
 
     def up(j):
         s = forward_order(j)
         for i in others:
             pl.when(j == i)(lambda: get_core(1, i))
-        pl.when(j == 1)(lambda: get_two(2, 2))
-        pl.when(j == 2)(lambda: get_two(2, 3))
+        pl.when(j == 1)(lambda: get_two(2, 3))
         for c in range(planes):
             span = pl.ds(c * block, block)
             z = dot(hb_s[span, :], u_w[s]) + bias[s, 0:1, :].astype(f32)
@@ -602,8 +631,10 @@
         v = v - jnp.mean(v, axis=1, keepdims=True)
         rstd = lax.rsqrt(jnp.mean(v * v, axis=1, keepdims=True) + EPSILON)
         xhat = v * rstd
-        g = cs[c].astype(f32)
-        cs[c] = (xhat * vec(4) + vec(5)).astype(bf16)
+        gb_s[span, :] = jnp.zeros((block, width), bf16)
+        gb_s[pl.ds(pl.multiple_of(c * block, block), real), :] = cs[c]
+        g = gb_s[span, :].astype(f32)
+        cs[c] = (xhat * vec(4) + vec(5)).astype(bf16)[0:real]
         d = g * vec(4)
         g2 = rstd * (
             d
@@ -615,30 +646,47 @@
         return sums[0] + add_up(g * xhat), sums[1] + add_up(g), sums[2] + add_up(g2)
 
     sums = lax.fori_loop(0, planes, second_norm, (zero, zero, zero))
-    sm[0, 0:3, :] = jnp.concatenate(list(sums), axis=0)
+    sm[0, 0, 0:3, :] = jnp.concatenate(list(sums), axis=0)
     start(y_send)
     own_y.start()
 
-    def back_down(s):
+    def poke_at(n, pokes):
+        for k, poke in pokes:
+            pl.when(n == k)(poke)
+
+    down_pokes = [(2, lambda: part_core(2, 0)), (3, lambda: part_core(2, 1))]
+    up_pokes = [
+        (0, lambda: part_core(2, 2)),
+        (0, lambda: part_pair(2, 0)),
+        (1, lambda: part_core(2, 3)),
+        (2, lambda: part_pair(2, 1)),
+        (2, lambda: part_core(1, 0)),
+        (3, lambda: part_core(1, 1)),
+    ]
+
+    def back_down(n):
+        s = back_shard(n)
+        poke_at(n, down_pokes)
         for c in range(planes):
             span = pl.ds(c * block, block)
             du = dot(gb_s[span, :], d_w[s], NT)
             dz_s[s, span, :] = (du * dz_s[s, span, :].astype(f32)).astype(bf16)
         d_w[s] = dot(act_s[s], gb_s[...], TN).astype(bf16)
         for k in range(planes):
-            pl.when(s == k)(ways[2].core[k].start)
+            pl.when(n == k)(ways[2].core[k][0].start)
 
     release(2)
     each(planes, back_down)
 
-    def back_up(s):
+    def back_up(n):
+        s = back_shard(n)
+        poke_at(n, up_pokes)
         dz = dz_s[s]
-        sm[0, pl.ds(6 + s, 1), :] = add_up(dz.astype(f32))
+        sm[0, 0, pl.ds(6 + s, 1), :] = add_up(dz.astype(f32))
         acc[...] += dot(dz, u_w[s], NT)
         u_w[s] = dot(hb_s[...], dz, TN).astype(bf16)
         for k in range(planes):
-            pl.when(s == k)(ways[1].core[k].start)
-        pl.when(s == 1)(lambda: after_core(2))
+            pl.when(n == k)(ways[1].core[k][0].start)
 
     release(1)
     each(planes, back_up)
@@ -646,7 +694,7 @@
         p_save(m).wait()
 
     p_load = lambda m: keep(
-        12 + m % 2, p_at(place.plane(m // hp + 1) * hp + m % hp), p2.at[m % 2]
+        12 + m % 2, p_at(back_shard(m // hp) * hp + m % hp), p2.at[m % 2]
     )
     p_load(0).start()
 
@@ -665,31 +713,42 @@
         return sums[0] + add_up(g * xhat), sums[1] + add_up(g), sums[2] + add_up(g1)
 
     sums = lax.fori_loop(0, planes, back_first_norm, (zero, zero, zero))
-    sm[0, 3:6, :] = jnp.concatenate(list(sums), axis=0)
-    after_core(1)
+    sm[0, 0, 3:6, :] = jnp.concatenate(list(sums), axis=0)
+    start(hops[0][0])
+    part_pair(2, 2)
+    part_one(2, 0)
 
     back_pokes = [
-        (1, lambda: after_pair(2)),
-        (3, lambda: after_one(2)),
-        (3, lambda: part_core(0)),
-        (4, lambda: after_pair(1)),
-        (5, lambda: part_pair(0)),
-        (6, lambda: after_one(1)),
-        (6, lambda: part_core(1)),
-        (7, lambda: part_one(0)),
-        (8, lambda: part_pair(1)),
-        (8, lambda: after_z(2)),
-        (9, lambda: after_back1(2)),
-        (9, lambda: part_core(2)),
-        (10, lambda: part_one(1)),
-        (10, lambda: after_back2(2)),
-        (11, lambda: part_pair(2)),
-        (11, lambda: after_z(1)),
-        (11, lambda: after_back3(2)),
+        (0, lambda: part_core(1, 2)),
+        (0, lambda: part_pair(2, 3)),
+        (1, lambda: part_core(1, 3)),
+        (1, lambda: part_one(2, 1)),
+        (1, lambda: hop(0, 0)),
+        (2, lambda: part_pair(1, 0)),
+        (3, lambda: part_pair(1, 1)),
+        (3, lambda: part_one(2, 2)),
+        (3, lambda: hop(0, 1)),
+        (4, lambda: part_core(0, 0)),
+        (5, lambda: part_pair(1, 2)),
+        (5, lambda: part_one(2, 3)),
+        (5, lambda: hop(0, 2)),
+        (6, lambda: part_pair(1, 3)),
+        (6, lambda: part_one(1, 0)),
+        (7, lambda: part_core(0, 1)),
+        (7, lambda: part_pair(0, 0)),
+        (8, lambda: part_one(1, 1)),
+        (9, lambda: part_one(1, 2)),
+        (9, lambda: part_one(0, 0)),
+        (9, lambda: part_pair(0, 1)),
+        (10, lambda: part_core(0, 2)),
+        (10, lambda: part_one(1, 3)),
+        (10, lambda: after_z(2)),
+        (11, lambda: part_one(0, 1)),
+        (11, lambda: after_back1(2)),
     ]
 
     def back_attention(n):
-        s = place.plane(n + 1)
+        s = back_shard(n)
         do = dot(gb_s[...], a_w[s, 3 * hw :, :], NT).astype(bf16)
         o = o_s[s]
         prod = do.astype(f32) * o.astype(f32)
@@ -703,8 +762,7 @@
             m = n * hp + i
             p_load(m).wait()
             pl.when(m + 1 < heads)(lambda: p_load(m + 1).start())
-            for k, poke in back_pokes:
-                pl.when(m == k)(poke)
+            poke_at(m, back_pokes)
             slot = m % 2
             k, v = k_s[h], v_s[h]
             for c in range(planes):
@@ -719,10 +777,10 @@
         each(hp, head)
         dqkv = jnp.concatenate([d9[i] for i in range(3 * hp)], axis=1)
         sums = add_up(dqkv.astype(f32))
-        sm[0, pl.ds(10 + s, 1), 0:hw] = sums[:, 0:hw]
-        sm[0, pl.ds(10 + s, 1), hw : 2 * hw] = sums[:, 2 * hw :]
+        sm[1, 0, pl.ds(10 + s, 1), 0:hw] = sums[:, 0:hw]
+        sm[1, 0, pl.ds(10 + s, 1), hw : 2 * hw] = sums[:, 2 * hw :]
         acc[...] += dot(dqkv, a_w[s, 0 : 3 * hw, :])
-        a_w[s, 0 : 3 * hw, :] = dot(dqkv, xs[...].reshape(rows, width), TN).astype(bf16)
+        a_w[s, 0 : 3 * hw, :] = dot(dqkv, x_s[...].reshape(rows, width), TN).astype(bf16)
         a_w[s, 3 * hw :, :] = dot(o, gb_s[...], TN).astype(bf16)
         for k in range(planes):
             pl.when(n == k)(ways[0].core[k][0].start)
@@ -731,41 +789,34 @@
     each(planes, back_attention)
 
     for c in range(planes):
-        span = pl.ds(c * block, block)
-        act_s[0, span, :] = acc[span, :].astype(bf16)
-    start(dx_send)
+        xs[c] = acc[c * block : c * block + real, :].astype(bf16)
+    start(dx_send[1:2])
     own_dx.start()
-    mem, first, last = edges
-    flag = flag_ref[0:1, 0:1]
-    sm[0, 14 : 14 + mem, :] = (acc[first : first + mem, :] + acc[last : last + mem, :]) * flag
-    start(small_hop[0])
-    part_core(3)
-    part_one(2)
+    dx_last = (planes - 1) * block + last
+    both = acc[0:mem, :] + acc[dx_last : dx_last + mem, :]
+    sm[1, 0, 0:mem, :] = jnp.where(afresh, both, 0.0)
+    start(hops[1][0])
+    part_core(0, 3)
+    part_pair(0, 2)
+    hop(1, 0)
+    after_z(1)
+    after_back2(2)
+    part_one(0, 2)
+    part_pair(0, 3)
+    start(dx_send[0:1])
+    hop(1, 1)
     after_back1(1)
-    arrive(small_hop[0])
-    sm[1] = sm[0] + sm_in[0]
-    start(small_hop[1])
+    hop(1, 2)
+    start(dx_send[2:3])
+    part_one(0, 3)
     after_back2(1)
-    part_pair(3)
-    arrive(small_hop[1])
-    sm[2] = sm[1] + sm_in[1]
-    start(small_hop[2])
+    after_z(0)
+    after_back1(0)
+    hop(0, 3)
+    after_back3(2)
+    after_back2(0)
+    hop(1, 3)
     after_back3(1)
-    part_one(3)
-    after_z(0)
-    arrive(small_hop[2])
-    sm[3] = sm[2] + sm_in[2]
-    start(small_hop[3])
-    after_back1(0)
-    after_back2(0)
-    arrive(small_hop[3])
-    parts = [sm[3]] + [sm_in[2 + j] for j in others]
-    total = jnp.zeros((SMALL, width), f32)
-    for s in range(planes):
-        for j in range(planes):
-            hit = lax.rem(t + planes - j, planes) == s
-            total = total + jnp.where(hit, parts[j], 0.0)
-    small_ref[...] = total
     after_back3(0)
 
     arrive(y_send)
@@ -777,8 +828,9 @@
     links.finish()
 
 
-def layer_call(planes, heads, edges, x_in, c_in, a_in, u_in, d_in, bias_in, small_ins):
-    block, width = x_in.shape[1:]
+def layer_call(planes, heads, x_in, c_in, a_in, u_in, d_in, bias_in, init, starts, reset):
+    real, width = x_in.shape[1:]
+    block = -(-real // 16) * 16
     rows = planes * block
     hp = heads // planes
     hw = hp * DH
@@ -791,23 +843,24 @@
         S(shard, bf16),
         S(shard, bf16),
         S(shard, bf16),
-        S((planes, block, width), bf16),
-        S((planes, block, width), bf16),
+        S((planes, real, width), bf16),
+        S((planes, real, width), bf16),
         S((heads, rows, rows), bf16),
-        S((SMALL, width), f32),
+        S((2 * SMALL, width), f32),
     )
     any_spec = pl.BlockSpec(memory_space=pl.ANY)
     vmem_spec = pl.BlockSpec(memory_space=pltpu.VMEM)
     return pl.pallas_call(
-        functools.partial(layer_kernel, planes, heads, edges),
+        functools.partial(layer_kernel, planes, heads, block),
         out_shape=outs,
-        in_specs=[any_spec] * 6 + [vmem_spec] * 4,
+        in_specs=[any_spec] * 5 + [vmem_spec] * 3 + [pl.BlockSpec(memory_space=pltpu.SMEM)],
         out_specs=[any_spec] * 6 + [vmem_spec],
         scratch_shapes=[
             V((planes, *shard), bf16),
             V((planes, *shard), bf16),
             V((planes, *shard), bf16),
-            V((planes, block, width), bf16),
+            V((planes, real, width), bf16),
+            V((planes, real, width), bf16),
             V((planes, block, width), bf16),
             V((planes, *bias_in.shape), bf16),
             V((heads, rows, DH), bf16),
@@ -831,8 +884,8 @@
             V((3, 2, planes, 2 * piece, hidden), bf16),
             V((3, 2, planes, piece, hidden), bf16),
             V((3, planes - 1, 2, piece, hidden), bf16),
-            V((4, SMALL, width), f32),
-            V((2 + planes, SMALL, width), f32),
+            V((2, 4, SMALL, width), f32),
+            V((2, 2 + planes, SMALL, width), f32),
             pltpu.SemaphoreType.DMA((LINKS,)),
             pltpu.SemaphoreType.DMA((LINKS,)),
             pltpu.SemaphoreType.DMA((3, planes, 2)),
@@ -841,7 +894,7 @@
         compiler_params=pltpu.CompilerParams(
             collective_id=0, has_side_effects=True, vmem_limit_bytes=63 * MIB
         ),
-    )(x_in, c_in, a_in, u_in, d_in, bias_in, *small_ins)
+    )(x_in, c_in, a_in, u_in, d_in, bias_in, init, starts, reset)
 
 
 def shards(
@@ -870,67 +923,45 @@
     tokens = starts.shape[1]
     hw = query_key_value_weight.shape[2]
     heads = hw * planes // DH
-    assert segs == planes == 4 and hw * 4 == width and dp_size % INNER == 0
-    block = -(-local_rows // 16) * 16
-    pad = ((0, 0), (0, block - local_rows), (0, 0))
+    assert segs == planes == 4 and mem <= local_rows and dp_size % INNER == 0
     t = lax.axis_index("tensor")
-
-    first_row = t * local_rows
-    position = first_row + jnp.arange(local_rows, dtype=jnp.int32)
+    position = t * local_rows + jnp.arange(local_rows, dtype=jnp.int32)
     is_memory = (position < mem) | (position >= mem + tokens)
     use_init = ((reset[:, None] > 0) & is_memory[None, :])[:, :, None]
-    table = jnp.concatenate([init_memory, jnp.zeros((tokens, width), bf16), init_memory], 0)
-    local_table = lax.dynamic_slice_in_dim(table, first_row, local_rows, 0)
-    x_in = jnp.pad(jnp.where(use_init, local_table[None], sequence), pad)
-    c_in = jnp.pad(cotangent, pad)
 
     a_in = jnp.concatenate(
         [query_key_value_weight.transpose(1, 2, 0).reshape(3 * hw, width), output_weight], 0
     )
-    qv_row = jnp.concatenate([qv_bias.reshape(2 * hw), jnp.zeros((width - 2 * hw,), bf16)])
-    bias_in = jnp.concatenate([up_bias[None], qv_row[None], jnp.zeros((14, width), bf16)], 0)
-    zero = jnp.zeros((width,), bf16)
-    vecs = jnp.stack(
-        [out_bias, back_bias, gain_one, shift_one, gain_two, shift_two, zero, zero]
-    ).astype(f32)
-
-    own_starts = lax.dynamic_slice_in_dim(starts, t, 1, 0)[0]
-    docs = jnp.cumsum(own_starts)
-    marker = jnp.full((mem,), -1, jnp.int32)
-    codes = jnp.concatenate([marker, docs, marker]).reshape(planes, local_rows)
-    codes = jnp.pad(codes, ((0, 0), (0, block - local_rows)), constant_values=-2)
-    codes = codes.reshape(planes * block)
-    flag = jnp.broadcast_to(
-        lax.dynamic_slice_in_dim((reset > 0).astype(f32), t, 1, 0)[:, None], (8, 128)
+    qv_row = jnp.pad(qv_bias.reshape(2 * hw), (0, width - 2 * hw))
+    bias_in = jnp.stack(
+        [up_bias, qv_row, out_bias, back_bias, gain_one, shift_one, gain_two, shift_two]
+        + [jnp.zeros((width,), bf16)] * 8
     )
-
-    last = planes * local_rows - mem
-    edges = (mem, 0, last // local_rows * block + last % local_rows)
     ga, gu, gd, dx, y, _, small = layer_call(
         planes,
         heads,
-        edges,
-        x_in,
-        c_in,
+        sequence,
+        cotangent,
         a_in,
         up_weight,
         down_weight,
         bias_in,
-        (vecs, codes[:, None], codes[None, :], flag),
+        init_memory,
+        starts,
+        reset,
     )
 
-    output = y[:, :local_rows]
-    input_grad = jnp.where(use_init, 0.0, dx[:, :local_rows].astype(f32))
+    input_grad = jnp.where(use_init, 0.0, dx.astype(f32))
     ga, gu, gd = ga.astype(f32), gu.astype(f32), gd.astype(f32)
     if dp_size > INNER:
         groups = [[o * INNER + i for o in range(dp_size // INNER)] for i in range(INNER)]
         ga, gu, gd, small = lax.psum((ga, gu, gd, small), "dp", axis_index_groups=groups)
     own = lambda first: lax.dynamic_slice_in_dim(small, first + t, 1, 0)[0]
     return (
-        output,
+        y,
         input_grad,
         ga[: 3 * hw].reshape(3, hw, width).transpose(2, 0, 1),
-        own(10)[: 2 * hw].reshape(2, hw),
+        own(SMALL + 10)[: 2 * hw].reshape(2, hw),
         ga[3 * hw :],
         small[5],
         gu,
@@ -941,7 +972,7 @@
         small[4],
         small[0],
         small[1],
-        small[14 : 14 + mem],
+        small[SMALL : SMALL + mem],
     )
 
 

time: 238 us -> 209 us (0.88)
  Pallas kernels: 210 us -> 190 us
  other arithmetic: 10.4 us -> 4.58 us
    pallas_call x1, Pallas kernels: 210 us -> 190 us  [layer_call(): pl.pallas_call(functools.partial(layer_kernel, planes, heads, block), out...]
    unnamed x37 -> x38, local copies, waits for them, and re-layouts: 3.77 us -> 7.64 us
    select_n x2 -> x1, other arithmetic: 2.79 us -> 0.25 us  [shards(): input_grad = jnp.where(use_init, 0.0, dx.astype(f32))]
where the time goes in v3:
time: 209 us
  Pallas kernels  190 us (91%)
  local copies, waits for them, and re-layouts  13.2 us (6%)
  other arithmetic  4.58 us (2%)
    pallas_call x1, Pallas kernels, layer_call(): pl.pallas_call(functools.partial(layer_kernel, planes, heads, block), out...  190 us
    unnamed x38, local copies, waits for them, and re-layouts  7.64 us

profile of v3, /device:TPU:0, one launch (start us, length us, event | category | flops | bytes accessed | tf_op | source)
XLA Modules:
  0.0 209.0 jit_solution(6866416916183409252)
XLA Ops:
  0.6 0.0 copy-start.5
  0.7 0.0 copy-start.6
  0.7 0.0 copy-start.3
  0.7 2.3 %copy.32.x_in = bf16[4,133,768]{2,1,0:T(8,128)(2,1)} copy(bf16[4,133,768]{2,0,1:T(4,128)(2,1)} %param.17) | data formatting | bytes 1634304 | tf_op args[0]
  2.9 0.0 copy-done.5
  3.0 0.0 copy-start.10
  3.0 0.0 copy-start.11
  3.0 0.0 copy-start.12
  3.0 0.0 copy-start.13
  3.0 0.0 copy-start.14
  3.0 1.0 copy.33.c_in
  4.0 0.0 copy-done.6
  4.0 1.1 pad_maximum_fusion.a_in
  5.1 0.1 reshape.81
  5.2 0.0 copy-done.9
  5.3 0.0 copy-done.13
  5.3 0.0 copy-done.14
  5.4 1.2 stack.39.bias_in
  6.6 190.4 %shard_map.280 = (bf16[768,768]{1,0:T(8,128)(2,1)}, bf16[768,768]{1,0:T(8,128)(2,1)}, bf16[768,768]{1,0:T(8,128)(2,1)}, bf16[4,133,768]{2,1,0:T(8,128)(2,1)}, bf...) custom-call(bf16[4,133,768]{2,1,0:T(8,128)(2,1)} %copy.32.x_in, ...), custom_call_target="tpu_custom_call" | custom-call | tf_op jit(solution)/shard_map/pallas_call | solution.py:853
  197.0 2.4 %copy.34 = bf16[4,133,768]{2,0,1:T(4,128)(2,1)} copy(bf16[4,133,768]{2,1,0:T(8,128)(2,1)} %get-tuple-element.27) | data formatting | bytes 1634304
  199.4 0.1 broadcast_and_fusion
  199.5 0.2 convert_select_fusion
  199.8 1.8 copy.35
  201.6 1.3 slice.41
  202.9 0.7 reshape.83
  203.6 0.9 slice.42
  204.5 0.7 slice_reduce_fusion
  205.1 0.0 copy-done.2
  205.1 1.6 convert_element_type.16
  206.7 0.1 copy-done.1
  206.8 1.6 convert_element_type.17
  208.4 0.6 slice.40
  (32 shorter events, 0.1 us)
Async XLA Ops:
  0.6 2.3 %copy-start.5 = (bf16[4,133,768]{2,0,1:T(4,128)(2,1)S(1)}, bf16[4,133,768]{2,0,1:T(4,128)(2,1)}, u32[]{:S(2)}) copy-start(bf16[4,133,768]{2,0,1:T(4,128)(2,1)} %param.33) | copy-start | bytes 2451460
  0.7 3.3 %copy-start.6 = (bf16[192,768]{1,0:T(8,128)(2,1)S(1)}, bf16[192,768]{1,0:T(8,128)(2,1)}, u32[]{:S(2)}) copy-start(bf16[192,768]{1,0:T(8,128)(2,1)} %param.20) | copy-start | bytes 884740
  0.7 3.3 %copy-start.3 = (bf16[768,3,192]{0,2,1:T(8,128)(2,1)S(1)}, bf16[768,3,192]{0,2,1:T(8,128)(2,1)}, u32[]{:S(2)}) copy-start(bf16[768,3,192]{0,2,1:T(8,128)(2,1)} %param.18) | copy-start | bytes 2654212
  2.9 2.2 %copy-start.8 = (bf16[768]{0:T(1024)(128)(2,1)S(1)}, bf16[768]{0:T(1024)(128)(2,1)}, u32[]{:S(2)}) copy-start(bf16[768]{0:T(1024)(128)(2,1)} %param.23) | copy-start | bytes 4612
  2.9 2.2 %copy-start.15 = (bf16[2,192]{1,0:T(2,128)(2,1)S(1)}, bf16[2,192]{1,0:T(2,128)(2,1)}, u32[]{:S(2)}) copy-start(bf16[2,192]{1,0:T(2,128)(2,1)} %param.19) | copy-start | bytes 2308
  2.9 2.3 %copy-start.9 = (bf16[768]{0:T(1024)(128)(2,1)S(1)}, bf16[768]{0:T(1024)(128)(2,1)}, u32[]{:S(2)}) copy-start(bf16[768]{0:T(1024)(128)(2,1)} %param.21) | copy-start | bytes 4612
  3.0 2.3 %copy-start.10 = (bf16[768]{0:T(1024)(128)(2,1)S(1)}, bf16[768]{0:T(1024)(128)(2,1)}, u32[]{:S(2)}) copy-start(bf16[768]{0:T(1024)(128)(2,1)} %param.25) | copy-start | bytes 4612
  3.0 2.3 %copy-start.11 = (bf16[768]{0:T(1024)(128)(2,1)S(1)}, bf16[768]{0:T(1024)(128)(2,1)}, u32[]{:S(2)}) copy-start(bf16[768]{0:T(1024)(128)(2,1)} %param.26) | copy-start | bytes 4612
  3.0 2.3 %copy-start.12 = (bf16[768]{0:T(1024)(128)(2,1)S(1)}, bf16[768]{0:T(1024)(128)(2,1)}, u32[]{:S(2)}) copy-start(bf16[768]{0:T(1024)(128)(2,1)} %param.27) | copy-start | bytes 4612
  3.0 2.3 %copy-start.13 = (bf16[768]{0:T(1024)(128)(2,1)S(1)}, bf16[768]{0:T(1024)(128)(2,1)}, u32[]{:S(2)}) copy-start(bf16[768]{0:T(1024)(128)(2,1)} %param.28) | copy-start | bytes 4612
  3.0 2.3 %copy-start.14 = (bf16[768]{0:T(1024)(128)(2,1)S(1)}, bf16[768]{0:T(1024)(128)(2,1)}, u32[]{:S(2)}) copy-start(bf16[768]{0:T(1024)(128)(2,1)} %param.29) | copy-start | bytes 4612
  6.6 192.8 %copy-start.16 = (s32[4]{0:T(128)S(1)}, s32[4]{0:T(128)}, u32[]{:S(2)}) copy-start(s32[4]{0:T(128)} %reset_ref.1) | copy-start | bytes 52
  197.0 2.5 %copy-start.4 = (bf16[4,133,768]{2,1,0:T(8,128)(2,1)S(1)}, bf16[4,133,768]{2,1,0:T(8,128)(2,1)}, u32[]{:S(2)}) copy-start(bf16[4,133,768]{2,1,0:T(8,128)(2,1)} %get-tuple-element.22) | copy-start | bytes 2451460
  199.8 1.8 copy-start
  201.6 1.3 copy-start.7
  201.6 3.5 %copy-start.2 = (bf16[768,768]{1,0:T(8,128)(2,1)S(1)}, bf16[768,768]{1,0:T(8,128)(2,1)}, u32[]{:S(2)}) copy-start(bf16[768,768]{1,0:T(8,128)(2,1)} %get-tuple-element.25) | copy-start | bytes 3538948
  205.1 1.7 copy-start.1

commit v4 on v3

--- a/solution.py
+++ b/solution.py
@@ -52,7 +52,8 @@
         return (self.dp, self.plane(j))
 
     def partners(self):
-        return [self.to_core, self.to_x, self.to_y] + [
+        both = (self.to_x[0] + self.to_y[0] - self.dp, self.t)
+        return [self.to_core, self.to_x, self.to_y, both] + [
             self.to_plane(j) for j in range(1, self.planes)
         ]
 
@@ -141,7 +142,8 @@
     block,
     x_in,
     c_in,
-    a_in,
+    qkv_in,
+    o_in,
     u_in,
     d_in,
     bias_in,
@@ -167,10 +169,9 @@
     v_s,
     p2,
     o_s,
-    o3,
-    delta3,
-    d9,
-    ds_s,
+    do_s,
+    delta_s,
+    d_s,
     mask,
     acc,
     xhat_s,
@@ -184,6 +185,8 @@
     one_in,
     z_in,
     sm,
+    sm_core,
+    sm_low,
     sm_in,
     send,
     recv,
@@ -199,7 +202,7 @@
     hp = heads // planes
     hw = hp * DH
     links = Links(send, recv)
-    r = Rows(place, a_in.shape[0])
+    r = Rows(place, a_w.shape[1])
     piece, half = r.piece, r.half
     vec = lambda i: bias_in[2 + i : 3 + i, :].astype(f32)
     add_up = lambda v: jnp.sum(v, axis=0, keepdims=True)
@@ -207,7 +210,7 @@
     def keep(k, src, dst):
         return pltpu.make_async_copy(src, dst, local.at[k])
 
-    ins, weights, g_outs = (a_in, u_in, d_in), (a_w, u_w, d_w), (ga_out, gu_out, gd_out)
+    weights, g_outs = (a_w, u_w, d_w), (ga_out, gu_out, gd_out)
 
     low = t // 2
     middle = mirror_end(t, low, planes) == 1
@@ -231,7 +234,7 @@
                     inside,
                     [
                         links.copy(
-                            ins[w].at[pl.ds(at, piece)],
+                            weights[w].at[t, pl.ds(at, piece)],
                             weights[w].at[t, pl.ds(at, piece)],
                             device,
                             recv_z.at[w, t, n],
@@ -301,7 +304,7 @@
 
     def release(w):
         way = gather[w]
-        links.finish([c for _, z in way.z for c in z])
+        links.finish([c for _, z in way.own + way.z for c in z])
         links.finish([c for part in way.one + way.two + way.core for c in part])
 
     def spread(sends, d):
@@ -317,6 +320,14 @@
         else:
             go(1, 3)
             go(2, 1)
+
+    def to_next(sends):
+        pl.when((t == 0) | (t == 2))(lambda: start(sends[0:1]))
+        pl.when((t == 1) | (t == 3))(lambda: start(sends[2:3]))
+
+    def to_middle(sends):
+        pl.when((t == 0) | (t == 2))(lambda: start(sends[2:3]))
+        pl.when((t == 1) | (t == 3))(lambda: start(sends[0:1]))
 
     back_order = (2, 1, 3, 0)
     ways = []
@@ -421,32 +432,49 @@
     y_send = [links.copy(cs.at[place.plane(j)], y_out.at[t], place.to_plane(j)) for j in others]
     dx_send = [links.copy(xs.at[place.plane(j)], dx_out.at[t], place.to_plane(j)) for j in others]
     hops = []
+    to_both = (place.to_x[0] + place.to_y[0] - place.dp, t)
     for e in range(2):
-        mine, got = sm.at[e], sm_in.at[e]
+        mine, got = sm_low.at[e], sm_in.at[e]
         hops.append(
             [
-                [links.copy(mine.at[0], got.at[0], place.to_core)],
-                [links.copy(mine.at[1], got.at[1], place.to_x)],
-                [links.copy(mine.at[2], got.at[2], place.to_y)],
-                [links.copy(mine.at[3], got.at[2 + j], place.to_plane(j)) for j in others],
+                [links.copy(sm.at[e], sm_core.at[e], place.to_core)],
+                [
+                    links.copy(mine.at[0], got.at[n], to)
+                    for n, to in enumerate((place.to_x, place.to_y, to_both))
+                ],
+                [links.copy(mine.at[1], got.at[2 + j], place.to_plane(j)) for j in others],
             ]
         )
 
+    def in_order(parts, device):
+        total = jnp.zeros_like(parts[0])
+        for n in range(len(parts)):
+            for part, who in zip(parts, device):
+                total = total + jnp.where(who == n, part, 0.0)
+        return total
+
     def hop(e, n):
         arrive(hops[e][n])
-        if n < 3:
-            sm[e, n + 1] = sm[e, n] + sm_in[e, n]
-            start(hops[e][n + 1])
+        low = lambda k: sm_in[e, k].astype(f32)
+        if n == 0:
+            sm_low[e, 0] = (sm[e] + sm_core[e]).astype(bf16)
+        elif n == 1:
+            x, y = place.x, place.y
+            near = [2 * y + x, 2 * y + 1 - x, 2 * (1 - y) + x, 2 * (1 - y) + 1 - x]
+            parts = [sm_low[e, 0].astype(f32)] + [low(k) for k in range(3)]
+            sm_low[e, 1] = in_order(parts, near).astype(bf16)
+        else:
+            planes_of = [lax.rem(t + planes - j, planes) for j in range(planes)]
+            total = in_order([sm_low[e, 1].astype(f32)] + [low(2 + j) for j in others], planes_of)
+            small_ref[e * SMALL : (e + 1) * SMALL, :] = total
             return
-        parts = [sm[e, 3]] + [sm_in[e, 2 + j] for j in others]
-        total = jnp.zeros_like(parts[0])
-        for s in range(planes):
-            for j in range(planes):
-                hit = lax.rem(t + planes - j, planes) == s
-                total = total + jnp.where(hit, parts[j], 0.0)
-        small_ref[e * SMALL : (e + 1) * SMALL, :] = total
-
-    own = [keep(w, ins[w], weights[w].at[t]) for w in range(3)]
+        start(hops[e][n + 1])
+
+    own_a = [
+        keep(0, qkv_in, a_w.at[t, pl.ds(0, 3 * hw)]),
+        keep(5, o_in, a_w.at[t, pl.ds(3 * hw, hw)]),
+    ]
+    own_u, own_d = keep(1, u_in, u_w.at[t]), keep(2, d_in, d_w.at[t])
     own_x = keep(3, x_in.at[t], xs.at[t])
     own_c = keep(4, c_in.at[t], cs.at[t])
     own_y = keep(6, cs.at[t], y_out.at[t])
@@ -457,10 +485,14 @@
 
     p_save = lambda m: keep(12 + m % 2, p2.at[m % 2], p_at(m))
 
-    start([own_x, *own, own_c])
+    start([*own_a, own_u, own_d, own_x, own_c])
     place.greet()
+    for c in own_a:
+        c.wait()
     get_own(0)
     start(b_send)
+    own_u.wait()
+    get_own(1)
     spread(x_send, 0)
 
     bias[t] = bias_in[...]
@@ -482,29 +514,40 @@
         docs = jnp.where((token < 0) | (token >= tokens), -1.0, docs)
         return jnp.where(inside >= real, -2.0, docs)
 
-    kc = codes(docs, 1)[0:1, :]
-    qcodes = codes(docs.T, 0)[:, 0:1]
+    qc = codes(docs, 1)[0:1, :]
+    kcodes = codes(docs.T, 0)[:, 0:1]
     for c in range(planes):
         span = slice(c * block, (c + 1) * block)
-        qc = qcodes[span, :]
+        kc = kcodes[span, :]
         allowed = ((qc == kc) | (qc < 0) | (kc < 0)) & (kc != -2.0)
         mask[span, :] = jnp.where(allowed, 0.0, NEGATIVE)
     for e in range(2):
-        sm[e, 0] = jnp.zeros((SMALL, width), f32)
+        sm[e] = jnp.zeros((SMALL, width), f32)
 
     get_stage(0, 1)
+    get_stage(1, 1)
     spread(x_send, 1)
+    get_one(0, 1)
+    pl.when(middle)(lambda: get_one(0, 2))
     get_stage(0, 2)
+    get_one(1, 1)
+    get_stage(1, 2)
     spread(x_send, 2)
-    get_own(1)
+    own_d.wait()
     get_own(2)
-    get_one(0, 1)
-    get_one(0, 2)
     get_two(0, 1)
+    pl.when(~middle)(lambda: get_one(0, 2))
     get_stage(0, 3)
+    get_two(1, 1)
+    get_one(1, 2)
+    get_stage(1, 3)
     get_two(0, 2)
     get_one(0, 3)
-    for c in (own_x, *own, own_c):
+    get_two(1, 2)
+    get_one(1, 3)
+    get_two(0, 3)
+    get_two(1, 3)
+    for c in (own_x, own_c):
         c.wait()
     arrive(x_send)
     arrive(b_send)
@@ -518,27 +561,23 @@
     acc[...] = x_s[...].reshape(rows, width).astype(f32) + vec(0)
 
     forward_pokes = [
-        (0, lambda: get_two(0, 3)),
-        (1, lambda: get_stage(1, 1)),
-        (2, lambda: get_stage(2, 1)),
-        (2, lambda: spread(c_send, 0)),
-        (2, lambda: spread(c_send, 1)),
-        (3, lambda: get_one(1, 1)),
-        (4, lambda: get_stage(1, 2)),
-        (4, lambda: get_one(2, 1)),
-        (5, lambda: get_two(1, 1)),
-        (5, lambda: get_stage(2, 2)),
-        (5, lambda: spread(c_send, 2)),
-        (6, lambda: get_one(1, 2)),
-        (7, lambda: get_two(2, 1)),
-        (7, lambda: get_one(2, 2)),
-        (8, lambda: get_two(1, 2)),
-        (8, lambda: get_stage(1, 3)),
-        (9, lambda: get_stage(2, 3)),
-        (9, lambda: get_two(2, 2)),
-        (10, lambda: get_one(1, 3)),
-        (11, lambda: get_one(2, 3)),
+        (0, 3, lambda: get_stage(2, 1)),
+        (0, 3, lambda: spread(c_send, 0)),
+        (0, 3, lambda: spread(c_send, 1)),
+        (1, 3, lambda: get_one(2, 1)),
+        (2, 0, lambda: get_stage(2, 2)),
+        (2, 0, lambda: spread(c_send, 2)),
+        (3, 0, lambda: get_two(2, 1)),
+        (3, 0, lambda: get_one(2, 2)),
+        (3, 1, lambda: get_stage(2, 3)),
     ]
+
+    def poke_at(pokes, *now):
+        for *when, poke in pokes:
+            hit = now[0] == when[0]
+            for a, b in zip(now[1:], when[1:]):
+                hit = hit & (a == b)
+            pl.when(hit)(poke)
 
     def forward_order(j):
         picked = t
@@ -546,42 +585,38 @@
             picked = jnp.where(j == i, slot_shard(i), picked)
         return picked
 
+    head_feats = lambda i: pl.ds(pl.multiple_of(i * DH, DH), DH)
+
     def attention(j):
         s = forward_order(j)
         for i in others:
             pl.when(j == i)(lambda: get_core(0, i))
 
+        poke_at([p for p in forward_pokes if p[1] == 0], j, 0)
         x = x_s[...].reshape(rows, width)
-        qkv = dot(x, a_w[s, 0 : 3 * hw, :], NT)
-        b = bias[s, 1:2, :].astype(f32)
+        qkv = dot(a_w[s, 0 : 3 * hw, :], x, NT)
+        b = bias[s].astype(f32).T[:, 1:2]
+        q = ((qkv[0:hw] + b[0:hw]).astype(bf16).astype(f32) * (DH**-0.5)).astype(bf16)
+        k = qkv[hw : 2 * hw].astype(bf16)
+        v = (qkv[2 * hw :] + b[hw : 2 * hw]).astype(bf16)
         for i in range(hp):
-            cols = slice(i * DH, (i + 1) * DH)
-            bq, bv = b[:, cols], b[:, hw + i * DH : hw + (i + 1) * DH]
-            q = (qkv[:, cols] + bq).astype(bf16)
-            q_s[s * hp + i] = (q.astype(f32) * (DH**-0.5)).astype(bf16)
-            k_s[s * hp + i] = qkv[:, hw + i * DH : hw + (i + 1) * DH].astype(bf16)
-            v_s[s * hp + i] = (qkv[:, 2 * hw + i * DH : 2 * hw + (i + 1) * DH] + bv).astype(bf16)
+            feats = slice(i * DH, (i + 1) * DH)
+            q_s[s * hp + i], k_s[s * hp + i], v_s[s * hp + i] = q[feats], k[feats], v[feats]
 
         def head(i):
             h = s * hp + i
             m = j * hp + i
-            for n, poke in forward_pokes:
-                pl.when(m == n)(poke)
+            poke_at([p for p in forward_pokes if p[1] > 0], j, i + 1)
             pl.when(m >= 2)(lambda: p_save(m).wait())
-            k, v = k_s[h], v_s[h]
-            for c in range(planes):
-                span = pl.ds(c * block, block)
-                scores = dot(q_s[h, span, :], k, NT) + mask[span, :]
-                e = jnp.exp(scores - jnp.max(scores, axis=1, keepdims=True))
-                p = (e / jnp.sum(e, axis=1, keepdims=True)).astype(bf16)
-                p2[m % 2, span, :] = p
-                o3[i, span, :] = dot(p, v).astype(bf16)
+            scores = dot(k_s[h], q_s[h], TN) + mask[...]
+            e = jnp.exp(scores - jnp.max(scores, axis=0, keepdims=True))
+            p = (e * (1.0 / jnp.sum(e, axis=0, keepdims=True))).astype(bf16)
+            p2[m % 2] = p
+            o_s[s, head_feats(i), :] = dot(v_s[h], p).astype(bf16)
             keep(12 + m % 2, p2.at[m % 2], p_at(h)).start()
 
         each(hp, head)
-        o = jnp.concatenate([o3[i] for i in range(hp)], axis=1)
-        o_s[s] = o
-        acc[...] += dot(o, a_w[s, 3 * hw :, :])
+        acc[...] += dot(o_s[s], a_w[s, 3 * hw :, :], TN)
 
     each(planes, attention)
 
@@ -598,13 +633,13 @@
         acc[span, :] = h + vec(1)
 
     each(planes, first_norm)
-    get_two(1, 3)
+    get_one(2, 3)
 
     def up(j):
         s = forward_order(j)
         for i in others:
             pl.when(j == i)(lambda: get_core(1, i))
-        pl.when(j == 1)(lambda: get_two(2, 3))
+        pl.when(j == 0)(lambda: get_two(2, 2))
         for c in range(planes):
             span = pl.ds(c * block, block)
             z = dot(hb_s[span, :], u_w[s]) + bias[s, 0:1, :].astype(f32)
@@ -613,6 +648,7 @@
             dz_s[s, span, :] = (phi + z * jnp.exp(-0.5 * z * z) * 0.3989422804014327).astype(bf16)
 
     each(planes, up)
+    get_two(2, 3)
 
     def down(j):
         s = forward_order(j)
@@ -646,31 +682,28 @@
         return sums[0] + add_up(g * xhat), sums[1] + add_up(g), sums[2] + add_up(g2)
 
     sums = lax.fori_loop(0, planes, second_norm, (zero, zero, zero))
-    sm[0, 0, 0:3, :] = jnp.concatenate(list(sums), axis=0)
+    sm[0, 0:3, :] = jnp.concatenate(list(sums), axis=0)
     start(y_send)
     own_y.start()
 
-    def poke_at(n, pokes):
-        for k, poke in pokes:
-            pl.when(n == k)(poke)
-
-    down_pokes = [(2, lambda: part_core(2, 0)), (3, lambda: part_core(2, 1))]
+    down_pokes = [
+        (3, lambda: part_core(2, 0)),
+    ]
     up_pokes = [
-        (0, lambda: part_core(2, 2)),
-        (0, lambda: part_pair(2, 0)),
-        (1, lambda: part_core(2, 3)),
-        (2, lambda: part_pair(2, 1)),
-        (2, lambda: part_core(1, 0)),
+        (0, lambda: part_core(2, 1)),
+        (1, lambda: part_core(2, 2)),
+        (2, lambda: part_pair(2, 0)),
+        (2, lambda: part_core(2, 3)),
+        (3, lambda: part_core(1, 0)),
+        (3, lambda: part_pair(2, 1)),
         (3, lambda: part_core(1, 1)),
     ]
 
     def back_down(n):
         s = back_shard(n)
-        poke_at(n, down_pokes)
-        for c in range(planes):
-            span = pl.ds(c * block, block)
-            du = dot(gb_s[span, :], d_w[s], NT)
-            dz_s[s, span, :] = (du * dz_s[s, span, :].astype(f32)).astype(bf16)
+        poke_at(down_pokes, n)
+        du = dot(gb_s[...], d_w[s], NT)
+        dz_s[s] = (du * dz_s[s].astype(f32)).astype(bf16)
         d_w[s] = dot(act_s[s], gb_s[...], TN).astype(bf16)
         for k in range(planes):
             pl.when(n == k)(ways[2].core[k][0].start)
@@ -680,9 +713,9 @@
 
     def back_up(n):
         s = back_shard(n)
-        poke_at(n, up_pokes)
+        poke_at(up_pokes, n)
         dz = dz_s[s]
-        sm[0, 0, pl.ds(6 + s, 1), :] = add_up(dz.astype(f32))
+        sm[0, pl.ds(6 + s, 1), :] = add_up(dz.astype(f32))
         acc[...] += dot(dz, u_w[s], NT)
         u_w[s] = dot(hb_s[...], dz, TN).astype(bf16)
         for k in range(planes):
@@ -697,6 +730,9 @@
         12 + m % 2, p_at(back_shard(m // hp) * hp + m % hp), p2.at[m % 2]
     )
     p_load(0).start()
+
+    part_pair(2, 2)
+    part_core(1, 2)
 
     def back_first_norm(c, sums):
         span = pl.ds(pl.multiple_of(c * block, block), block)
@@ -713,75 +749,64 @@
         return sums[0] + add_up(g * xhat), sums[1] + add_up(g), sums[2] + add_up(g1)
 
     sums = lax.fori_loop(0, planes, back_first_norm, (zero, zero, zero))
-    sm[0, 0, 3:6, :] = jnp.concatenate(list(sums), axis=0)
+    sm[0, 3:6, :] = jnp.concatenate(list(sums), axis=0)
     start(hops[0][0])
-    part_pair(2, 2)
-    part_one(2, 0)
-
     back_pokes = [
-        (0, lambda: part_core(1, 2)),
-        (0, lambda: part_pair(2, 3)),
-        (1, lambda: part_core(1, 3)),
-        (1, lambda: part_one(2, 1)),
-        (1, lambda: hop(0, 0)),
-        (2, lambda: part_pair(1, 0)),
-        (3, lambda: part_pair(1, 1)),
-        (3, lambda: part_one(2, 2)),
-        (3, lambda: hop(0, 1)),
-        (4, lambda: part_core(0, 0)),
-        (5, lambda: part_pair(1, 2)),
-        (5, lambda: part_one(2, 3)),
-        (5, lambda: hop(0, 2)),
-        (6, lambda: part_pair(1, 3)),
-        (6, lambda: part_one(1, 0)),
-        (7, lambda: part_core(0, 1)),
-        (7, lambda: part_pair(0, 0)),
-        (8, lambda: part_one(1, 1)),
-        (9, lambda: part_one(1, 2)),
-        (9, lambda: part_one(0, 0)),
-        (9, lambda: part_pair(0, 1)),
-        (10, lambda: part_core(0, 2)),
-        (10, lambda: part_one(1, 3)),
-        (10, lambda: after_z(2)),
-        (11, lambda: part_one(0, 1)),
-        (11, lambda: after_back1(2)),
+        (0, 0, lambda: part_one(2, 0)),
+        (0, 1, lambda: part_core(1, 3)),
+        (0, 2, lambda: hop(0, 0)),
+        (0, 2, lambda: part_pair(2, 3)),
+        (0, 4, lambda: part_pair(1, 0)),
+        (1, 0, lambda: part_one(2, 1)),
+        (1, 3, lambda: part_pair(1, 1)),
+        (1, 3, lambda: part_core(0, 0)),
+        (1, 3, lambda: part_one(2, 2)),
+        (2, 0, lambda: part_pair(1, 2)),
+        (2, 3, lambda: part_pair(1, 3)),
+        (2, 3, lambda: hop(0, 1)),
+        (2, 3, lambda: part_core(0, 1)),
+        (2, 4, lambda: part_one(2, 3)),
+        (2, 4, lambda: after_z(2)),
+        (3, 0, lambda: part_one(1, 0)),
+        (3, 0, lambda: hop(0, 2)),
+        (3, 1, lambda: part_one(1, 1)),
+        (3, 3, lambda: part_core(0, 2)),
+        (3, 3, lambda: part_pair(0, 0)),
+        (3, 4, lambda: part_one(1, 2)),
     ]
 
     def back_attention(n):
         s = back_shard(n)
-        do = dot(gb_s[...], a_w[s, 3 * hw :, :], NT).astype(bf16)
-        o = o_s[s]
-        prod = do.astype(f32) * o.astype(f32)
+        poke_at([p for p in back_pokes if p[1] == 0], n, 0)
+        do = dot(a_w[s, 3 * hw :, :], gb_s[...], NT).astype(bf16)
+        do_s[...] = do
+        prod = do.astype(f32) * o_s[s].astype(f32)
         for i in range(hp):
-            cols = slice(i * DH, (i + 1) * DH)
-            o3[i] = do[:, cols]
-            delta3[i] = jnp.sum(prod[:, cols], axis=1, keepdims=True)
+            delta_s[i] = add_up(prod[i * DH : (i + 1) * DH])
 
         def head(i):
             h = s * hp + i
             m = n * hp + i
             p_load(m).wait()
             pl.when(m + 1 < heads)(lambda: p_load(m + 1).start())
-            poke_at(m, back_pokes)
+            poke_at([p for p in back_pokes if 0 < p[1] < 4], n, i + 1)
             slot = m % 2
-            k, v = k_s[h], v_s[h]
-            for c in range(planes):
-                span = pl.ds(c * block, block)
-                dp = dot(o3[i, span, :], v, NT)
-                ds = (p2[slot, span, :].astype(f32) * (dp - delta3[i, span, :])).astype(bf16)
-                ds_s[span, :] = ds
-                d9[i, span, :] = (dot(ds, k) * (DH**-0.5)).astype(bf16)
-            d9[hp + i] = dot(ds_s[...], q_s[h], TN).astype(bf16)
-            d9[2 * hp + i] = dot(p2[slot], o3[i], TN).astype(bf16)
+            p, do = p2[slot], do_s[head_feats(i), :]
+            dp = dot(v_s[h], do, TN)
+            ds = (p.astype(f32) * (dp - delta_s[i])).astype(bf16)
+            d_s[head_feats(i), :] = (dot(k_s[h], ds) * (DH**-0.5)).astype(bf16)
+            d_s[head_feats(hp + i), :] = dot(q_s[h], ds, NT).astype(bf16)
+            d_s[head_feats(2 * hp + i), :] = dot(do, p, NT).astype(bf16)
 
         each(hp, head)
-        dqkv = jnp.concatenate([d9[i] for i in range(3 * hp)], axis=1)
-        sums = add_up(dqkv.astype(f32))
-        sm[1, 0, pl.ds(10 + s, 1), 0:hw] = sums[:, 0:hw]
-        sm[1, 0, pl.ds(10 + s, 1), hw : 2 * hw] = sums[:, 2 * hw :]
-        acc[...] += dot(dqkv, a_w[s, 0 : 3 * hw, :])
-        a_w[s, 0 : 3 * hw, :] = dot(dqkv, x_s[...].reshape(rows, width), TN).astype(bf16)
-        a_w[s, 3 * hw :, :] = dot(o, gb_s[...], TN).astype(bf16)
+        poke_at([p for p in back_pokes if p[1] == 4], n, 4)
+        dqkv = d_s[...]
+        sums = dot(jnp.ones((8, rows), bf16), dqkv, NT)[0:1, :]
+        sm[1, pl.ds(10 + s, 1), 0:hw] = sums[:, 0:hw]
+        sm[1, pl.ds(10 + s, 1), hw : 2 * hw] = sums[:, 2 * hw :]
+        acc[...] += dot(dqkv, a_w[s, 0 : 3 * hw, :], TN)
+        a_w[s, 0 : 3 * hw, :] = dot(dqkv, x_s[...].reshape(rows, width)).astype(bf16)
+        a_w[s, 3 * hw :, :] = dot(o_s[s], gb_s[...]).astype(bf16)
         for k in range(planes):
             pl.when(n == k)(ways[0].core[k][0].start)
 
@@ -790,33 +815,36 @@
 
     for c in range(planes):
         xs[c] = acc[c * block : c * block + real, :].astype(bf16)
-    start(dx_send[1:2])
+    part_one(1, 3)
+    to_next(dx_send)
     own_dx.start()
     dx_last = (planes - 1) * block + last
     both = acc[0:mem, :] + acc[dx_last : dx_last + mem, :]
-    sm[1, 0, 0:mem, :] = jnp.where(afresh, both, 0.0)
+    sm[1, 0:mem, :] = jnp.where(afresh, both, 0.0)
     start(hops[1][0])
+    part_pair(0, 1)
     part_core(0, 3)
+    hop(1, 0)
+    after_back1(2)
     part_pair(0, 2)
-    hop(1, 0)
     after_z(1)
+    part_one(0, 0)
+    part_one(0, 1)
+    part_pair(0, 3)
+    hop(1, 1)
     after_back2(2)
     part_one(0, 2)
-    part_pair(0, 3)
-    start(dx_send[0:1])
-    hop(1, 1)
+    start(dx_send[1:2])
     after_back1(1)
+    after_back3(2)
+    part_one(0, 3)
+    to_middle(dx_send)
+    after_z(0)
+    after_back2(1)
+    after_back3(1)
+    after_back1(0)
+    after_back2(0)
     hop(1, 2)
-    start(dx_send[2:3])
-    part_one(0, 3)
-    after_back2(1)
-    after_z(0)
-    after_back1(0)
-    hop(0, 3)
-    after_back3(2)
-    after_back2(0)
-    hop(1, 3)
-    after_back3(1)
     after_back3(0)
 
     arrive(y_send)
@@ -828,13 +856,13 @@
     links.finish()
 
 
-def layer_call(planes, heads, x_in, c_in, a_in, u_in, d_in, bias_in, init, starts, reset):
+def layer_call(planes, heads, x_in, c_in, qkv_in, o_in, u_in, d_in, bias_in, init, starts, reset):
     real, width = x_in.shape[1:]
     block = -(-real // 16) * 16
     rows = planes * block
     hp = heads // planes
     hw = hp * DH
-    shard = a_in.shape
+    shard = u_in.shape
     hidden = shard[1]
     piece, half = shard[0] // (2 * INNER), shard[0] // 2
     S = jax.ShapeDtypeStruct
@@ -853,7 +881,7 @@
     return pl.pallas_call(
         functools.partial(layer_kernel, planes, heads, block),
         out_shape=outs,
-        in_specs=[any_spec] * 5 + [vmem_spec] * 3 + [pl.BlockSpec(memory_space=pltpu.SMEM)],
+        in_specs=[any_spec] * 6 + [vmem_spec] * 3 + [pl.BlockSpec(memory_space=pltpu.SMEM)],
         out_specs=[any_spec] * 6 + [vmem_spec],
         scratch_shapes=[
             V((planes, *shard), bf16),
@@ -863,15 +891,14 @@
             V((planes, real, width), bf16),
             V((planes, block, width), bf16),
             V((planes, *bias_in.shape), bf16),
-            V((heads, rows, DH), bf16),
-            V((heads, rows, DH), bf16),
-            V((heads, rows, DH), bf16),
+            V((heads, DH, rows), bf16),
+            V((heads, DH, rows), bf16),
+            V((heads, DH, rows), bf16),
             V((2, rows, rows), bf16),
-            V((planes, rows, hw), bf16),
-            V((hp, rows, DH), bf16),
-            V((hp, rows, 1), f32),
-            V((3 * hp, rows, DH), bf16),
-            V((rows, rows), bf16),
+            V((planes, hw, rows), bf16),
+            V((hw, rows), bf16),
+            V((hp, 1, rows), f32),
+            V((3 * hw, rows), bf16),
             V((rows, rows), f32),
             V((rows, width), f32),
             V((rows, width), f32),
@@ -884,8 +911,10 @@
             V((3, 2, planes, 2 * piece, hidden), bf16),
             V((3, 2, planes, piece, hidden), bf16),
             V((3, planes - 1, 2, piece, hidden), bf16),
-            V((2, 4, SMALL, width), f32),
-            V((2, 2 + planes, SMALL, width), f32),
+            V((2, SMALL, width), f32),
+            V((2, SMALL, width), f32),
+            V((2, 2, SMALL, width), bf16),
+            V((2, 2 + planes, SMALL, width), bf16),
             pltpu.SemaphoreType.DMA((LINKS,)),
             pltpu.SemaphoreType.DMA((LINKS,)),
             pltpu.SemaphoreType.DMA((3, planes, 2)),
@@ -894,7 +923,7 @@
         compiler_params=pltpu.CompilerParams(
             collective_id=0, has_side_effects=True, vmem_limit_bytes=63 * MIB
         ),
-    )(x_in, c_in, a_in, u_in, d_in, bias_in, init, starts, reset)
+    )(x_in, c_in, qkv_in, o_in, u_in, d_in, bias_in, init, starts, reset)
 
 
 def shards(
@@ -923,15 +952,13 @@
     tokens = starts.shape[1]
     hw = query_key_value_weight.shape[2]
     heads = hw * planes // DH
-    assert segs == planes == 4 and mem <= local_rows and dp_size % INNER == 0
+    assert segs == planes == 4 and 4 * hw == up_weight.shape[1] and mem <= local_rows and dp_size % INNER == 0
     t = lax.axis_index("tensor")
     position = t * local_rows + jnp.arange(local_rows, dtype=jnp.int32)
     is_memory = (position < mem) | (position >= mem + tokens)
     use_init = ((reset[:, None] > 0) & is_memory[None, :])[:, :, None]
 
-    a_in = jnp.concatenate(
-        [query_key_value_weight.transpose(1, 2, 0).reshape(3 * hw, width), output_weight], 0
-    )
+    qkv_in = query_key_value_weight.transpose(1, 2, 0).reshape(3 * hw, width)
     qv_row = jnp.pad(qv_bias.reshape(2 * hw), (0, width - 2 * hw))
     bias_in = jnp.stack(
         [up_bias, qv_row, out_bias, back_bias, gain_one, shift_one, gain_two, shift_two]
@@ -942,7 +969,8 @@
         heads,
         sequence,
         cotangent,
-        a_in,
+        qkv_in,
+        output_weight,
         up_weight,
         down_weight,
         bias_in,

time: 209 us -> 192 us (0.919); the launches traced: 209 us -> 189 us
  Pallas kernels: 190 us -> 172 us
    pallas_call x1, Pallas kernels: 190 us -> 172 us  [layer_call(): pl.pallas_call(functools.partial(layer_kernel, planes, heads, block), out...]
    unnamed x38 -> x34, local copies, waits for them, and re-layouts: 7.64 us -> 7.54 us
where the time goes in v4:
time: 192 us; the launch traced here: 189 us
  Pallas kernels  172 us (90%)
  local copies, waits for them, and re-layouts  13.1 us (7%)
  other arithmetic  3.49 us (2%)
    pallas_call x1, Pallas kernels, layer_call(): pl.pallas_call(functools.partial(layer_kernel, planes, heads, block), out...  172 us
    unnamed x34, local copies, waits for them, and re-layouts  7.54 us

profile of v4, /device:TPU:0, one launch (start us, length us, event | category | flops | bytes accessed | tf_op | source)
XLA Modules:
  0.0 189.1 jit_solution(15736390798560256923)
XLA Ops:
  0.6 0.0 copy-start.4
  0.7 0.0 copy-start.6
  0.7 0.0 copy-start.13
  0.7 0.0 copy-start.7
  0.7 0.0 copy-start.8
  0.7 0.0 copy-start.9
  0.7 0.0 copy-start.10
  0.7 0.0 copy-start.11
  0.7 0.0 copy-start.12
  0.7 2.2 %copy.32.x_in = bf16[4,133,768]{2,1,0:T(8,128)(2,1)} copy(bf16[4,133,768]{2,0,1:T(4,128)(2,1)} %param.17) | data formatting | bytes 1634304 | tf_op args[0]
  2.9 0.0 copy-done.4
  2.9 1.0 copy.33.c_in
  3.9 0.0 copy-done.13
  3.9 0.1 reshape.81
  4.0 0.0 copy-done.8
  4.1 0.0 copy-done.9
  4.2 1.2 stack.39.bias_in
  5.4 171.7 %shard_map.280 = (bf16[768,768]{1,0:T(8,128)(2,1)}, bf16[768,768]{1,0:T(8,128)(2,1)}, bf16[768,768]{1,0:T(8,128)(2,1)}, bf16[4,133,768]{2,1,0:T(8,128)(2,1)}, bf...) custom-call(bf16[4,133,768]{2,1,0:T(8,128)(2,1)} %copy.32.x_in, ...), custom_call_target="tpu_custom_call" | custom-call | tf_op jit(solution)/shard_map/pallas_call | solution.py:881
  177.1 2.4 %copy.34 = bf16[4,133,768]{2,0,1:T(4,128)(2,1)} copy(bf16[4,133,768]{2,1,0:T(8,128)(2,1)} %get-tuple-element.27) | data formatting | bytes 1634304
  179.6 0.1 broadcast_and_fusion
  179.7 0.2 convert_select_fusion
  179.9 1.8 copy.35
  181.7 1.3 slice.41
  183.1 0.0 copy-done.5
  183.1 0.7 reshape.83
  183.7 0.9 slice.42
  184.6 0.7 slice_reduce_fusion
  185.2 0.0 copy-done.2
  185.3 1.6 convert_element_type.16
  186.8 0.1 copy-done.1
  186.9 1.6 convert_element_type.17
  188.5 0.6 slice.40
  (27 shorter events, 0.1 us)
Async XLA Ops:
  0.6 2.3 %copy-start.4 = (bf16[4,133,768]{2,0,1:T(4,128)(2,1)S(1)}, bf16[4,133,768]{2,0,1:T(4,128)(2,1)}, u32[]{:S(2)}) copy-start(bf16[4,133,768]{2,0,1:T(4,128)(2,1)} %param.33) | copy-start | bytes 2451460
  0.7 3.2 %copy-start.6 = (bf16[768]{0:T(1024)(128)(2,1)S(1)}, bf16[768]{0:T(1024)(128)(2,1)}, u32[]{:S(2)}) copy-start(bf16[768]{0:T(1024)(128)(2,1)} %param.23) | copy-start | bytes 4612
  0.7 3.2 %copy-start.13 = (bf16[2,192]{1,0:T(2,128)(2,1)S(1)}, bf16[2,192]{1,0:T(2,128)(2,1)}, u32[]{:S(2)}) copy-start(bf16[2,192]{1,0:T(2,128)(2,1)} %param.19) | copy-start | bytes 2308
  0.7 3.3 %copy-start.7 = (bf16[768]{0:T(1024)(128)(2,1)S(1)}, bf16[768]{0:T(1024)(128)(2,1)}, u32[]{:S(2)}) copy-start(bf16[768]{0:T(1024)(128)(2,1)} %param.21) | copy-start | bytes 4612
  0.7 3.4 %copy-start.8 = (bf16[768]{0:T(1024)(128)(2,1)S(1)}, bf16[768]{0:T(1024)(128)(2,1)}, u32[]{:S(2)}) copy-start(bf16[768]{0:T(1024)(128)(2,1)} %param.25) | copy-start | bytes 4612
  0.7 3.4 %copy-start.9 = (bf16[768]{0:T(1024)(128)(2,1)S(1)}, bf16[768]{0:T(1024)(128)(2,1)}, u32[]{:S(2)}) copy-start(bf16[768]{0:T(1024)(128)(2,1)} %param.26) | copy-start | bytes 4612
  0.7 3.4 %copy-start.10 = (bf16[768]{0:T(1024)(128)(2,1)S(1)}, bf16[768]{0:T(1024)(128)(2,1)}, u32[]{:S(2)}) copy-start(bf16[768]{0:T(1024)(128)(2,1)} %param.27) | copy-start | bytes 4612
  0.7 3.4 %copy-start.11 = (bf16[768]{0:T(1024)(128)(2,1)S(1)}, bf16[768]{0:T(1024)(128)(2,1)}, u32[]{:S(2)}) copy-start(bf16[768]{0:T(1024)(128)(2,1)} %param.28) | copy-start | bytes 4612
  0.7 3.4 %copy-start.12 = (bf16[768]{0:T(1024)(128)(2,1)S(1)}, bf16[768]{0:T(1024)(128)(2,1)}, u32[]{:S(2)}) copy-start(bf16[768]{0:T(1024)(128)(2,1)} %param.29) | copy-start | bytes 4612
  5.4 174.1 %copy-start.14 = (s32[4]{0:T(128)S(1)}, s32[4]{0:T(128)}, u32[]{:S(2)}) copy-start(s32[4]{0:T(128)} %reset_ref.1) | copy-start | bytes 52
  177.1 2.5 %copy-start.3 = (bf16[4,133,768]{2,1,0:T(8,128)(2,1)S(1)}, bf16[4,133,768]{2,1,0:T(8,128)(2,1)}, u32[]{:S(2)}) copy-start(bf16[4,133,768]{2,1,0:T(8,128)(2,1)} %get-tuple-element.22) | copy-start | bytes 2451460
  179.9 1.8 copy-start
  181.7 1.3 copy-start.5
  181.7 3.5 %copy-start.2 = (bf16[768,768]{1,0:T(8,128)(2,1)S(1)}, bf16[768,768]{1,0:T(8,128)(2,1)}, u32[]{:S(2)}) copy-start(bf16[768,768]{1,0:T(8,128)(2,1)} %get-tuple-element.25) | copy-start | bytes 3538948
  185.3 1.7 copy-start.1

commit v5 on v4

--- a/solution.py
+++ b/solution.py
@@ -131,8 +131,8 @@
     pass
 
 
-LINKS = 200
-LOCALS = 24
+LINKS = 197
+LOCALS = 16
 SMALL = 16
 
 
@@ -160,6 +160,10 @@
     a_w,
     u_w,
     d_w,
+    raw,
+    x_go,
+    c_go,
+    y_got,
     xs,
     cs,
     x_s,
@@ -375,8 +379,16 @@
         ways.append(way)
 
     def add_rows(g, s, at, size, got):
-        span = pl.ds(at, size)
-        g[s, span, :] = (g[s, span, :].astype(f32) + got.astype(f32)).astype(bf16)
+        def some(n):
+            here = pl.multiple_of(n * piece, piece)
+            span = pl.ds(pl.multiple_of(at + here, 16), piece)
+            more = got[pl.ds(here, piece), :].astype(f32)
+            g[s, span, :] = (g[s, span, :].astype(f32) + more).astype(bf16)
+
+        if size == piece:
+            some(0)
+        else:
+            each(size // piece, some)
 
     def back_shard(n):
         j = 0
@@ -386,21 +398,21 @@
 
     def part_core(w, i):
         arrive(ways[w].core[i])
-        add_rows(weights[w], back_shard(i), r.mine, half, half_in[w, i])
+        add_rows(weights[w], back_shard(i), r.mine, half, half_in.at[w, i])
         start(ways[w].pair[i])
 
     def part_pair(w, i):
         arrive(ways[w].pair[i])
         s = back_shard(i)
-        add_rows(weights[w], s, r.a_pair, 2 * piece, pair_in[w, 0, i])
-        add_rows(weights[w], s, r.b_pair, 2 * piece, pair_in[w, 1, i])
+        add_rows(weights[w], s, r.a_pair, 2 * piece, pair_in.at[w, 0, i])
+        add_rows(weights[w], s, r.b_pair, 2 * piece, pair_in.at[w, 1, i])
         start(ways[w].one[i])
 
     def part_one(w, i):
         arrive(ways[w].one[i])
         s = back_shard(i)
-        add_rows(weights[w], s, r.a, piece, one_in[w, 0, i])
-        add_rows(weights[w], s, r.b, piece, one_in[w, 1, i])
+        add_rows(weights[w], s, r.a, piece, one_in.at[w, 0, i])
+        add_rows(weights[w], s, r.b, piece, one_in.at[w, 1, i])
         if i + 1 < planes:
             start(ways[w].z[i])
 
@@ -426,10 +438,10 @@
     def after_back3(w):
         arrive(ways[w].back3)
 
-    x_send = [links.copy(x_in.at[place.plane(j)], xs.at[t], place.to_plane(j)) for j in others]
-    c_send = [links.copy(c_in.at[place.plane(j)], cs.at[t], place.to_plane(j)) for j in others]
+    x_send = [links.copy(x_go.at[place.plane(j)], xs.at[t], place.to_plane(j)) for j in others]
+    c_send = [links.copy(c_go.at[place.plane(j)], cs.at[t], place.to_plane(j)) for j in others]
     b_send = [links.copy(bias_in, bias.at[t], place.to_plane(j)) for j in others]
-    y_send = [links.copy(cs.at[place.plane(j)], y_out.at[t], place.to_plane(j)) for j in others]
+    y_send = [links.copy(cs.at[place.plane(j)], y_got.at[t], place.to_plane(j)) for j in others]
     dx_send = [links.copy(xs.at[place.plane(j)], dx_out.at[t], place.to_plane(j)) for j in others]
     hops = []
     to_both = (place.to_x[0] + place.to_y[0] - place.dp, t)
@@ -475,9 +487,9 @@
         keep(5, o_in, a_w.at[t, pl.ds(3 * hw, hw)]),
     ]
     own_u, own_d = keep(1, u_in, u_w.at[t]), keep(2, d_in, d_w.at[t])
-    own_x = keep(3, x_in.at[t], xs.at[t])
-    own_c = keep(4, c_in.at[t], cs.at[t])
-    own_y = keep(6, cs.at[t], y_out.at[t])
+    load_x, load_c = keep(3, x_in, raw), keep(4, c_in, raw)
+    own_y = keep(6, cs.at[t], y_got.at[t])
+    leave_y = keep(14, raw, y_out)
     own_dx = keep(7, xs.at[t], dx_out.at[t])
 
     def p_at(m):
@@ -485,7 +497,7 @@
 
     p_save = lambda m: keep(12 + m % 2, p2.at[m % 2], p_at(m))
 
-    start([*own_a, own_u, own_d, own_x, own_c])
+    start([*own_a, load_x, own_u, own_d])
     place.greet()
     for c in own_a:
         c.wait()
@@ -493,7 +505,11 @@
     start(b_send)
     own_u.wait()
     get_own(1)
+    load_x.wait()
+    x_go[...] = jnp.swapaxes(raw[...], 0, 1)
     spread(x_send, 0)
+    xs[t] = x_go[t]
+    load_c.start()
 
     bias[t] = bias_in[...]
     tokens = starts_ref.shape[1]
@@ -530,25 +546,21 @@
     get_one(0, 1)
     pl.when(middle)(lambda: get_one(0, 2))
     get_stage(0, 2)
+    spread(x_send, 2)
     get_one(1, 1)
-    get_stage(1, 2)
-    spread(x_send, 2)
-    own_d.wait()
-    get_own(2)
     get_two(0, 1)
     pl.when(~middle)(lambda: get_one(0, 2))
     get_stage(0, 3)
+    get_stage(1, 2)
+    own_d.wait()
+    get_own(2)
     get_two(1, 1)
-    get_one(1, 2)
-    get_stage(1, 3)
     get_two(0, 2)
     get_one(0, 3)
-    get_two(1, 2)
-    get_one(1, 3)
-    get_two(0, 3)
-    get_two(1, 3)
-    for c in (own_x, own_c):
-        c.wait()
+    get_one(1, 2)
+    load_c.wait()
+    c_go[...] = jnp.swapaxes(raw[...], 0, 1)
+    cs[t] = c_go[t]
     arrive(x_send)
     arrive(b_send)
     afresh = reset_ref[t] > 0
@@ -561,15 +573,20 @@
     acc[...] = x_s[...].reshape(rows, width).astype(f32) + vec(0)
 
     forward_pokes = [
-        (0, 3, lambda: get_stage(2, 1)),
-        (0, 3, lambda: spread(c_send, 0)),
-        (0, 3, lambda: spread(c_send, 1)),
-        (1, 3, lambda: get_one(2, 1)),
-        (2, 0, lambda: get_stage(2, 2)),
-        (2, 0, lambda: spread(c_send, 2)),
+        (0, 1, lambda: get_stage(1, 3)),
+        (0, 2, lambda: get_two(0, 3)),
+        (0, 3, lambda: get_two(1, 2)),
+        (1, 0, lambda: get_stage(2, 1)),
+        (1, 0, lambda: spread(c_send, 0)),
+        (1, 0, lambda: spread(c_send, 1)),
+        (1, 1, lambda: get_one(1, 3)),
+        (2, 0, lambda: get_one(2, 1)),
+        (2, 1, lambda: get_stage(2, 2)),
+        (2, 1, lambda: spread(c_send, 2)),
+        (2, 2, lambda: get_two(1, 3)),
         (3, 0, lambda: get_two(2, 1)),
-        (3, 0, lambda: get_one(2, 2)),
-        (3, 1, lambda: get_stage(2, 3)),
+        (3, 1, lambda: get_one(2, 2)),
+        (3, 2, lambda: get_stage(2, 3)),
     ]
 
     def poke_at(pokes, *now):
@@ -595,10 +612,11 @@
         poke_at([p for p in forward_pokes if p[1] == 0], j, 0)
         x = x_s[...].reshape(rows, width)
         qkv = dot(a_w[s, 0 : 3 * hw, :], x, NT)
-        b = bias[s].astype(f32).T[:, 1:2]
-        q = ((qkv[0:hw] + b[0:hw]).astype(bf16).astype(f32) * (DH**-0.5)).astype(bf16)
+        b = bias[s].astype(f32).T
+        bq, bv = b[0:hw, 1:2], b[0:hw, 8:9]
+        q = ((qkv[0:hw] + bq).astype(bf16).astype(f32) * (DH**-0.5)).astype(bf16)
         k = qkv[hw : 2 * hw].astype(bf16)
-        v = (qkv[2 * hw :] + b[hw : 2 * hw]).astype(bf16)
+        v = (qkv[2 * hw :] + bv).astype(bf16)
         for i in range(hp):
             feats = slice(i * DH, (i + 1) * DH)
             q_s[s * hp + i], k_s[s * hp + i], v_s[s * hp + i] = q[feats], k[feats], v[feats]
@@ -768,7 +786,6 @@
         (2, 4, lambda: part_one(2, 3)),
         (2, 4, lambda: after_z(2)),
         (3, 0, lambda: part_one(1, 0)),
-        (3, 0, lambda: hop(0, 2)),
         (3, 1, lambda: part_one(1, 1)),
         (3, 3, lambda: part_core(0, 2)),
         (3, 3, lambda: part_pair(0, 0)),
@@ -822,6 +839,10 @@
     both = acc[0:mem, :] + acc[dx_last : dx_last + mem, :]
     sm[1, 0:mem, :] = jnp.where(afresh, both, 0.0)
     start(hops[1][0])
+    arrive(y_send)
+    own_y.wait()
+    raw[...] = jnp.swapaxes(y_got[...], 0, 1)
+    leave_y.start()
     part_pair(0, 1)
     part_core(0, 3)
     hop(1, 0)
@@ -841,15 +862,15 @@
     to_middle(dx_send)
     after_z(0)
     after_back2(1)
-    after_back3(1)
     after_back1(0)
     after_back2(0)
+    after_back3(1)
+    hop(0, 2)
     hop(1, 2)
     after_back3(0)
 
-    arrive(y_send)
     arrive(dx_send)
-    own_y.wait()
+    leave_y.wait()
     own_dx.wait()
     for way in ways:
         way.out.wait()
@@ -857,7 +878,7 @@
 
 
 def layer_call(planes, heads, x_in, c_in, qkv_in, o_in, u_in, d_in, bias_in, init, starts, reset):
-    real, width = x_in.shape[1:]
+    real, _, width = x_in.shape
     block = -(-real // 16) * 16
     rows = planes * block
     hp = heads // planes
@@ -872,7 +893,7 @@
         S(shard, bf16),
         S(shard, bf16),
         S((planes, real, width), bf16),
-        S((planes, real, width), bf16),
+        S((real, planes, width), bf16),
         S((heads, rows, rows), bf16),
         S((2 * SMALL, width), f32),
     )
@@ -887,6 +908,10 @@
             V((planes, *shard), bf16),
             V((planes, *shard), bf16),
             V((planes, *shard), bf16),
+            V((real, planes, width), bf16),
+            V((planes, real, width), bf16),
+            V((planes, real, width), bf16),
+            V((planes, real, width), bf16),
             V((planes, real, width), bf16),
             V((planes, real, width), bf16),
             V((planes, block, width), bf16),
@@ -959,16 +984,18 @@
     use_init = ((reset[:, None] > 0) & is_memory[None, :])[:, :, None]
 
     qkv_in = query_key_value_weight.transpose(1, 2, 0).reshape(3 * hw, width)
-    qv_row = jnp.pad(qv_bias.reshape(2 * hw), (0, width - 2 * hw))
-    bias_in = jnp.stack(
-        [up_bias, qv_row, out_bias, back_bias, gain_one, shift_one, gain_two, shift_two]
-        + [jnp.zeros((width,), bf16)] * 8
-    )
+    qv_rows = jnp.pad(qv_bias, ((0, 0), (0, width - hw)))
+    vectors = (out_bias, back_bias, gain_one, shift_one, gain_two, shift_two)
+    bias_rows = [up_bias[None], qv_rows[0:1], *(v[None] for v in vectors), qv_rows[1:2]]
+    place = jnp.arange(16)[:, None]
+    bias_in = jnp.zeros((16, width), bf16)
+    for k, row in enumerate(bias_rows):
+        bias_in = jnp.where(place == k, row, bias_in)
     ga, gu, gd, dx, y, _, small = layer_call(
         planes,
         heads,
-        sequence,
-        cotangent,
+        jnp.swapaxes(sequence, 0, 1),
+        jnp.swapaxes(cotangent, 0, 1),
         qkv_in,
         output_weight,
         up_weight,
@@ -986,7 +1013,7 @@
         ga, gu, gd, small = lax.psum((ga, gu, gd, small), "dp", axis_index_groups=groups)
     own = lambda first: lax.dynamic_slice_in_dim(small, first + t, 1, 0)[0]
     return (
-        y,
+        jnp.swapaxes(y, 0, 1),
         input_grad,
         ga[: 3 * hw].reshape(3, hw, width).transpose(2, 0, 1),
         own(SMALL + 10)[: 2 * hw].reshape(2, hw),

time: 192 us -> 183 us (0.953)
  Pallas kernels: 172 us -> 165 us
  local copies, waits for them, and re-layouts: 13.1 us -> 9.54 us
  other arithmetic: 3.49 us -> 6.15 us
    pallas_call x1, Pallas kernels: 172 us -> 165 us  [layer_call(): pl.pallas_call(functools.partial(layer_kernel, planes, heads, block), out...]
    unnamed x34 -> x14, local copies, waits for them, and re-layouts: 7.54 us -> 2.8 us
where the time goes in v5:
time: 183 us; the launch traced here: 181 us
  Pallas kernels  165 us (90%)
  local copies, waits for them, and re-layouts  9.54 us (5%)
  other arithmetic  6.15 us (3%)
    pallas_call x1, Pallas kernels, layer_call(): pl.pallas_call(functools.partial(layer_kernel, planes, heads, block), out...  165 us

profile of v5, /device:TPU:0, one launch (start us, length us, event | category | flops | bytes accessed | tf_op | source)
XLA Modules:
  0.0 181.2 jit_solution(1762633378268145108)
XLA Ops:
  0.6 0.8 slice_reduce_fusion.7
  1.5 1.5 select_select_fusion.bias_in
  3.0 0.0 copy-start.5
  3.0 164.8 %shard_map.280 = (bf16[768,768]{1,0:T(8,128)(2,1)}, bf16[768,768]{1,0:T(8,128)(2,1)}, bf16[768,768]{1,0:T(8,128)(2,1)}, bf16[4,133,768]{2,1,0:T(8,128)(2,1)}, bf...) custom-call(bf16[133,4,768]{2,1,0:T(4,128)(2,1)} %bitcast.12, ...), custom_call_target="tpu_custom_call" | custom-call | tf_op jit(solution)/shard_map/pallas_call | solution.py:902
  167.7 1.8 slice_reduce_fusion
  169.5 0.7 dynamic-slice_reduce_fusion.1
  170.2 0.7 reshape.131
  170.9 0.0 copy-done.5
  170.9 0.1 broadcast_and_fusion
  171.0 1.4 convert_select_fusion
  172.4 0.0 copy-start.4
  172.4 0.0 copy-start
  172.4 1.8 copy.32
  174.2 0.0 copy-done.4
  174.2 0.6 slice.48
  174.8 0.0 copy-done
  174.8 0.0 copy-start.2
  174.8 1.3 slice.49
  176.2 0.9 slice.50
  177.0 0.0 copy-done.2
  177.0 0.0 copy-start.1
  177.0 1.6 convert_element_type.16
  178.6 0.1 copy-done.1
  178.7 0.0 copy-start.3
  178.7 1.6 convert_element_type.17
  180.3 0.0 copy-done.3
  180.3 0.9 copy.34
  (7 shorter events, 0.0 us)
Async XLA Ops:
  3.0 167.9 %copy-start.5 = (s32[4]{0:T(128)S(1)}, s32[4]{0:T(128)}, u32[]{:S(2)}) copy-start(s32[4]{0:T(128)} %reset_ref.1) | copy-start | bytes 52
  172.4 1.8 %copy-start.4 = (f32[32,768]{1,0:T(8,128)S(1)}, f32[32,768]{1,0:T(8,128)}, u32[]{:S(2)}) copy-start(f32[32,768]{1,0:T(8,128)} %get-tuple-element.24) | copy-start | bytes 294916
  172.4 2.4 %copy-start = (bf16[768,768]{1,0:T(8,128)(2,1)S(1)}, bf16[768,768]{1,0:T(8,128)(2,1)}, u32[]{:S(2)}) copy-start(bf16[768,768]{1,0:T(8,128)(2,1)} %get-tuple-element.23) | copy-start | bytes 3538948
  174.8 2.2 %copy-start.2 = (bf16[768,768]{1,0:T(8,128)(2,1)S(1)}, bf16[768,768]{1,0:T(8,128)(2,1)}, u32[]{:S(2)}) copy-start(bf16[768,768]{1,0:T(8,128)(2,1)} %get-tuple-element.25) | copy-start | bytes 3538948
  177.0 1.7 copy-start.1
  178.7 1.6 copy-start.3

commit v6 on v5

--- a/solution.py
+++ b/solution.py
@@ -146,7 +146,14 @@
     o_in,
     u_in,
     d_in,
-    bias_in,
+    up_bias,
+    qv_bias,
+    out_bias,
+    back_bias,
+    gain_one,
+    shift_one,
+    gain_two,
+    shift_two,
     init_ref,
     starts_ref,
     reset_ref,
@@ -203,12 +210,14 @@
     real, width = xs.shape[1:]
     rows = planes * block
     mem = init_ref.shape[0]
+    hidden = u_w.shape[2]
     hp = heads // planes
     hw = hp * DH
     links = Links(send, recv)
     r = Rows(place, a_w.shape[1])
     piece, half = r.piece, r.half
-    vec = lambda i: bias_in[2 + i : 3 + i, :].astype(f32)
+    vectors = (out_bias, back_bias, gain_one, shift_one, gain_two, shift_two)
+    vec = lambda i: vectors[i][...].astype(f32).reshape(1, width)
     add_up = lambda v: jnp.sum(v, axis=0, keepdims=True)
 
     def keep(k, src, dst):
@@ -440,7 +449,7 @@
 
     x_send = [links.copy(x_go.at[place.plane(j)], xs.at[t], place.to_plane(j)) for j in others]
     c_send = [links.copy(c_go.at[place.plane(j)], cs.at[t], place.to_plane(j)) for j in others]
-    b_send = [links.copy(bias_in, bias.at[t], place.to_plane(j)) for j in others]
+    b_send = [links.copy(bias.at[t], bias.at[t], place.to_plane(j)) for j in others]
     y_send = [links.copy(cs.at[place.plane(j)], y_got.at[t], place.to_plane(j)) for j in others]
     dx_send = [links.copy(xs.at[place.plane(j)], dx_out.at[t], place.to_plane(j)) for j in others]
     hops = []
@@ -498,6 +507,10 @@
     p_save = lambda m: keep(12 + m % 2, p2.at[m % 2], p_at(m))
 
     start([*own_a, load_x, own_u, own_d])
+    bias[t] = jnp.zeros(bias.shape[1:], bf16)
+    bias[t, 0:1, :] = up_bias[...].astype(f32).reshape(1, hidden).astype(bf16)
+    bias[t, 1:2, 0:hw] = qv_bias[0:1, :]
+    bias[t, 8:9, 0:hw] = qv_bias[1:2, :]
     place.greet()
     for c in own_a:
         c.wait()
@@ -511,7 +524,6 @@
     xs[t] = x_go[t]
     load_c.start()
 
-    bias[t] = bias_in[...]
     tokens = starts_ref.shape[1]
 
     def token_of(shape, axis):
@@ -877,7 +889,7 @@
     links.finish()
 
 
-def layer_call(planes, heads, x_in, c_in, qkv_in, o_in, u_in, d_in, bias_in, init, starts, reset):
+def layer_call(planes, heads, x_in, c_in, qkv_in, o_in, u_in, d_in, vectors, init, starts, reset):
     real, _, width = x_in.shape
     block = -(-real // 16) * 16
     rows = planes * block
@@ -902,7 +914,7 @@
     return pl.pallas_call(
         functools.partial(layer_kernel, planes, heads, block),
         out_shape=outs,
-        in_specs=[any_spec] * 6 + [vmem_spec] * 3 + [pl.BlockSpec(memory_space=pltpu.SMEM)],
+        in_specs=[any_spec] * 6 + [vmem_spec] * 10 + [pl.BlockSpec(memory_space=pltpu.SMEM)],
         out_specs=[any_spec] * 6 + [vmem_spec],
         scratch_shapes=[
             V((planes, *shard), bf16),
@@ -915,7 +927,7 @@
             V((planes, real, width), bf16),
             V((planes, real, width), bf16),
             V((planes, block, width), bf16),
-            V((planes, *bias_in.shape), bf16),
+            V((planes, 16, hidden), bf16),
             V((heads, DH, rows), bf16),
             V((heads, DH, rows), bf16),
             V((heads, DH, rows), bf16),
@@ -948,7 +960,123 @@
         compiler_params=pltpu.CompilerParams(
             collective_id=0, has_side_effects=True, vmem_limit_bytes=63 * MIB
         ),
-    )(x_in, c_in, qkv_in, o_in, u_in, d_in, bias_in, init, starts, reset)
+    )(x_in, c_in, qkv_in, o_in, u_in, d_in, *vectors, init, starts, reset)
+
+
+STEPS = 2
+
+
+def finish_kernel(
+    planes,
+    mem,
+    qkv_in,
+    o_in,
+    u_in,
+    d_in,
+    dx_in,
+    small_in,
+    reset_ref,
+    y_in,
+    qkv_out,
+    o_out,
+    u_out,
+    d_out,
+    qv_out,
+    mem_out,
+    dx_out,
+    y_out,
+    *rest,
+):
+    sums, (dx_s, y_s, sem) = rest[:-3], rest[-3:]
+    step = pl.program_id(0)
+    leave = pltpu.make_async_copy(dx_s, dx_out, sem.at[0])
+    take_y = pltpu.make_async_copy(y_in, y_s, sem.at[1])
+    leave_y = pltpu.make_async_copy(y_s, y_out, sem.at[2])
+    real = dx_in.shape[1]
+    hw = qv_out.shape[1]
+
+    @pl.when(step == 0)
+    def _():
+        take_y.start()
+        t = lax.axis_index("tensor")
+        qv = small_in[pl.ds(SMALL + 10 + t, 1), :]
+        qv_out[0:1, :] = qv[:, 0:hw]
+        qv_out[1:2, :] = qv[:, hw : 2 * hw]
+        mem_out[...] = small_in[SMALL : SMALL + mem, :]
+        for k, out in enumerate(sums):
+            at = pl.ds(6 + t, 1) if k == 6 else slice(k, k + 1)
+            out[...] = small_in[at, :].reshape(out.shape)
+        row = lax.broadcasted_iota(jnp.int32, dx_in.shape[1:], 0)
+        memory = ((t == 0) & (row < mem)) | ((t == planes - 1) & (row >= real - mem))
+        kept = [
+            jnp.where(memory & (reset_ref[k] > 0), 0.0, dx_in[k].astype(f32))[None]
+            for k in range(dx_in.shape[0])
+        ]
+        dx_s[...] = jnp.swapaxes(jnp.concatenate(kept, 0), 0, 1)
+        leave.start()
+        take_y.wait()
+        leave_y.start()
+
+    for ins, outs in ((qkv_in, qkv_out), (o_in, o_out), (u_in, u_out), (d_in, d_out)):
+        outs[...] = ins[...].astype(f32)
+
+    @pl.when(step == STEPS - 1)
+    def _():
+        leave.wait()
+        leave_y.wait()
+
+
+def finish_call(planes, mem, qkv_rows, ga, gu, gd, dx, small, reset, y):
+    rows, width = ga.shape
+    o_rows = rows - qkv_rows
+    S = jax.ShapeDtypeStruct
+    segs, real, _ = dx.shape
+    whole = lambda *shape: pl.BlockSpec(shape, lambda i: (0,) * len(shape))
+    part = lambda size, first=0: pl.BlockSpec(
+        (size // STEPS, width), lambda i: (first // (size // STEPS) + i, 0)
+    )
+    return pl.pallas_call(
+        functools.partial(finish_kernel, planes, mem),
+        grid=(STEPS,),
+        out_shape=(
+            S((qkv_rows, width), f32),
+            S((o_rows, width), f32),
+            S(gu.shape, f32),
+            S(gd.shape, f32),
+            S((2, o_rows), f32),
+            S((mem, width), f32),
+            S((real, segs, width), f32),
+            S(y.shape, y.dtype),
+            *[S((width,), f32)] * 7,
+        ),
+        in_specs=[
+            part(qkv_rows),
+            part(o_rows, qkv_rows),
+            part(rows),
+            part(rows),
+            whole(*dx.shape),
+            whole(*small.shape),
+            pl.BlockSpec(memory_space=pltpu.SMEM),
+            pl.BlockSpec(memory_space=pl.ANY),
+        ],
+        out_specs=[
+            part(qkv_rows),
+            part(o_rows),
+            part(rows),
+            part(rows),
+            whole(2, o_rows),
+            whole(mem, width),
+            pl.BlockSpec(memory_space=pl.ANY),
+            pl.BlockSpec(memory_space=pl.ANY),
+            *[whole(width)] * 7,
+        ],
+        scratch_shapes=[
+            pltpu.VMEM((real, segs, width), f32),
+            pltpu.VMEM(y.shape, y.dtype),
+            pltpu.SemaphoreType.DMA((3,)),
+        ],
+        compiler_params=pltpu.CompilerParams(vmem_limit_bytes=63 * MIB),
+    )(ga, ga, gu, gd, dx, small, reset, y)
 
 
 def shards(
@@ -978,19 +1106,7 @@
     hw = query_key_value_weight.shape[2]
     heads = hw * planes // DH
     assert segs == planes == 4 and 4 * hw == up_weight.shape[1] and mem <= local_rows and dp_size % INNER == 0
-    t = lax.axis_index("tensor")
-    position = t * local_rows + jnp.arange(local_rows, dtype=jnp.int32)
-    is_memory = (position < mem) | (position >= mem + tokens)
-    use_init = ((reset[:, None] > 0) & is_memory[None, :])[:, :, None]
-
     qkv_in = query_key_value_weight.transpose(1, 2, 0).reshape(3 * hw, width)
-    qv_rows = jnp.pad(qv_bias, ((0, 0), (0, width - hw)))
-    vectors = (out_bias, back_bias, gain_one, shift_one, gain_two, shift_two)
-    bias_rows = [up_bias[None], qv_rows[0:1], *(v[None] for v in vectors), qv_rows[1:2]]
-    place = jnp.arange(16)[:, None]
-    bias_in = jnp.zeros((16, width), bf16)
-    for k, row in enumerate(bias_rows):
-        bias_in = jnp.where(place == k, row, bias_in)
     ga, gu, gd, dx, y, _, small = layer_call(
         planes,
         heads,
@@ -1000,34 +1116,38 @@
         output_weight,
         up_weight,
         down_weight,
-        bias_in,
+        (up_bias, qv_bias, out_bias, back_bias, gain_one, shift_one, gain_two, shift_two),
         init_memory,
         starts,
         reset,
     )
 
-    input_grad = jnp.where(use_init, 0.0, dx.astype(f32))
-    ga, gu, gd = ga.astype(f32), gu.astype(f32), gd.astype(f32)
     if dp_size > INNER:
         groups = [[o * INNER + i for o in range(dp_size // INNER)] for i in range(INNER)]
-        ga, gu, gd, small = lax.psum((ga, gu, gd, small), "dp", axis_index_groups=groups)
-    own = lambda first: lax.dynamic_slice_in_dim(small, first + t, 1, 0)[0]
+        ga, gu, gd, small = lax.psum(
+            (ga.astype(f32), gu.astype(f32), gd.astype(f32), small),
+            "dp",
+            axis_index_groups=groups,
+        )
+    g_qkv, g_o, g_u, g_d, g_qv, g_mem, input_grad, y, *sums = finish_call(
+        planes, mem, 3 * hw, ga, gu, gd, dx, small, reset, y
+    )
     return (
         jnp.swapaxes(y, 0, 1),
-        input_grad,
-        ga[: 3 * hw].reshape(3, hw, width).transpose(2, 0, 1),
-        own(SMALL + 10)[: 2 * hw].reshape(2, hw),
-        ga[3 * hw :],
-        small[5],
-        gu,
-        own(6),
-        gd,
-        small[2],
-        small[3],
-        small[4],
-        small[0],
-        small[1],
-        small[SMALL : SMALL + mem],
+        jnp.swapaxes(input_grad, 0, 1),
+        g_qkv.reshape(3, hw, width).transpose(2, 0, 1),
+        g_qv,
+        g_o,
+        sums[5],
+        g_u,
+        sums[6],
+        g_d,
+        sums[2],
+        sums[3],
+        sums[4],
+        sums[0],
+        sums[1],
+        g_mem,
     )
 
 

time: 183 us -> 174 us (0.951)
  local copies, waits for them, and re-layouts: 9.54 us -> 0 us
  other arithmetic: 6.15 us -> 0 us
  Pallas kernels: 165 us -> 171 us
    pallas_call x0 -> x1, Pallas kernels: none -> 6.26 us  [finish_call(): pl.pallas_call(functools.partial(finish_kernel, planes, mem), grid=(STEPS...]
    slice x6 -> x0, local copies, waits for them, and re-layouts: 6.08 us -> none  [the longest x1 1.76 us: shards(): small[1]]
    convert_element_type x2 -> x0, other arithmetic: 3.15 us -> none  [shards(): ga, gu, gd = (ga.astype(f32), gu.astype(f32), gd.astype(f32))]
    select_n x2 -> x0, other arithmetic: 2.88 us -> none  [the longest x1 1.49 us: shards(): bias_in = jnp.where(place == k, row, bias_in)]
    unnamed x14 -> x0, local copies, waits for them, and re-layouts: 2.8 us -> none
where the time goes in v6:
time: 174 us; the launch traced here: 172 us
  Pallas kernels  171 us (98%)
    pallas_call x1, Pallas kernels, layer_call(): pl.pallas_call(functools.partial(layer_kernel, planes, heads, block), out...  165 us
    pallas_call x1, Pallas kernels, finish_call(): pl.pallas_call(functools.partial(finish_kernel, planes, mem), grid=(STEPS...  6.26 us

profile of v6, /device:TPU:0, one launch (start us, length us, event | category | flops | bytes accessed | tf_op | source)
XLA Modules:
  0.0 172.0 jit_solution(946204706495895267)
XLA Ops:
  0.7 164.9 %shard_map.280 = (bf16[768,768]{1,0:T(8,128)(2,1)}, bf16[768,768]{1,0:T(8,128)(2,1)}, bf16[768,768]{1,0:T(8,128)(2,1)}, bf16[4,133,768]{2,1,0:T(8,128)(2,1)}, bf...) custom-call(bf16[133,4,768]{2,1,0:T(4,128)(2,1)} %bitcast.11, ...), custom_call_target="tpu_custom_call" | custom-call | tf_op jit(solution)/shard_map/pallas_call | solution.py:914
  165.6 6.3 %shard_map.281 = (f32[576,768]{1,0:T(8,128)}, f32[192,768]{1,0:T(8,128)}, f32[768,768]{1,0:T(8,128)}, f32[768,768]{1,0:T(8,128)}, f32[2,192]{1,0:T(2,128)}, /*in...) custom-call(bf16[768,768]{1,0:T(8,128)(2,1)} %get-tuple-element.36.q, ...), custom_call_target="tpu_custom_call" | custom-call | tf_op jit(solution)/shard_map/pallas_call | solution.py:1038

commit v7 on v6

--- a/solution.py
+++ b/solution.py
@@ -58,11 +58,13 @@
         ]
 
     def greet(self):
-        barrier = pltpu.get_barrier_semaphore()
-        partners = self.partners()
-        for device in partners:
-            pl.semaphore_signal(barrier, inc=1, device_id=device, device_id_type=MESH)
-        pl.semaphore_wait(barrier, len(partners))
+        for device in self.partners():
+            pl.semaphore_signal(
+                pltpu.get_barrier_semaphore(), inc=1, device_id=device, device_id_type=MESH
+            )
+
+    def all_here(self):
+        pl.semaphore_wait(pltpu.get_barrier_semaphore(), len(self.partners()))
 
 
 class Rows:
@@ -342,7 +344,7 @@
         pl.when((t == 0) | (t == 2))(lambda: start(sends[2:3]))
         pl.when((t == 1) | (t == 3))(lambda: start(sends[0:1]))
 
-    back_order = (2, 1, 3, 0)
+    back_order = (2, 3, 1, 0)
     ways = []
     for w in range(3):
         g = weights[w]
@@ -506,12 +508,13 @@
 
     p_save = lambda m: keep(12 + m % 2, p2.at[m % 2], p_at(m))
 
+    place.greet()
     start([*own_a, load_x, own_u, own_d])
     bias[t] = jnp.zeros(bias.shape[1:], bf16)
     bias[t, 0:1, :] = up_bias[...].astype(f32).reshape(1, hidden).astype(bf16)
     bias[t, 1:2, 0:hw] = qv_bias[0:1, :]
     bias[t, 8:9, 0:hw] = qv_bias[1:2, :]
-    place.greet()
+    place.all_here()
     for c in own_a:
         c.wait()
     get_own(0)
@@ -796,7 +799,6 @@
         (2, 3, lambda: hop(0, 1)),
         (2, 3, lambda: part_core(0, 1)),
         (2, 4, lambda: part_one(2, 3)),
-        (2, 4, lambda: after_z(2)),
         (3, 0, lambda: part_one(1, 0)),
         (3, 1, lambda: part_one(1, 1)),
         (3, 3, lambda: part_core(0, 2)),
@@ -858,24 +860,25 @@
     part_pair(0, 1)
     part_core(0, 3)
     hop(1, 0)
-    after_back1(2)
     part_pair(0, 2)
-    after_z(1)
     part_one(0, 0)
     part_one(0, 1)
     part_pair(0, 3)
-    hop(1, 1)
-    after_back2(2)
+    after_z(2)
+    after_z(1)
     part_one(0, 2)
     start(dx_send[1:2])
-    after_back1(1)
-    after_back3(2)
+    hop(1, 1)
     part_one(0, 3)
     to_middle(dx_send)
     after_z(0)
+    after_back1(2)
+    after_back1(1)
+    after_back1(0)
+    after_back2(2)
     after_back2(1)
-    after_back1(0)
     after_back2(0)
+    after_back3(2)
     after_back3(1)
     hop(0, 2)
     hop(1, 2)

time: 174 us -> 171 us (0.983)
  Pallas kernels: 171 us -> 168 us
    pallas_call x1, Pallas kernels: 165 us -> 162 us  [layer_call(): pl.pallas_call(functools.partial(layer_kernel, planes, heads, block), out...]
where the time goes in v7:
time: 171 us; the launch traced here: 169 us
  Pallas kernels  168 us (98%)
    pallas_call x1, Pallas kernels, layer_call(): pl.pallas_call(functools.partial(layer_kernel, planes, heads, block), out...  162 us
    pallas_call x1, Pallas kernels, finish_call(): pl.pallas_call(functools.partial(finish_kernel, planes, mem), grid=(STEPS...  6.26 us

profile of v7, /device:TPU:0, one launch (start us, length us, event | category | flops | bytes accessed | tf_op | source)
XLA Modules:
  0.0 169.0 jit_solution(7937569096373049227)
XLA Ops:
  0.7 161.9 %shard_map.280 = (bf16[768,768]{1,0:T(8,128)(2,1)}, bf16[768,768]{1,0:T(8,128)(2,1)}, bf16[768,768]{1,0:T(8,128)(2,1)}, bf16[4,133,768]{2,1,0:T(8,128)(2,1)}, bf...) custom-call(bf16[133,4,768]{2,1,0:T(4,128)(2,1)} %bitcast.11, ...), custom_call_target="tpu_custom_call" | custom-call | tf_op jit(solution)/shard_map/pallas_call | solution.py:917
  162.6 6.3 %shard_map.281 = (f32[576,768]{1,0:T(8,128)}, f32[192,768]{1,0:T(8,128)}, f32[768,768]{1,0:T(8,128)}, f32[768,768]{1,0:T(8,128)}, f32[2,192]{1,0:T(2,128)}, /*in...) custom-call(bf16[768,768]{1,0:T(8,128)(2,1)} %get-tuple-element.36.q, ...), custom_call_target="tpu_custom_call" | custom-call | tf_op jit(solution)/shard_map/pallas_call | solution.py:1041

commit v8 on v7

--- a/solution.py
+++ b/solution.py
@@ -867,14 +867,18 @@
     after_z(2)
     after_z(1)
     part_one(0, 2)
+    part_one(0, 3)
     start(dx_send[1:2])
     hop(1, 1)
-    part_one(0, 3)
     to_middle(dx_send)
     after_z(0)
     after_back1(2)
     after_back1(1)
     after_back1(0)
+    gone = [*x_send, *c_send, *b_send, *y_send]
+    for way in ways:
+        gone += [c for part in way.core + way.pair + way.one + way.z for c in part]
+    links.finish(gone + ways[2].back1 + ways[1].back1)
     after_back2(2)
     after_back2(1)
     after_back2(0)

time: 171 us -> 171 us (level)
  no operation moved by 1% of the time
where the time goes in v8:
time: 171 us; the launch traced here: 170 us
  Pallas kernels  169 us (99%)
    pallas_call x1, Pallas kernels, layer_call(): pl.pallas_call(functools.partial(layer_kernel, planes, heads, block), out...  162 us
    pallas_call x1, Pallas kernels, finish_call(): pl.pallas_call(functools.partial(finish_kernel, planes, mem), grid=(STEPS...  6.26 us

profile of v8, /device:TPU:0, one launch (start us, length us, event | category | flops | bytes accessed | tf_op | source)
XLA Modules:
  0.0 169.6 jit_solution(3914122240655953956)
XLA Ops:
  0.7 162.5 %shard_map.280 = (bf16[768,768]{1,0:T(8,128)(2,1)}, bf16[768,768]{1,0:T(8,128)(2,1)}, bf16[768,768]{1,0:T(8,128)(2,1)}, bf16[4,133,768]{2,1,0:T(8,128)(2,1)}, bf...) custom-call(bf16[133,4,768]{2,1,0:T(4,128)(2,1)} %bitcast.11, ...), custom_call_target="tpu_custom_call" | custom-call | tf_op jit(solution)/shard_map/pallas_call | solution.py:921
  163.1 6.3 %shard_map.281 = (f32[576,768]{1,0:T(8,128)}, f32[192,768]{1,0:T(8,128)}, f32[768,768]{1,0:T(8,128)}, f32[768,768]{1,0:T(8,128)}, f32[2,192]{1,0:T(2,128)}, /*in...) custom-call(bf16[768,768]{1,0:T(8,128)(2,1)} %get-tuple-element.36.q, ...), custom_call_target="tpu_custom_call" | custom-call | tf_op jit(solution)/shard_map/pallas_call | solution.py:1045
